TPU v7x, 512 devices: a whole 4x4x16 slice. The times are simulated.
512 devices in a mesh: tx: 32 (over z, core), ty: 16 (over x, y).
Axes of the slice: x: 4, y: 4, z: 16, core: 2. Of those that a mesh axis runs over, the one named last changes fastest.
Arguments:
- rhs: bfloat16 [16, 262144], P(None, ('tx', 'ty')), may hold values from -6 to 6
- diag_blocks: bfloat16 [262144, 512], P(('tx', 'ty')), may hold values from -0.25 to 0.25
- leaf_in: bfloat16 [262144, 128], P(('tx', 'ty')), may hold values from -0.25 to 0.25
- leaf_out: bfloat16 [65536, 512], P(('tx', 'ty')), may hold values from -0.5 to 0.5
- up_maps: bfloat16 [2, 512, 512, 512], P(None, ('tx', 'ty')), may hold values from -0.25 to 0.25
- cross_maps: bfloat16 [2, 512, 512, 512], P(None, ('tx', 'ty')), may hold values from -0.3125 to 0.3125
- down_maps: bfloat16 [2, 512, 512, 512], P(None, ('tx', 'ty')), may hold values from -0.3125 to 0.3125
- node_rank: int32 [512, 2], P(('tx', 'ty')), may hold values from 64 to 512, as said below
Outputs:
- product: float32 [16, 262144], P(None, ('tx', 'ty'))
Inputs may be any that keep to these rules, and one draw needn't show every extreme that they name: node_rank[d,0] is a multiple of 16 from 64 to 128; node_rank[d,1] is a multiple of 64 from 128 to 512, and the root's owner has 512; device 0 owns no upper node.
All inputs are finite; a program needn't handle non-finite values.
Results may differ from a plain program's by a relative error of at most 0.023.
Values may be sent and summed in bfloat16 or wider, within the bound.
A program may use at most 64 MiB of HBM per device.

v0:
```python
import jax
import jax.numpy as jnp
from jax import lax
from jax.sharding import PartitionSpec as P


def from_behind(x, axis, by):
    count = lax.axis_size(axis)
    pairs = [(i, i + by) for i in range(count) if 0 <= i + by < count]
    return lax.ppermute(x, axis, pairs)


def relay(values, by):
    return from_behind(values, ("tx", "ty"), by)


def on_device(rhs, diag_blocks, leaf_in, leaf_out, up_maps, cross_maps, down_maps, node_rank):
    f32 = jnp.float32
    row_len = lax.axis_size("ty")
    device_count = lax.axis_size("tx") * row_len
    levels = device_count.bit_length() - 1
    position = lax.axis_index("tx") * row_len + lax.axis_index("ty")
    width = up_maps.shape[-1]
    leaf_width = leaf_in.shape[1]
    columns = jnp.arange(width, dtype=jnp.int32)
    leaf_keep = columns[None, :] < node_rank[0, 0]
    node_keep = columns[None, :] < node_rank[0, 1]
    up_left, up_right = (up_maps[0, 0], up_maps[1, 0])
    cross_left, cross_right = (cross_maps[0, 0], cross_maps[1, 0])
    down_left, down_right = (down_maps[0, 0], down_maps[1, 0])
    projected = jnp.dot(rhs, leaf_in, preferred_element_type=f32)
    projected = jnp.pad(projected, ((0, 0), (0, width - leaf_width)))
    leaf_coef = jnp.where(leaf_keep, projected, 0.0).astype(jnp.bfloat16)

    def lift(operands):
        summed = jnp.dot(operands[0], up_left, preferred_element_type=f32)
        summed = summed + jnp.dot(operands[1], up_right, preferred_element_type=f32)
        return jnp.where(node_keep, summed, 0.0).astype(jnp.bfloat16)

    def unchanged(operands):
        return operands[2]

    owned_coef = jnp.zeros_like(leaf_coef)
    kept_left = jnp.zeros_like(leaf_coef)
    kept_right = jnp.zeros_like(leaf_coef)
    for height in range(1, levels + 1):
        block_size = 2**height
        distance = max(1, block_size // 4)
        outgoing = leaf_coef if height == 1 else owned_coef
        from_left = relay(outgoing, distance)
        from_right = leaf_coef if height == 1 else relay(outgoing, -distance)
        is_owner = position % block_size == block_size // 2
        kept_left = jnp.where(is_owner, from_left, kept_left)
        kept_right = jnp.where(is_owner, from_right, kept_right)
        if height < levels:
            owned_coef = lax.cond(is_owner, lift, unchanged, (from_left, from_right, owned_coef))

    def lower(operands):
        to_left = jnp.dot(operands[1], cross_left, preferred_element_type=f32)
        to_left = to_left + jnp.dot(operands[2], down_left, preferred_element_type=f32)
        to_right = jnp.dot(operands[0], cross_right, preferred_element_type=f32)
        to_right = to_right + jnp.dot(operands[2], down_right, preferred_element_type=f32)
        return (to_left.astype(jnp.bfloat16), to_right.astype(jnp.bfloat16))

    def silent(operands):
        blank = jnp.zeros_like(operands[2])
        return (blank, blank)

    down_coef = jnp.zeros_like(leaf_coef)
    leaf_down = jnp.zeros_like(leaf_coef)
    for height in range(levels, 0, -1):
        block_size = 2**height
        distance = max(1, block_size // 4)
        is_owner = position % block_size == block_size // 2
        to_left, to_right = lax.cond(is_owner, lower, silent, (kept_left, kept_right, down_coef))
        at_left = relay(to_left, -distance)
        at_right = to_right if height == 1 else relay(to_right, distance)
        if height == 1:
            arrived = jnp.where(position % 2 == 0, at_left, at_right)
            leaf_down = jnp.where(leaf_keep, arrived, 0)
        else:
            child_size = block_size // 2
            child_owner = position % child_size == child_size // 2
            on_left = position % block_size < child_size
            arrived = jnp.where(on_left, at_left, at_right)
            down_coef = jnp.where(child_owner, jnp.where(node_keep, arrived, 0), down_coef)
    direct = jnp.dot(rhs, diag_blocks, preferred_element_type=f32)
    return direct + jnp.dot(leaf_down[:, :leaf_width], leaf_out, preferred_element_type=f32)


def solution(mesh):
    in_specs = (
        P(None, ("tx", "ty")),
        P(("tx", "ty"), None),
        P(("tx", "ty"), None),
        P(("tx", "ty"), None),
        P(None, ("tx", "ty"), None, None),
        P(None, ("tx", "ty"), None, None),
        P(None, ("tx", "ty"), None, None),
        P(("tx", "ty"), None),
    )
    out_specs = P(None, ("tx", "ty"))
    return jax.shard_map(
        on_device, mesh=mesh, in_specs=in_specs, out_specs=out_specs, check_vma=False
    )
```

profile of v0, /device:TPU:127, one launch (start us, length us, event | category | flops | bytes accessed | tf_op | source)
XLA Modules:
  0.0 209.3 jit_solution(5664080625878223859)
XLA Ops:
  3.1 4.9 %collective-permute-start = (bf16[16,512]{1,0:T(8,128)(2,1)S(1)}, bf16[16,512]{1,0:T(8,128)(2,1)S(1)}, u32[]{:S(2)}, u32[]{:S(2)}) collective-permute-start(bf16[16,512]{1,0:T(8,128)(2,1)S(1)} %select_convert_fusion), channel_id=1, source_target_pairs={{0,1},{1,2},{2,3},{3,4},{4,5},{5,6},{6,7},{7,8},{8,9},{9,10},{10,1... | collective-permute-start | bytes 49160 | tf_op jit(solution)/shard_map/ppermute | solution.py:10
  10.3 8.2 %collective-permute-start.1 = (bf16[16,512]{1,0:T(8,128)(2,1)S(1)}, bf16[16,512]{1,0:T(8,128)(2,1)S(1)}, u32[]{:S(2)}, u32[]{:S(2)}) collective-permute-start(bf16[16,512]{1,0:T(8,128)(2,1)S(1)} %get-tuple-element.450), channel_id=1, source_target_pairs={{0,1},{1,2},{2,3},{3,4},{4,5},{5,6},{6,7},{7,8},{8,9},{9,10},{10,1... | collective-permute-start | bytes 49160 | tf_op jit(solution)/shard_map/ppermute | solution.py:10
  20.4 8.5 %collective-permute-done.2 = bf16[16,512]{1,0:T(8,128)(2,1)S(1)} collective-permute-done((bf16[16,512]{1,0:T(8,128)(2,1)S(1)}, bf16[16,512]{1,0:T(8,128)(2,1)S(1)}, u32[]{:S(2)}, u32[]{:S(2)}) %collective-permute-start.2) | collective-permute-done | bytes 16416 | tf_op jit(solution)/shard_map/ppermute | solution.py:10
  30.9 4.9 %collective-permute-start.4 = (bf16[16,512]{1,0:T(8,128)(2,1)S(1)}, bf16[16,512]{1,0:T(8,128)(2,1)S(1)}, u32[]{:S(2)}, u32[]{:S(2)}) collective-permute-start(bf16[16,512]{1,0:T(8,128)(2,1)S(1)} %get-tuple-element.451), channel_id=1, source_target_pairs={{2,0},{3,1},{4,2},{5,3},{6,4},{7,5},{8,6},{9,7},{10,8},{11,9},{12,... | collective-permute-start | bytes 49160 | tf_op jit(solution)/shard_map/ppermute | solution.py:10
  35.8 5.9 %collective-permute-done.4 = bf16[16,512]{1,0:T(8,128)(2,1)S(1)} collective-permute-done((bf16[16,512]{1,0:T(8,128)(2,1)S(1)}, bf16[16,512]{1,0:T(8,128)(2,1)S(1)}, u32[]{:S(2)}, u32[]{:S(2)}) %collective-permute-start.4) | collective-permute-done | bytes 16416 | tf_op jit(solution)/shard_map/ppermute | solution.py:10
  43.6 3.4 %collective-permute-start.6 = (bf16[16,512]{1,0:T(8,128)(2,1)S(1)}, bf16[16,512]{1,0:T(8,128)(2,1)S(1)}, u32[]{:S(2)}, u32[]{:S(2)}) collective-permute-start(bf16[16,512]{1,0:T(8,128)(2,1)S(1)} %get-tuple-element.452), channel_id=1, source_target_pairs={{4,0},{5,1},{6,2},{7,3},{8,4},{9,5},{10,6},{11,7},{12,8},{13,9},{1... | collective-permute-start | bytes 49160 | tf_op jit(solution)/shard_map/ppermute | solution.py:10
  46.9 5.0 %collective-permute-done.6 = bf16[16,512]{1,0:T(8,128)(2,1)S(1)} collective-permute-done((bf16[16,512]{1,0:T(8,128)(2,1)S(1)}, bf16[16,512]{1,0:T(8,128)(2,1)S(1)}, u32[]{:S(2)}, u32[]{:S(2)}) %collective-permute-start.6) | collective-permute-done | bytes 16416 | tf_op jit(solution)/shard_map/ppermute | solution.py:10
  53.8 4.9 %collective-permute-start.8 = (bf16[16,512]{1,0:T(8,128)(2,1)S(1)}, bf16[16,512]{1,0:T(8,128)(2,1)S(1)}, u32[]{:S(2)}, u32[]{:S(2)}) collective-permute-start(bf16[16,512]{1,0:T(8,128)(2,1)S(1)} %get-tuple-element.453), channel_id=1, source_target_pairs={{8,0},{9,1},{10,2},{11,3},{12,4},{13,5},{14,6},{15,7},{16,8},{17,9... | collective-permute-start | bytes 49160 | tf_op jit(solution)/shard_map/ppermute | solution.py:10
  58.7 3.8 %collective-permute-done.8 = bf16[16,512]{1,0:T(8,128)(2,1)S(1)} collective-permute-done((bf16[16,512]{1,0:T(8,128)(2,1)S(1)}, bf16[16,512]{1,0:T(8,128)(2,1)S(1)}, u32[]{:S(2)}, u32[]{:S(2)}) %collective-permute-start.8) | collective-permute-done | bytes 16416 | tf_op jit(solution)/shard_map/ppermute | solution.py:10
  64.4 4.9 %collective-permute-start.9 = (bf16[16,512]{1,0:T(8,128)(2,1)S(1)}, bf16[16,512]{1,0:T(8,128)(2,1)S(1)}, u32[]{:S(2)}, u32[]{:S(2)}) collective-permute-start(bf16[16,512]{1,0:T(8,128)(2,1)S(1)} %get-tuple-element.454), channel_id=1, source_target_pairs={{0,16},{1,17},{2,18},{3,19},{4,20},{5,21},{6,22},{7,23},{8,24},{9,... | collective-permute-start | bytes 49160 | tf_op jit(solution)/shard_map/ppermute | solution.py:10
  72.1 3.4 %collective-permute-start.12 = (bf16[16,512]{1,0:T(8,128)(2,1)S(1)}, bf16[16,512]{1,0:T(8,128)(2,1)S(1)}, u32[]{:S(2)}, u32[]{:S(2)}) collective-permute-start(bf16[16,512]{1,0:T(8,128)(2,1)S(1)} %get-tuple-element.455), channel_id=1, source_target_pairs={{32,0},{33,1},{34,2},{35,3},{36,4},{37,5},{38,6},{39,7},{40,8},{41... | collective-permute-start | bytes 49160 | tf_op jit(solution)/shard_map/ppermute | solution.py:10
  75.5 2.3 %collective-permute-done.12 = bf16[16,512]{1,0:T(8,128)(2,1)S(1)} collective-permute-done((bf16[16,512]{1,0:T(8,128)(2,1)S(1)}, bf16[16,512]{1,0:T(8,128)(2,1)S(1)}, u32[]{:S(2)}, u32[]{:S(2)}) %collective-permute-start.12) | collective-permute-done | bytes 16416 | tf_op jit(solution)/shard_map/ppermute | solution.py:10
  77.8 6.7 %collective-permute-start.13 = (bf16[16,512]{1,0:T(8,128)(2,1)S(1)}, bf16[16,512]{1,0:T(8,128)(2,1)S(1)}, u32[]{:S(2)}, u32[]{:S(2)}) collective-permute-start(bf16[16,512]{1,0:T(8,128)(2,1)S(1)} %get-tuple-element.456), channel_id=1, source_target_pairs={{0,64},{1,65},{2,66},{3,67},{4,68},{5,69},{6,70},{7,71},{8,72},{9,... | collective-permute-start | bytes 49160 | tf_op jit(solution)/shard_map/ppermute | solution.py:10
  86.4 4.8 %collective-permute-done.14 = bf16[16,512]{1,0:T(8,128)(2,1)S(1)} collective-permute-done((bf16[16,512]{1,0:T(8,128)(2,1)S(1)}, bf16[16,512]{1,0:T(8,128)(2,1)S(1)}, u32[]{:S(2)}, u32[]{:S(2)}) %collective-permute-start.14) | collective-permute-done | bytes 16416 | tf_op jit(solution)/shard_map/ppermute | solution.py:10
  91.2 4.0 %collective-permute-start.16 = (bf16[16,512]{1,0:T(8,128)(2,1)S(1)}, bf16[16,512]{1,0:T(8,128)(2,1)S(1)}, u32[]{:S(2)}, u32[]{:S(2)}) collective-permute-start(bf16[16,512]{1,0:T(8,128)(2,1)S(1)} %get-tuple-element.457), channel_id=1, source_target_pairs={{0,128},{1,129},{2,130},{3,131},{4,132},{5,133},{6,134},{7,135},{8... | collective-permute-start | bytes 49160 | tf_op jit(solution)/shard_map/ppermute | solution.py:10
  98.2 7.1 %collective-permute-done.15 = bf16[16,512]{1,0:T(8,128)(2,1)S(1)} collective-permute-done((bf16[16,512]{1,0:T(8,128)(2,1)S(1)}, bf16[16,512]{1,0:T(8,128)(2,1)S(1)}, u32[]{:S(2)}, u32[]{:S(2)}) %collective-permute-start.15) | collective-permute-done | bytes 16416 | tf_op jit(solution)/shard_map/ppermute | solution.py:10
  106.7 7.9 %collective-permute-start.18 = (bf16[16,512]{1,0:T(8,128)(2,1)S(1)}, bf16[16,512]{1,0:T(8,128)(2,1)S(1)}, u32[]{:S(2)}, u32[]{:S(2)}) collective-permute-start(bf16[16,512]{1,0:T(8,128)(2,1)S(1)} %get-tuple-element.387), channel_id=1, source_target_pairs={{0,128},{1,129},{2,130},{3,131},{4,132},{5,133},{6,134},{7,135},{8... | collective-permute-start | bytes 49160 | tf_op jit(solution)/shard_map/ppermute | solution.py:10
  115.5 2.9 %collective-permute-start.19 = (bf16[16,512]{1,0:T(8,128)(2,1)S(1)}, bf16[16,512]{1,0:T(8,128)(2,1)S(1)}, u32[]{:S(2)}, u32[]{:S(2)}) collective-permute-start(bf16[16,512]{1,0:T(8,128)(2,1)S(1)} %get-tuple-element.388), channel_id=1, source_target_pairs={{64,0},{65,1},{66,2},{67,3},{68,4},{69,5},{70,6},{71,7},{72,8},{73... | collective-permute-start | bytes 49160 | tf_op jit(solution)/shard_map/ppermute | solution.py:10
  118.4 5.6 %collective-permute-start.20 = (bf16[16,512]{1,0:T(8,128)(2,1)S(1)}, bf16[16,512]{1,0:T(8,128)(2,1)S(1)}, u32[]{:S(2)}, u32[]{:S(2)}) collective-permute-start(bf16[16,512]{1,0:T(8,128)(2,1)S(1)} %get-tuple-element.389), channel_id=1, source_target_pairs={{0,64},{1,65},{2,66},{3,67},{4,68},{5,69},{6,70},{7,71},{8,72},{9,... | collective-permute-start | bytes 49160 | tf_op jit(solution)/shard_map/ppermute | solution.py:10
  126.9 4.6 %collective-permute-start.22 = (bf16[16,512]{1,0:T(8,128)(2,1)S(1)}, bf16[16,512]{1,0:T(8,128)(2,1)S(1)}, u32[]{:S(2)}, u32[]{:S(2)}) collective-permute-start(bf16[16,512]{1,0:T(8,128)(2,1)S(1)} %get-tuple-element.391), channel_id=1, source_target_pairs={{0,32},{1,33},{2,34},{3,35},{4,36},{5,37},{6,38},{7,39},{8,40},{9,... | collective-permute-start | bytes 49160 | tf_op jit(solution)/shard_map/ppermute | solution.py:10
  132.4 13.1 %collective-permute-start.23 = (bf16[16,512]{1,0:T(8,128)(2,1)S(1)}, bf16[16,512]{1,0:T(8,128)(2,1)S(1)}, u32[]{:S(2)}, u32[]{:S(2)}) collective-permute-start(bf16[16,512]{1,0:T(8,128)(2,1)S(1)} %get-tuple-element.392), channel_id=1, source_target_pairs={{16,0},{17,1},{18,2},{19,3},{20,4},{21,5},{22,6},{23,7},{24,8},{25... | collective-permute-start | bytes 49160 | tf_op jit(solution)/shard_map/ppermute | solution.py:10
  145.5 5.0 %collective-permute-start.24 = (bf16[16,512]{1,0:T(8,128)(2,1)S(1)}, bf16[16,512]{1,0:T(8,128)(2,1)S(1)}, u32[]{:S(2)}, u32[]{:S(2)}) collective-permute-start(bf16[16,512]{1,0:T(8,128)(2,1)S(1)} %get-tuple-element.393), channel_id=1, source_target_pairs={{0,16},{1,17},{2,18},{3,19},{4,20},{5,21},{6,22},{7,23},{8,24},{9,... | collective-permute-start | bytes 49160 | tf_op jit(solution)/shard_map/ppermute | solution.py:10
  151.5 2.2 %collective-permute-start.25 = (bf16[16,512]{1,0:T(8,128)(2,1)S(1)}, bf16[16,512]{1,0:T(8,128)(2,1)S(1)}, u32[]{:S(2)}, u32[]{:S(2)}) collective-permute-start(bf16[16,512]{1,0:T(8,128)(2,1)S(1)} %get-tuple-element.394), channel_id=1, source_target_pairs={{8,0},{9,1},{10,2},{11,3},{12,4},{13,5},{14,6},{15,7},{16,8},{17,9... | collective-permute-start | bytes 49160 | tf_op jit(solution)/shard_map/ppermute | solution.py:10
  153.7 7.0 %collective-permute-start.26 = (bf16[16,512]{1,0:T(8,128)(2,1)S(1)}, bf16[16,512]{1,0:T(8,128)(2,1)S(1)}, u32[]{:S(2)}, u32[]{:S(2)}) collective-permute-start(bf16[16,512]{1,0:T(8,128)(2,1)S(1)} %get-tuple-element.395), channel_id=1, source_target_pairs={{0,8},{1,9},{2,10},{3,11},{4,12},{5,13},{6,14},{7,15},{8,16},{9,17... | collective-permute-start | bytes 49160 | tf_op jit(solution)/shard_map/ppermute | solution.py:10
  161.6 2.5 %collective-permute-start.27 = (bf16[16,512]{1,0:T(8,128)(2,1)S(1)}, bf16[16,512]{1,0:T(8,128)(2,1)S(1)}, u32[]{:S(2)}, u32[]{:S(2)}) collective-permute-start(bf16[16,512]{1,0:T(8,128)(2,1)S(1)} %get-tuple-element.396), channel_id=1, source_target_pairs={{4,0},{5,1},{6,2},{7,3},{8,4},{9,5},{10,6},{11,7},{12,8},{13,9},{1... | collective-permute-start | bytes 49160 | tf_op jit(solution)/shard_map/ppermute | solution.py:10
  164.1 7.3 %collective-permute-start.28 = (bf16[16,512]{1,0:T(8,128)(2,1)S(1)}, bf16[16,512]{1,0:T(8,128)(2,1)S(1)}, u32[]{:S(2)}, u32[]{:S(2)}) collective-permute-start(bf16[16,512]{1,0:T(8,128)(2,1)S(1)} %get-tuple-element.397), channel_id=1, source_target_pairs={{0,4},{1,5},{2,6},{3,7},{4,8},{5,9},{6,10},{7,11},{8,12},{9,13},{1... | collective-permute-start | bytes 49160 | tf_op jit(solution)/shard_map/ppermute | solution.py:10
  172.2 2.2 %collective-permute-start.29 = (bf16[16,512]{1,0:T(8,128)(2,1)S(1)}, bf16[16,512]{1,0:T(8,128)(2,1)S(1)}, u32[]{:S(2)}, u32[]{:S(2)}) collective-permute-start(bf16[16,512]{1,0:T(8,128)(2,1)S(1)} %get-tuple-element.398), channel_id=1, source_target_pairs={{2,0},{3,1},{4,2},{5,3},{6,4},{7,5},{8,6},{9,7},{10,8},{11,9},{12,... | collective-permute-start | bytes 49160 | tf_op jit(solution)/shard_map/ppermute | solution.py:10
  174.4 9.1 %collective-permute-start.30 = (bf16[16,512]{1,0:T(8,128)(2,1)S(1)}, bf16[16,512]{1,0:T(8,128)(2,1)S(1)}, u32[]{:S(2)}, u32[]{:S(2)}) collective-permute-start(bf16[16,512]{1,0:T(8,128)(2,1)S(1)} %get-tuple-element.399), channel_id=1, source_target_pairs={{0,2},{1,3},{2,4},{3,5},{4,6},{5,7},{6,8},{7,9},{8,10},{9,11},{10,... | collective-permute-start | bytes 49160 | tf_op jit(solution)/shard_map/ppermute | solution.py:10
  184.4 3.2 %collective-permute-start.31 = (bf16[16,512]{1,0:T(8,128)(2,1)S(1)}, bf16[16,512]{1,0:T(8,128)(2,1)S(1)}, u32[]{:S(2)}, u32[]{:S(2)}) collective-permute-start(bf16[16,512]{1,0:T(8,128)(2,1)S(1)} %get-tuple-element.400), channel_id=1, source_target_pairs={{1,0},{2,1},{3,2},{4,3},{5,4},{6,5},{7,6},{8,7},{9,8},{10,9},{11,1... | collective-permute-start | bytes 49160 | tf_op jit(solution)/shard_map/ppermute | solution.py:10
  187.6 8.7 %collective-permute-start.32 = (bf16[16,512]{1,0:T(8,128)(2,1)S(1)}, bf16[16,512]{1,0:T(8,128)(2,1)S(1)}, u32[]{:S(2)}, u32[]{:S(2)}) collective-permute-start(bf16[16,512]{1,0:T(8,128)(2,1)S(1)} %get-tuple-element.401), channel_id=1, source_target_pairs={{0,1},{1,2},{2,3},{3,4},{4,5},{5,6},{6,7},{7,8},{8,9},{9,10},{10,1... | collective-permute-start | bytes 49160 | tf_op jit(solution)/shard_map/ppermute | solution.py:10
  197.9 2.1 collective-permute-start.33
  200.2 8.4 %collective-permute-done.33 = bf16[16,512]{1,0:T(8,128)(2,1)S(1)} collective-permute-done((bf16[16,512]{1,0:T(8,128)(2,1)S(1)}, bf16[16,512]{1,0:T(8,128)(2,1)S(1)}, u32[]{:S(2)}, u32[]{:S(2)}) %collective-permute-start.33) | collective-permute-done | bytes 16416 | tf_op jit(solution)/shard_map/ppermute | solution.py:10
  (103 shorter events, 35.8 us)
Async XLA Ops:
  3.1 6.8 %collective-permute-start = (bf16[16,512]{1,0:T(8,128)(2,1)S(1)}, bf16[16,512]{1,0:T(8,128)(2,1)S(1)}, u32[]{:S(2)}, u32[]{:S(2)}) collective-permute-start(bf16[16,512]{1,0:T(8,128)(2,1)S(1)} %select_convert_fusion), channel_id=1, source_target_pairs={{0,1},{1,2},{2,3},{3,4},{4,5},{5,6},{6,7},{7,8},{8,9},{9,10},{10,1... | collective-permute-start | bytes 49160 | tf_op jit(solution)/shard_map/ppermute | solution.py:10
  10.3 10.1 %collective-permute-start.1 = (bf16[16,512]{1,0:T(8,128)(2,1)S(1)}, bf16[16,512]{1,0:T(8,128)(2,1)S(1)}, u32[]{:S(2)}, u32[]{:S(2)}) collective-permute-start(bf16[16,512]{1,0:T(8,128)(2,1)S(1)} %get-tuple-element.450), channel_id=1, source_target_pairs={{0,1},{1,2},{2,3},{3,4},{4,5},{5,6},{6,7},{7,8},{8,9},{9,10},{10,1... | collective-permute-start | bytes 49160 | tf_op jit(solution)/shard_map/ppermute | solution.py:10
  18.4 10.5 %collective-permute-start.2 = (bf16[16,512]{1,0:T(8,128)(2,1)S(1)}, bf16[16,512]{1,0:T(8,128)(2,1)S(1)}, u32[]{:S(2)}, u32[]{:S(2)}) collective-permute-start(bf16[16,512]{1,0:T(8,128)(2,1)S(1)} %get-tuple-element.450), channel_id=1, source_target_pairs={{1,0},{2,1},{3,2},{4,3},{5,4},{6,5},{7,6},{8,7},{9,8},{10,9},{11,1... | collective-permute-start | bytes 49160 | tf_op jit(solution)/shard_map/ppermute | solution.py:10
  28.9 6.8 %collective-permute-start.3 = (bf16[16,512]{1,0:T(8,128)(2,1)S(1)}, bf16[16,512]{1,0:T(8,128)(2,1)S(1)}, u32[]{:S(2)}, u32[]{:S(2)}) collective-permute-start(bf16[16,512]{1,0:T(8,128)(2,1)S(1)} %get-tuple-element.451), channel_id=1, source_target_pairs={{0,2},{1,3},{2,4},{3,5},{4,6},{5,7},{6,8},{7,9},{8,10},{9,11},{10,... | collective-permute-start | bytes 49160 | tf_op jit(solution)/shard_map/ppermute | solution.py:10
  30.9 10.8 %collective-permute-start.4 = (bf16[16,512]{1,0:T(8,128)(2,1)S(1)}, bf16[16,512]{1,0:T(8,128)(2,1)S(1)}, u32[]{:S(2)}, u32[]{:S(2)}) collective-permute-start(bf16[16,512]{1,0:T(8,128)(2,1)S(1)} %get-tuple-element.451), channel_id=1, source_target_pairs={{2,0},{3,1},{4,2},{5,3},{6,4},{7,5},{8,6},{9,7},{10,8},{11,9},{12,... | collective-permute-start | bytes 49160 | tf_op jit(solution)/shard_map/ppermute | solution.py:10
  43.6 8.4 %collective-permute-start.6 = (bf16[16,512]{1,0:T(8,128)(2,1)S(1)}, bf16[16,512]{1,0:T(8,128)(2,1)S(1)}, u32[]{:S(2)}, u32[]{:S(2)}) collective-permute-start(bf16[16,512]{1,0:T(8,128)(2,1)S(1)} %get-tuple-element.452), channel_id=1, source_target_pairs={{4,0},{5,1},{6,2},{7,3},{8,4},{9,5},{10,6},{11,7},{12,8},{13,9},{1... | collective-permute-start | bytes 49160 | tf_op jit(solution)/shard_map/ppermute | solution.py:10
  51.9 6.8 %collective-permute-start.7 = (bf16[16,512]{1,0:T(8,128)(2,1)S(1)}, bf16[16,512]{1,0:T(8,128)(2,1)S(1)}, u32[]{:S(2)}, u32[]{:S(2)}) collective-permute-start(bf16[16,512]{1,0:T(8,128)(2,1)S(1)} %get-tuple-element.453), channel_id=1, source_target_pairs={{0,8},{1,9},{2,10},{3,11},{4,12},{5,13},{6,14},{7,15},{8,16},{9,17... | collective-permute-start | bytes 49160 | tf_op jit(solution)/shard_map/ppermute | solution.py:10
  53.8 8.7 %collective-permute-start.8 = (bf16[16,512]{1,0:T(8,128)(2,1)S(1)}, bf16[16,512]{1,0:T(8,128)(2,1)S(1)}, u32[]{:S(2)}, u32[]{:S(2)}) collective-permute-start(bf16[16,512]{1,0:T(8,128)(2,1)S(1)} %get-tuple-element.453), channel_id=1, source_target_pairs={{8,0},{9,1},{10,2},{11,3},{12,4},{13,5},{14,6},{15,7},{16,8},{17,9... | collective-permute-start | bytes 49160 | tf_op jit(solution)/shard_map/ppermute | solution.py:10
  62.5 6.8 %collective-permute-start.10 = (bf16[16,512]{1,0:T(8,128)(2,1)S(1)}, bf16[16,512]{1,0:T(8,128)(2,1)S(1)}, u32[]{:S(2)}, u32[]{:S(2)}) collective-permute-start(bf16[16,512]{1,0:T(8,128)(2,1)S(1)} %get-tuple-element.454), channel_id=1, source_target_pairs={{16,0},{17,1},{18,2},{19,3},{20,4},{21,5},{22,6},{23,7},{24,8},{25... | collective-permute-start | bytes 49160 | tf_op jit(solution)/shard_map/ppermute | solution.py:10
  64.4 5.7 %collective-permute-start.9 = (bf16[16,512]{1,0:T(8,128)(2,1)S(1)}, bf16[16,512]{1,0:T(8,128)(2,1)S(1)}, u32[]{:S(2)}, u32[]{:S(2)}) collective-permute-start(bf16[16,512]{1,0:T(8,128)(2,1)S(1)} %get-tuple-element.454), channel_id=1, source_target_pairs={{0,16},{1,17},{2,18},{3,19},{4,20},{5,21},{6,22},{7,23},{8,24},{9,... | collective-permute-start | bytes 49160 | tf_op jit(solution)/shard_map/ppermute | solution.py:10
  72.1 5.7 %collective-permute-start.12 = (bf16[16,512]{1,0:T(8,128)(2,1)S(1)}, bf16[16,512]{1,0:T(8,128)(2,1)S(1)}, u32[]{:S(2)}, u32[]{:S(2)}) collective-permute-start(bf16[16,512]{1,0:T(8,128)(2,1)S(1)} %get-tuple-element.455), channel_id=1, source_target_pairs={{32,0},{33,1},{34,2},{35,3},{36,4},{37,5},{38,6},{39,7},{40,8},{41... | collective-permute-start | bytes 49160 | tf_op jit(solution)/shard_map/ppermute | solution.py:10
  77.8 8.7 %collective-permute-start.13 = (bf16[16,512]{1,0:T(8,128)(2,1)S(1)}, bf16[16,512]{1,0:T(8,128)(2,1)S(1)}, u32[]{:S(2)}, u32[]{:S(2)}) collective-permute-start(bf16[16,512]{1,0:T(8,128)(2,1)S(1)} %get-tuple-element.456), channel_id=1, source_target_pairs={{0,64},{1,65},{2,66},{3,67},{4,68},{5,69},{6,70},{7,71},{8,72},{9,... | collective-permute-start | bytes 49160 | tf_op jit(solution)/shard_map/ppermute | solution.py:10
  84.5 6.7 %collective-permute-start.14 = (bf16[16,512]{1,0:T(8,128)(2,1)S(1)}, bf16[16,512]{1,0:T(8,128)(2,1)S(1)}, u32[]{:S(2)}, u32[]{:S(2)}) collective-permute-start(bf16[16,512]{1,0:T(8,128)(2,1)S(1)} %get-tuple-element.456), channel_id=1, source_target_pairs={{64,0},{65,1},{66,2},{67,3},{68,4},{69,5},{70,6},{71,7},{72,8},{73... | collective-permute-start | bytes 49160 | tf_op jit(solution)/shard_map/ppermute | solution.py:10
  91.2 7.0 %collective-permute-start.16 = (bf16[16,512]{1,0:T(8,128)(2,1)S(1)}, bf16[16,512]{1,0:T(8,128)(2,1)S(1)}, u32[]{:S(2)}, u32[]{:S(2)}) collective-permute-start(bf16[16,512]{1,0:T(8,128)(2,1)S(1)} %get-tuple-element.457), channel_id=1, source_target_pairs={{0,128},{1,129},{2,130},{3,131},{4,132},{5,133},{6,134},{7,135},{8... | collective-permute-start | bytes 49160 | tf_op jit(solution)/shard_map/ppermute | solution.py:10
  96.9 8.4 %collective-permute-start.15 = (bf16[16,512]{1,0:T(8,128)(2,1)S(1)}, bf16[16,512]{1,0:T(8,128)(2,1)S(1)}, u32[]{:S(2)}, u32[]{:S(2)}) collective-permute-start(bf16[16,512]{1,0:T(8,128)(2,1)S(1)} %get-tuple-element.457), channel_id=1, source_target_pairs={{128,0},{129,1},{130,2},{131,3},{132,4},{133,5},{134,6},{135,7},{1... | collective-permute-start | bytes 49160 | tf_op jit(solution)/shard_map/ppermute | solution.py:10
  105.4 9.8 %collective-permute-start.17 = (bf16[16,512]{1,0:T(8,128)(2,1)S(1)}, bf16[16,512]{1,0:T(8,128)(2,1)S(1)}, u32[]{:S(2)}, u32[]{:S(2)}) collective-permute-start(bf16[16,512]{1,0:T(8,128)(2,1)S(1)} %get-tuple-element.386), channel_id=1, source_target_pairs={{128,0},{129,1},{130,2},{131,3},{132,4},{133,5},{134,6},{135,7},{1... | collective-permute-start | bytes 49160 | tf_op jit(solution)/shard_map/ppermute | solution.py:10
  106.7 8.8 %collective-permute-start.18 = (bf16[16,512]{1,0:T(8,128)(2,1)S(1)}, bf16[16,512]{1,0:T(8,128)(2,1)S(1)}, u32[]{:S(2)}, u32[]{:S(2)}) collective-permute-start(bf16[16,512]{1,0:T(8,128)(2,1)S(1)} %get-tuple-element.387), channel_id=1, source_target_pairs={{0,128},{1,129},{2,130},{3,131},{4,132},{5,133},{6,134},{7,135},{8... | collective-permute-start | bytes 49160 | tf_op jit(solution)/shard_map/ppermute | solution.py:10
  115.5 8.6 %collective-permute-start.19 = (bf16[16,512]{1,0:T(8,128)(2,1)S(1)}, bf16[16,512]{1,0:T(8,128)(2,1)S(1)}, u32[]{:S(2)}, u32[]{:S(2)}) collective-permute-start(bf16[16,512]{1,0:T(8,128)(2,1)S(1)} %get-tuple-element.388), channel_id=1, source_target_pairs={{64,0},{65,1},{66,2},{67,3},{68,4},{69,5},{70,6},{71,7},{72,8},{73... | collective-permute-start | bytes 49160 | tf_op jit(solution)/shard_map/ppermute | solution.py:10
  118.4 6.5 %collective-permute-start.20 = (bf16[16,512]{1,0:T(8,128)(2,1)S(1)}, bf16[16,512]{1,0:T(8,128)(2,1)S(1)}, u32[]{:S(2)}, u32[]{:S(2)}) collective-permute-start(bf16[16,512]{1,0:T(8,128)(2,1)S(1)} %get-tuple-element.389), channel_id=1, source_target_pairs={{0,64},{1,65},{2,66},{3,67},{4,68},{5,69},{6,70},{7,71},{8,72},{9,... | collective-permute-start | bytes 49160 | tf_op jit(solution)/shard_map/ppermute | solution.py:10
  124.9 6.6 %collective-permute-start.21 = (bf16[16,512]{1,0:T(8,128)(2,1)S(1)}, bf16[16,512]{1,0:T(8,128)(2,1)S(1)}, u32[]{:S(2)}, u32[]{:S(2)}) collective-permute-start(bf16[16,512]{1,0:T(8,128)(2,1)S(1)} %get-tuple-element.390), channel_id=1, source_target_pairs={{32,0},{33,1},{34,2},{35,3},{36,4},{37,5},{38,6},{39,7},{40,8},{41... | collective-permute-start | bytes 49160 | tf_op jit(solution)/shard_map/ppermute | solution.py:10
  126.9 5.4 %collective-permute-start.22 = (bf16[16,512]{1,0:T(8,128)(2,1)S(1)}, bf16[16,512]{1,0:T(8,128)(2,1)S(1)}, u32[]{:S(2)}, u32[]{:S(2)}) collective-permute-start(bf16[16,512]{1,0:T(8,128)(2,1)S(1)} %get-tuple-element.391), channel_id=1, source_target_pairs={{0,32},{1,33},{2,34},{3,35},{4,36},{5,37},{6,38},{7,39},{8,40},{9,... | collective-permute-start | bytes 49160 | tf_op jit(solution)/shard_map/ppermute | solution.py:10
  132.4 18.1 %collective-permute-start.23 = (bf16[16,512]{1,0:T(8,128)(2,1)S(1)}, bf16[16,512]{1,0:T(8,128)(2,1)S(1)}, u32[]{:S(2)}, u32[]{:S(2)}) collective-permute-start(bf16[16,512]{1,0:T(8,128)(2,1)S(1)} %get-tuple-element.392), channel_id=1, source_target_pairs={{16,0},{17,1},{18,2},{19,3},{20,4},{21,5},{22,6},{23,7},{24,8},{25... | collective-permute-start | bytes 49160 | tf_op jit(solution)/shard_map/ppermute | solution.py:10
  145.5 5.9 %collective-permute-start.24 = (bf16[16,512]{1,0:T(8,128)(2,1)S(1)}, bf16[16,512]{1,0:T(8,128)(2,1)S(1)}, u32[]{:S(2)}, u32[]{:S(2)}) collective-permute-start(bf16[16,512]{1,0:T(8,128)(2,1)S(1)} %get-tuple-element.393), channel_id=1, source_target_pairs={{0,16},{1,17},{2,18},{3,19},{4,20},{5,21},{6,22},{7,23},{8,24},{9,... | collective-permute-start | bytes 49160 | tf_op jit(solution)/shard_map/ppermute | solution.py:10
  151.5 9.2 %collective-permute-start.25 = (bf16[16,512]{1,0:T(8,128)(2,1)S(1)}, bf16[16,512]{1,0:T(8,128)(2,1)S(1)}, u32[]{:S(2)}, u32[]{:S(2)}) collective-permute-start(bf16[16,512]{1,0:T(8,128)(2,1)S(1)} %get-tuple-element.394), channel_id=1, source_target_pairs={{8,0},{9,1},{10,2},{11,3},{12,4},{13,5},{14,6},{15,7},{16,8},{17,9... | collective-permute-start | bytes 49160 | tf_op jit(solution)/shard_map/ppermute | solution.py:10
  153.7 7.8 %collective-permute-start.26 = (bf16[16,512]{1,0:T(8,128)(2,1)S(1)}, bf16[16,512]{1,0:T(8,128)(2,1)S(1)}, u32[]{:S(2)}, u32[]{:S(2)}) collective-permute-start(bf16[16,512]{1,0:T(8,128)(2,1)S(1)} %get-tuple-element.395), channel_id=1, source_target_pairs={{0,8},{1,9},{2,10},{3,11},{4,12},{5,13},{6,14},{7,15},{8,16},{9,17... | collective-permute-start | bytes 49160 | tf_op jit(solution)/shard_map/ppermute | solution.py:10
  161.6 9.8 %collective-permute-start.27 = (bf16[16,512]{1,0:T(8,128)(2,1)S(1)}, bf16[16,512]{1,0:T(8,128)(2,1)S(1)}, u32[]{:S(2)}, u32[]{:S(2)}) collective-permute-start(bf16[16,512]{1,0:T(8,128)(2,1)S(1)} %get-tuple-element.396), channel_id=1, source_target_pairs={{4,0},{5,1},{6,2},{7,3},{8,4},{9,5},{10,6},{11,7},{12,8},{13,9},{1... | collective-permute-start | bytes 49160 | tf_op jit(solution)/shard_map/ppermute | solution.py:10
  164.1 8.1 %collective-permute-start.28 = (bf16[16,512]{1,0:T(8,128)(2,1)S(1)}, bf16[16,512]{1,0:T(8,128)(2,1)S(1)}, u32[]{:S(2)}, u32[]{:S(2)}) collective-permute-start(bf16[16,512]{1,0:T(8,128)(2,1)S(1)} %get-tuple-element.397), channel_id=1, source_target_pairs={{0,4},{1,5},{2,6},{3,7},{4,8},{5,9},{6,10},{7,11},{8,12},{9,13},{1... | collective-permute-start | bytes 49160 | tf_op jit(solution)/shard_map/ppermute | solution.py:10
  172.2 11.3 %collective-permute-start.29 = (bf16[16,512]{1,0:T(8,128)(2,1)S(1)}, bf16[16,512]{1,0:T(8,128)(2,1)S(1)}, u32[]{:S(2)}, u32[]{:S(2)}) collective-permute-start(bf16[16,512]{1,0:T(8,128)(2,1)S(1)} %get-tuple-element.398), channel_id=1, source_target_pairs={{2,0},{3,1},{4,2},{5,3},{6,4},{7,5},{8,6},{9,7},{10,8},{11,9},{12,... | collective-permute-start | bytes 49160 | tf_op jit(solution)/shard_map/ppermute | solution.py:10
  174.4 9.9 %collective-permute-start.30 = (bf16[16,512]{1,0:T(8,128)(2,1)S(1)}, bf16[16,512]{1,0:T(8,128)(2,1)S(1)}, u32[]{:S(2)}, u32[]{:S(2)}) collective-permute-start(bf16[16,512]{1,0:T(8,128)(2,1)S(1)} %get-tuple-element.399), channel_id=1, source_target_pairs={{0,2},{1,3},{2,4},{3,5},{4,6},{5,7},{6,8},{7,9},{8,10},{9,11},{10,... | collective-permute-start | bytes 49160 | tf_op jit(solution)/shard_map/ppermute | solution.py:10
  184.4 11.9 %collective-permute-start.31 = (bf16[16,512]{1,0:T(8,128)(2,1)S(1)}, bf16[16,512]{1,0:T(8,128)(2,1)S(1)}, u32[]{:S(2)}, u32[]{:S(2)}) collective-permute-start(bf16[16,512]{1,0:T(8,128)(2,1)S(1)} %get-tuple-element.400), channel_id=1, source_target_pairs={{1,0},{2,1},{3,2},{4,3},{5,4},{6,5},{7,6},{8,7},{9,8},{10,9},{11,1... | collective-permute-start | bytes 49160 | tf_op jit(solution)/shard_map/ppermute | solution.py:10
  187.6 9.5 %collective-permute-start.32 = (bf16[16,512]{1,0:T(8,128)(2,1)S(1)}, bf16[16,512]{1,0:T(8,128)(2,1)S(1)}, u32[]{:S(2)}, u32[]{:S(2)}) collective-permute-start(bf16[16,512]{1,0:T(8,128)(2,1)S(1)} %get-tuple-element.401), channel_id=1, source_target_pairs={{0,1},{1,2},{2,3},{3,4},{4,5},{5,6},{6,7},{7,8},{8,9},{9,10},{10,1... | collective-permute-start | bytes 49160 | tf_op jit(solution)/shard_map/ppermute | solution.py:10
  197.9 10.6 %collective-permute-start.33 = (bf16[16,512]{1,0:T(8,128)(2,1)S(1)}, bf16[16,512]{1,0:T(8,128)(2,1)S(1)}, u32[]{:S(2)}, u32[]{:S(2)}) collective-permute-start(bf16[16,512]{1,0:T(8,128)(2,1)S(1)} %get-tuple-element.402), channel_id=1, source_target_pairs={{1,0},{2,1},{3,2},{4,3},{5,4},{6,5},{7,6},{8,7},{9,8},{10,9},{11,1... | collective-permute-start | bytes 49160 | tf_op jit(solution)/shard_map/ppermute | solution.py:10
  (5 other events, 224.0 us)
where the time goes:
time: 210 us; the launch traced here: 209 us
  starting transfers between devices  146 us (70%)
  waiting for transfers between devices  52.6 us (25%)
  local copies, waits for them, and re-layouts  4.37 us (2%)
  matrix products  3.05 us (1%)
    ppermute x34, starting transfers between devices, from_behind(): return lax.ppermute(x, axis, pairs)  146 us
    ppermute x34, waiting for transfers between devices, from_behind(): return lax.ppermute(x, axis, pairs)  52.6 us
  transfers between devices with their start and end apart: 34, of which 17 were waited for; matrix products, arithmetic and copies ran while one was open for 2% of the time, Pallas kernels for 0%

commit v1 on v0

v1 whole, which is shorter than its diff:
```python
import functools

import jax
import jax.numpy as jnp
from jax import lax
from jax.experimental import pallas as pl
from jax.experimental.pallas import tpu as pltpu
from jax.sharding import PartitionSpec as P

MESH = pl.DeviceIdType.MESH
F32 = jnp.float32
BF16 = jnp.bfloat16


def kernel(
    row_len,
    levels,
    rhs_hbm,
    diag_hbm,
    in_hbm,
    out_hbm,
    up_hbm,
    cross_hbm,
    down_hbm,
    rank_hbm,
    product,
    rhs,
    diag,
    leaf_in,
    leaf_out,
    up,
    cross,
    down,
    rank,
    leaf_coef,
    coef,
    child,
    cross_sum,
    to_child,
    down_in,
    leaf_down,
    load_sem,
    send_sem,
    recv_sem,
):
    me = lax.axis_index("tx") * row_len + lax.axis_index("ty")
    rows, width = coef.shape
    leaf_width = leaf_coef.shape[1]
    half = 1
    for height in range(2, levels + 1):
        half = jnp.where(me % 2 ** (height - 1) == 0, 2 ** (height - 1), half)
    is_leaf_only = me == 0
    is_odd = me % 2 == 1
    is_root = me == 2 ** (levels - 1)
    is_upper = jnp.logical_and(me % 2 == 0, me > 0)
    sends_up = jnp.logical_and(me > 0, jnp.logical_not(is_root))
    on_left = (me // (2 * half)) % 2 == 0
    parent = jnp.where(on_left, me + half, me - half)
    quarter = half // 2
    peer = jnp.where(is_odd, me - 1, me + 1)

    def device(number):
        return (number // row_len, number % row_len)

    loads = [
        pltpu.make_async_copy(source, target, load_sem.at[at])
        for at, (source, target) in enumerate(
            (
                (rhs_hbm, rhs),
                (in_hbm, leaf_in),
                (rank_hbm, rank),
                (up_hbm, up),
                (cross_hbm, cross),
                (down_hbm, down),
                (diag_hbm, diag),
                (out_hbm, leaf_out),
            )
        )
    ]
    load_rhs, load_in, load_rank, load_up, load_cross, load_down, load_diag, load_out = loads
    for load in loads:
        load.start()

    barrier = pltpu.get_barrier_semaphore()

    def greet(number):
        pl.semaphore_signal(barrier, inc=1, device_id=device(number), device_id_type=MESH)

    greet(peer)

    @pl.when(sends_up)
    def _():
        greet(parent)

    @pl.when(is_upper)
    def _():
        greet(me - quarter)
        greet(me + quarter)

    def remote(source, target, at_send, at_recv, number):
        return pltpu.make_async_remote_copy(
            src_ref=source,
            dst_ref=target,
            send_sem=send_sem.at[at_send],
            recv_sem=recv_sem.at[at_recv],
            device_id=device(number),
            device_id_type=MESH,
        )

    left_part, right_part = pl.ds(0, width), pl.ds(width, width)
    narrow, narrow_right = pl.ds(0, leaf_width), pl.ds(width, leaf_width)

    load_rhs.wait()
    load_in.wait()
    load_rank.wait()
    leaf_keep = lax.broadcasted_iota(jnp.int32, (rows, leaf_width), 1) < rank[0, 0]
    node_keep = lax.broadcasted_iota(jnp.int32, (rows, width), 1) < rank[0, 1]
    projected = jnp.dot(rhs[...], leaf_in[...], preferred_element_type=F32)
    leaf_coef[...] = jnp.where(leaf_keep, projected, 0.0).astype(BF16)

    greeted = 1 + sends_up.astype(jnp.int32) + 2 * is_upper.astype(jnp.int32)
    pl.semaphore_wait(barrier, greeted)

    leaf_up = remote(leaf_coef, child.at[:, narrow], 0, 0, peer)
    up_left = remote(coef, child.at[:, left_part], 1, 0, parent)
    up_right = remote(coef, child.at[:, right_part], 1, 1, parent)
    down_left = remote(to_child.at[0], down_in, 2, 2, me - quarter)
    down_right = remote(to_child.at[1], down_in, 3, 2, me + quarter)
    leaf_left = remote(to_child.at[0, :, narrow], leaf_down, 2, 3, peer)

    def send_up(summed):
        coef[...] = jnp.where(node_keep, summed, 0.0).astype(BF16)

        @pl.when(on_left)
        def _():
            up_left.start()

        @pl.when(jnp.logical_not(on_left))
        def _():
            up_right.start()

    @pl.when(jnp.logical_not(is_odd))
    def _():
        leaf_up.start()

    @pl.when(is_odd)
    def _():
        load_up.wait()
        summed = jnp.dot(leaf_coef[...], up[1, 0, narrow, :], preferred_element_type=F32)
        leaf_up.wait_recv()
        summed += jnp.dot(child[:, narrow], up[0, 0, narrow, :], preferred_element_type=F32)
        send_up(summed)
        load_cross.wait()
        cross_sum[0, :, narrow] = jnp.dot(leaf_coef[...], cross[0, 0, narrow, narrow], preferred_element_type=F32)
        cross_sum[1, :, narrow] = jnp.dot(child[:, narrow], cross[1, 0, narrow, narrow], preferred_element_type=F32)

    @pl.when(is_upper)
    def _():
        load_up.wait()
        up_left.wait_recv()

        @pl.when(sends_up)
        def _():
            summed = jnp.dot(child[:, left_part], up[0, 0], preferred_element_type=F32)
            up_right.wait_recv()
            summed += jnp.dot(child[:, right_part], up[1, 0], preferred_element_type=F32)
            send_up(summed)
            load_cross.wait()
            cross_sum[0] = jnp.dot(child[:, right_part], cross[0, 0], preferred_element_type=F32)
            cross_sum[1] = jnp.dot(child[:, left_part], cross[1, 0], preferred_element_type=F32)

        @pl.when(is_root)
        def _():
            load_cross.wait()
            to_child[1] = jnp.dot(child[:, left_part], cross[1, 0], preferred_element_type=F32).astype(BF16)
            down_right.start()
            up_right.wait_recv()
            to_child[0] = jnp.dot(child[:, right_part], cross[0, 0], preferred_element_type=F32).astype(BF16)
            down_left.start()

    load_diag.wait()
    product[...] = jnp.dot(rhs[...], diag[...], preferred_element_type=F32)
    load_out.wait()
    load_down.wait()

    @pl.when(sends_up)
    def _():
        down_left.wait_recv()
        down_in[...] = jnp.where(node_keep, down_in[...], jnp.zeros_like(down_in))

    @pl.when(is_odd)
    def _():
        to_left = cross_sum[0, :, narrow] + jnp.dot(down_in[...], down[0, 0, :, narrow], preferred_element_type=F32)
        to_child[0, :, narrow] = to_left.astype(BF16)
        leaf_left.start()
        to_right = cross_sum[1, :, narrow] + jnp.dot(down_in[...], down[1, 0, :, narrow], preferred_element_type=F32)
        leaf_down[...] = to_right.astype(BF16)

    @pl.when(jnp.logical_and(is_upper, sends_up))
    def _():
        to_left = cross_sum[0] + jnp.dot(down_in[...], down[0, 0], preferred_element_type=F32)
        to_child[0] = to_left.astype(BF16)
        down_left.start()
        to_right = cross_sum[1] + jnp.dot(down_in[...], down[1, 0], preferred_element_type=F32)
        to_child[1] = to_right.astype(BF16)
        down_right.start()

    @pl.when(jnp.logical_not(is_odd))
    def _():
        leaf_left.wait_recv()

    kept = jnp.where(leaf_keep, leaf_down[...], jnp.zeros_like(leaf_down))
    product[...] += jnp.dot(kept, leaf_out[...], preferred_element_type=F32)

    @pl.when(is_leaf_only)
    def _():
        load_up.wait()
        load_cross.wait()

    @pl.when(is_root)
    def _():
        pass

    @pl.when(jnp.logical_not(is_odd))
    def _():
        leaf_up.wait_send()

    @pl.when(is_odd)
    def _():
        leaf_left.wait_send()

    @pl.when(sends_up)
    def _():
        up_left.wait_send()

    @pl.when(is_upper)
    def _():
        down_left.wait_send()
        down_right.wait_send()


def on_device(levels, row_len, rhs, diag_blocks, leaf_in, leaf_out, up_maps, cross_maps, down_maps, node_rank):
    rows, leaf = rhs.shape
    width, leaf_width = up_maps.shape[-1], leaf_in.shape[1]
    operands = (rhs, diag_blocks, leaf_in, leaf_out, up_maps, cross_maps, down_maps)
    return pl.pallas_call(
        functools.partial(kernel, row_len, levels),
        out_shape=jax.ShapeDtypeStruct((rows, leaf), F32),
        in_specs=[pl.BlockSpec(memory_space=pl.ANY)] * 8,
        out_specs=pl.BlockSpec(memory_space=pltpu.VMEM),
        scratch_shapes=[pltpu.VMEM(each.shape, each.dtype) for each in operands]
        + [
            pltpu.SMEM(node_rank.shape, node_rank.dtype),
            pltpu.VMEM((rows, leaf_width), BF16),
            pltpu.VMEM((rows, width), BF16),
            pltpu.VMEM((rows, 2 * width), BF16),
            pltpu.VMEM((2, rows, width), F32),
            pltpu.VMEM((2, rows, width), BF16),
            pltpu.VMEM((rows, width), BF16),
            pltpu.VMEM((rows, leaf_width), BF16),
            pltpu.SemaphoreType.DMA((8,)),
            pltpu.SemaphoreType.DMA((4,)),
            pltpu.SemaphoreType.DMA((4,)),
        ],
        compiler_params=pltpu.CompilerParams(
            collective_id=0, has_side_effects=True, vmem_limit_bytes=48 * 2**20
        ),
    )(*operands, node_rank)


def solution(mesh):
    row_len = mesh.shape["ty"]
    levels = (mesh.shape["tx"] * row_len).bit_length() - 1
    in_specs = (
        P(None, ("tx", "ty")),
        P(("tx", "ty"), None),
        P(("tx", "ty"), None),
        P(("tx", "ty"), None),
        P(None, ("tx", "ty"), None, None),
        P(None, ("tx", "ty"), None, None),
        P(None, ("tx", "ty"), None, None),
        P(("tx", "ty"), None),
    )
    return jax.shard_map(
        functools.partial(on_device, levels, row_len),
        mesh=mesh,
        in_specs=in_specs,
        out_specs=P(None, ("tx", "ty")),
        check_vma=False,
    )
```

time: 210 us -> 83.1 us (0.40)
  the two profiles are of different devices: /device:TPU:127 before, /device:TPU:2 now
where the time goes in v1:
time: 83.1 us; the launch traced here: 82.7 us
  Pallas kernels  74.2 us (89%)
  local copies, waits for them, and re-layouts  8.51 us (10%)
    pallas_call x1, Pallas kernels, on_device(): pl.pallas_call(functools.partial(kernel, row_len, levels), out_shape=jax....  74.2 us
    unnamed x17, local copies, waits for them, and re-layouts  8.51 us

profile of v1, /device:TPU:2, one launch (start us, length us, event | category | flops | bytes accessed | tf_op | source)
XLA Modules:
  0.0 82.7 jit_solution(3456486941012141982)
XLA Ops:
  0.0 0.0 copy-start
  0.0 1.2 %copy-done = bf16[2,1,512,512]{3,2,1,0:T(8,128)(2,1)S(1)} copy-done((bf16[2,1,512,512]{3,2,1,0:T(8,128)(2,1)S(1)}, bf16[2,1,512,512]{3,2,1,0:T(8,128)(2,1)}, u32[]{:S(2)}) %copy-start) | copy-done | bytes 1048600
  1.2 0.0 copy-start.1
  1.2 1.2 %copy-done.1 = bf16[2,1,512,512]{3,2,1,0:T(8,128)(2,1)S(1)} copy-done((bf16[2,1,512,512]{3,2,1,0:T(8,128)(2,1)S(1)}, bf16[2,1,512,512]{3,2,1,0:T(8,128)(2,1)}, u32[]{:S(2)}) %copy-start.1) | copy-done | bytes 1048600
  2.5 0.0 copy-start.2
  2.5 1.2 %copy-done.2 = bf16[2,1,512,512]{3,2,1,0:T(8,128)(2,1)S(1)} copy-done((bf16[2,1,512,512]{3,2,1,0:T(8,128)(2,1)S(1)}, bf16[2,1,512,512]{3,2,1,0:T(8,128)(2,1)}, u32[]{:S(2)}) %copy-start.2) | copy-done | bytes 1048600
  3.7 0.0 copy-start.3
  3.7 1.0 %copy-done.3 = bf16[512,512]{1,0:T(8,128)(2,1)S(1)} copy-done((bf16[512,512]{1,0:T(8,128)(2,1)S(1)}, bf16[512,512]{1,0:T(8,128)(2,1)}, u32[]{:S(2)}) %copy-start.3) | copy-done | bytes 524312
  4.7 0.0 copy-start.4
  4.7 0.9 %copy-done.4 = bf16[512,128]{1,0:T(8,128)(2,1)S(1)} copy-done((bf16[512,128]{1,0:T(8,128)(2,1)S(1)}, bf16[512,128]{1,0:T(8,128)(2,1)}, u32[]{:S(2)}) %copy-start.4) | copy-done | bytes 131096
  5.6 0.0 copy-start.5
  5.6 0.9 %copy-done.5 = bf16[128,512]{1,0:T(8,128)(2,1)S(1)} copy-done((bf16[128,512]{1,0:T(8,128)(2,1)S(1)}, bf16[128,512]{1,0:T(8,128)(2,1)}, u32[]{:S(2)}) %copy-start.5) | copy-done | bytes 131096
  6.5 0.0 copy-start.6
  6.5 0.7 copy-done.6
  7.2 0.0 copy-start.7
  7.2 0.7 copy-done.7
  7.9 74.2 %shard_map.82 = f32[16,512]{1,0:T(8,128)S(1)} custom-call(bf16[16,512]{1,0:T(8,128)(2,1)S(1)} %copy-done.6, bf16[512,512]{1,0:T(8,128)(2,1)S(1)} %copy-done.3, bf16[512,128]{1,0:T(8,128)(2,1)S(1)} %copy-done.4, bf16[128,512]{1,0:T(8,128)(2,1)S(1)} %copy-done.5, bf16[2,1,512,512]{3,2,1,0:T(8,128)(2,1)S(1)} %copy-done, bf16[2,1,512,512]{3,2,1,0:T(8,128)(2,1)S(1)} %copy-done.1, ...), custom_call_target="tpu_custom_call" | custom-call | tf_op jit(solution)/shard_map/pallas_call | solution.py:246
  82.1 0.6 copy.10
Async XLA Ops:
  0.0 1.2 %copy-start = (bf16[2,1,512,512]{3,2,1,0:T(8,128)(2,1)S(1)}, bf16[2,1,512,512]{3,2,1,0:T(8,128)(2,1)}, u32[]{:S(2)}) copy-start(bf16[2,1,512,512]{3,2,1,0:T(8,128)(2,1)} %up_hbm.1) | copy-start | bytes 3145732
  1.2 1.2 %copy-start.1 = (bf16[2,1,512,512]{3,2,1,0:T(8,128)(2,1)S(1)}, bf16[2,1,512,512]{3,2,1,0:T(8,128)(2,1)}, u32[]{:S(2)}) copy-start(bf16[2,1,512,512]{3,2,1,0:T(8,128)(2,1)} %cross_hbm.1) | copy-start | bytes 3145732
  2.5 1.2 %copy-start.2 = (bf16[2,1,512,512]{3,2,1,0:T(8,128)(2,1)S(1)}, bf16[2,1,512,512]{3,2,1,0:T(8,128)(2,1)}, u32[]{:S(2)}) copy-start(bf16[2,1,512,512]{3,2,1,0:T(8,128)(2,1)} %down_hbm.1) | copy-start | bytes 3145732
  3.7 1.0 %copy-start.3 = (bf16[512,512]{1,0:T(8,128)(2,1)S(1)}, bf16[512,512]{1,0:T(8,128)(2,1)}, u32[]{:S(2)}) copy-start(bf16[512,512]{1,0:T(8,128)(2,1)} %diag_hbm.1) | copy-start | bytes 1572868
  4.7 0.9 %copy-start.4 = (bf16[512,128]{1,0:T(8,128)(2,1)S(1)}, bf16[512,128]{1,0:T(8,128)(2,1)}, u32[]{:S(2)}) copy-start(bf16[512,128]{1,0:T(8,128)(2,1)} %in_hbm.1) | copy-start | bytes 393220
  5.6 0.9 %copy-start.5 = (bf16[128,512]{1,0:T(8,128)(2,1)S(1)}, bf16[128,512]{1,0:T(8,128)(2,1)}, u32[]{:S(2)}) copy-start(bf16[128,512]{1,0:T(8,128)(2,1)} %out_hbm.1) | copy-start | bytes 393220
  6.5 0.7 copy-start.6
  7.2 0.7 copy-start.7

commit v2 on v1

--- a/solution.py
+++ b/solution.py
@@ -246,7 +246,7 @@
     return pl.pallas_call(
         functools.partial(kernel, row_len, levels),
         out_shape=jax.ShapeDtypeStruct((rows, leaf), F32),
-        in_specs=[pl.BlockSpec(memory_space=pl.ANY)] * 8,
+        in_specs=[pl.BlockSpec(memory_space=pltpu.HBM)] * 8,
         out_specs=pl.BlockSpec(memory_space=pltpu.VMEM),
         scratch_shapes=[pltpu.VMEM(each.shape, each.dtype) for each in operands]
         + [
@@ -263,7 +263,7 @@
             pltpu.SemaphoreType.DMA((4,)),
         ],
         compiler_params=pltpu.CompilerParams(
-            collective_id=0, has_side_effects=True, vmem_limit_bytes=48 * 2**20
+            collective_id=0, has_side_effects=True, vmem_limit_bytes=32 * 2**20
         ),
     )(*operands, node_rank)
 

time: 83.1 us -> 83.1 us (level)
  no operation moved by 1% of the time
where the time goes in v2:
time: 83.1 us; the launch traced here: 82.7 us
  Pallas kernels  74.2 us (89%)
  local copies, waits for them, and re-layouts  8.51 us (10%)
    pallas_call x1, Pallas kernels, on_device(): pl.pallas_call(functools.partial(kernel, row_len, levels), out_shape=jax....  74.2 us
    unnamed x17, local copies, waits for them, and re-layouts  8.51 us

profile of v2, /device:TPU:2, one launch (start us, length us, event | category | flops | bytes accessed | tf_op | source)
XLA Modules:
  0.0 82.7 jit_solution(6813503926885036128)
XLA Ops:
  0.0 0.0 copy-start
  0.0 1.2 %copy-done = bf16[2,1,512,512]{3,2,1,0:T(8,128)(2,1)S(1)} copy-done((bf16[2,1,512,512]{3,2,1,0:T(8,128)(2,1)S(1)}, bf16[2,1,512,512]{3,2,1,0:T(8,128)(2,1)}, u32[]{:S(2)}) %copy-start) | copy-done | bytes 1048600
  1.2 0.0 copy-start.1
  1.2 1.2 %copy-done.1 = bf16[2,1,512,512]{3,2,1,0:T(8,128)(2,1)S(1)} copy-done((bf16[2,1,512,512]{3,2,1,0:T(8,128)(2,1)S(1)}, bf16[2,1,512,512]{3,2,1,0:T(8,128)(2,1)}, u32[]{:S(2)}) %copy-start.1) | copy-done | bytes 1048600
  2.5 0.0 copy-start.2
  2.5 1.2 %copy-done.2 = bf16[2,1,512,512]{3,2,1,0:T(8,128)(2,1)S(1)} copy-done((bf16[2,1,512,512]{3,2,1,0:T(8,128)(2,1)S(1)}, bf16[2,1,512,512]{3,2,1,0:T(8,128)(2,1)}, u32[]{:S(2)}) %copy-start.2) | copy-done | bytes 1048600
  3.7 0.0 copy-start.3
  3.7 1.0 %copy-done.3 = bf16[512,512]{1,0:T(8,128)(2,1)S(1)} copy-done((bf16[512,512]{1,0:T(8,128)(2,1)S(1)}, bf16[512,512]{1,0:T(8,128)(2,1)}, u32[]{:S(2)}) %copy-start.3) | copy-done | bytes 524312
  4.7 0.0 copy-start.4
  4.7 0.9 %copy-done.4 = bf16[512,128]{1,0:T(8,128)(2,1)S(1)} copy-done((bf16[512,128]{1,0:T(8,128)(2,1)S(1)}, bf16[512,128]{1,0:T(8,128)(2,1)}, u32[]{:S(2)}) %copy-start.4) | copy-done | bytes 131096
  5.6 0.0 copy-start.5
  5.6 0.9 %copy-done.5 = bf16[128,512]{1,0:T(8,128)(2,1)S(1)} copy-done((bf16[128,512]{1,0:T(8,128)(2,1)S(1)}, bf16[128,512]{1,0:T(8,128)(2,1)}, u32[]{:S(2)}) %copy-start.5) | copy-done | bytes 131096
  6.5 0.0 copy-start.6
  6.5 0.7 copy-done.6
  7.2 0.0 copy-start.7
  7.2 0.7 copy-done.7
  7.9 74.2 %shard_map.82 = f32[16,512]{1,0:T(8,128)S(1)} custom-call(bf16[16,512]{1,0:T(8,128)(2,1)S(1)} %copy-done.6, bf16[512,512]{1,0:T(8,128)(2,1)S(1)} %copy-done.3, bf16[512,128]{1,0:T(8,128)(2,1)S(1)} %copy-done.4, bf16[128,512]{1,0:T(8,128)(2,1)S(1)} %copy-done.5, bf16[2,1,512,512]{3,2,1,0:T(8,128)(2,1)S(1)} %copy-done, bf16[2,1,512,512]{3,2,1,0:T(8,128)(2,1)S(1)} %copy-done.1, ...), custom_call_target="tpu_custom_call" | custom-call | tf_op jit(solution)/shard_map/pallas_call | solution.py:246
  82.1 0.6 copy.10
Async XLA Ops:
  0.0 1.2 %copy-start = (bf16[2,1,512,512]{3,2,1,0:T(8,128)(2,1)S(1)}, bf16[2,1,512,512]{3,2,1,0:T(8,128)(2,1)}, u32[]{:S(2)}) copy-start(bf16[2,1,512,512]{3,2,1,0:T(8,128)(2,1)} %up_hbm.1) | copy-start | bytes 3145732
  1.2 1.2 %copy-start.1 = (bf16[2,1,512,512]{3,2,1,0:T(8,128)(2,1)S(1)}, bf16[2,1,512,512]{3,2,1,0:T(8,128)(2,1)}, u32[]{:S(2)}) copy-start(bf16[2,1,512,512]{3,2,1,0:T(8,128)(2,1)} %cross_hbm.1) | copy-start | bytes 3145732
  2.5 1.2 %copy-start.2 = (bf16[2,1,512,512]{3,2,1,0:T(8,128)(2,1)S(1)}, bf16[2,1,512,512]{3,2,1,0:T(8,128)(2,1)}, u32[]{:S(2)}) copy-start(bf16[2,1,512,512]{3,2,1,0:T(8,128)(2,1)} %down_hbm.1) | copy-start | bytes 3145732
  3.7 1.0 %copy-start.3 = (bf16[512,512]{1,0:T(8,128)(2,1)S(1)}, bf16[512,512]{1,0:T(8,128)(2,1)}, u32[]{:S(2)}) copy-start(bf16[512,512]{1,0:T(8,128)(2,1)} %diag_hbm.1) | copy-start | bytes 1572868
  4.7 0.9 %copy-start.4 = (bf16[512,128]{1,0:T(8,128)(2,1)S(1)}, bf16[512,128]{1,0:T(8,128)(2,1)}, u32[]{:S(2)}) copy-start(bf16[512,128]{1,0:T(8,128)(2,1)} %in_hbm.1) | copy-start | bytes 393220
  5.6 0.9 %copy-start.5 = (bf16[128,512]{1,0:T(8,128)(2,1)S(1)}, bf16[128,512]{1,0:T(8,128)(2,1)}, u32[]{:S(2)}) copy-start(bf16[128,512]{1,0:T(8,128)(2,1)} %out_hbm.1) | copy-start | bytes 393220
  6.5 0.7 copy-start.6
  7.2 0.7 copy-start.7

commit v3 on v1

--- a/solution.py
+++ b/solution.py
@@ -263,7 +263,7 @@
             pltpu.SemaphoreType.DMA((4,)),
         ],
         compiler_params=pltpu.CompilerParams(
-            collective_id=0, has_side_effects=True, vmem_limit_bytes=48 * 2**20
+            collective_id=0, has_side_effects=True, vmem_limit_bytes=60 * 2**20
         ),
     )(*operands, node_rank)
 

time: 83.1 us -> 75.8 us (0.912)
  local copies, waits for them, and re-layouts: 8.51 us -> 1.38 us
    unnamed x17 -> x1, local copies, waits for them, and re-layouts: 8.51 us -> 1.38 us
where the time goes in v3:
time: 75.8 us; the launch traced here: 75.6 us
  Pallas kernels  74.2 us (98%)
  local copies, waits for them, and re-layouts  1.38 us (2%)
    pallas_call x1, Pallas kernels, on_device(): pl.pallas_call(functools.partial(kernel, row_len, levels), out_shape=jax....  74.2 us

profile of v3, /device:TPU:2, one launch (start us, length us, event | category | flops | bytes accessed | tf_op | source)
XLA Modules:
  0.0 75.6 jit_solution(8131259587541537279)
XLA Ops:
  0.0 74.2 %shard_map.82 = f32[16,512]{1,0:T(8,128)} custom-call(bf16[16,512]{1,0:T(8,128)(2,1)} %rhs_hbm.1, bf16[512,512]{1,0:T(8,128)(2,1)} %diag_hbm.1, bf16[512,128]{1,0:T(8,128)(2,1)} %in_hbm.1, bf16[128,512]{1,0:T(8,128)(2,1)} %out_hbm.1, bf16[2,1,512,512]{3,2,1,0:T(8,128)(2,1)} %up_hbm.1, bf16[2,1,512,512]{3,2,1,0:T(8,128)(2,1)} %cross_hbm.1, ...), custom_call_target="tpu_custom_call" | custom-call | tf_op jit(solution)/shard_map/pallas_call | solution.py:246
  74.2 1.4 %copy.10 = f32[16,512]{1,0:T(8,128)} copy(f32[16,512]{1,0:T(8,128)} %shard_map.82) | data formatting | bytes 65536

commit v4 on v3

v4 whole, which is shorter than its diff:
```python
import functools

import jax
import jax.numpy as jnp
from jax import lax
from jax.experimental import pallas as pl
from jax.experimental.pallas import tpu as pltpu
from jax.sharding import PartitionSpec as P

MESH = pl.DeviceIdType.MESH
F32 = jnp.float32
BF16 = jnp.bfloat16
N_Z, N_CORE, N_X, N_Y = 16, 2, 4, 4


def kernel(
    rhs_hbm,
    diag_hbm,
    in_hbm,
    out_hbm,
    up_hbm,
    cross_hbm,
    down_hbm,
    rank_hbm,
    product,
    rhs,
    diag,
    leaf_in,
    leaf_out,
    up,
    cross,
    down,
    rank,
    leaf_coef,
    coef,
    child,
    cross_sum,
    path_coef,
    outgoing,
    map_a,
    map_b,
    map_c,
    map_d,
    leaf_map2,
    leaf_map1,
    cross_a,
    cross_b,
    leaf_cross2,
    leaf_cross1,
    above,
    leaf_above,
    parts7,
    parts8,
    load_sem,
    send_sem,
    recv_sem,
):
    rows, width = coef.shape
    leaf_width = leaf_coef.shape[1]
    tx, ty = lax.axis_index("tx"), lax.axis_index("ty")
    z, core = tx // N_CORE, tx % N_CORE
    x, y = ty // N_Y, ty % N_Y

    def at(z, core, x, y):
        return (z * N_CORE + core, x * N_Y + y)

    both = jnp.logical_and
    on_line = ty == 0
    on_top = both(on_line, core == 0)
    is_p1 = y % 2 == 1
    is_p2 = y == 2
    is_p3 = both(y == 0, x % 2 == 1)
    is_p4 = both(y == 0, x == 2)
    is_gate = both(on_line, core == 1)
    is_p6 = both(on_top, z % 2 == 1)
    is_p7 = both(on_top, z % 4 == 2)
    is_p8 = both(on_top, z % 8 == 4)
    is_p9 = both(on_top, z == 8)
    is_even = y % 2 == 0

    loads = [
        pltpu.make_async_copy(source, target, load_sem.at[n])
        for n, (source, target) in enumerate(
            (
                (rhs_hbm, rhs),
                (in_hbm, leaf_in),
                (rank_hbm, rank),
                (up_hbm, up),
                (cross_hbm, cross),
                (down_hbm, down),
                (diag_hbm, diag),
                (out_hbm, leaf_out),
            )
        )
    ]
    load_rhs, load_in, load_rank, load_up, load_cross, load_down, load_diag, load_out = loads
    for load in loads:
        load.start()

    x_odd = x // 2 * 2 + 1
    z_odd, z_seven, z_eight = z // 2 * 2 + 1, z // 4 * 4 + 2, z // 8 * 8 + 4
    z_far = (z + N_Z // 2) % N_Z
    z_far_half = z_far // 8 * 8
    leaf_peer = at(z, core, x, y + 1)
    left_leaf = at(z, core, x, y - 1)
    column = [at(z, core, x, k) for k in range(N_Y)]
    left_column = [at(z, core, x - 1, k) for k in range(N_Y)]
    my_p3 = at(z, core, x_odd, 0)
    p3s = [at(z, core, 1, 0), at(z, core, 3, 0)]
    p4 = at(z, core, 2, 0)
    gate = at(z, 1, 0, 0)
    p3s_of_gate = [at(z, c, k, 0) for c in range(N_CORE) for k in (1, 3)]
    p4s_of_gate = [at(z, c, 2, 0) for c in range(N_CORE)]
    p6, p7, p8 = at(z_odd, 0, 0, 0), at(z_seven, 0, 0, 0), at(z_eight, 0, 0, 0)
    gates_of_p6 = [at(z_odd - 1, 1, 0, 0), at(z_odd, 1, 0, 0)]
    gates_of_p7 = [at(z_seven - 2 + k, 1, 0, 0) for k in range(4)]
    p6s_of_p7 = [at(z_seven - 1, 0, 0, 0), at(z_seven + 1, 0, 0, 0)]
    p7s_of_p8 = [at(z_eight - 2, 0, 0, 0), at(z_eight + 2, 0, 0, 0)]
    far_same, far_other = at(z_far, 0, 0, 0), at(z_far_half + 8 - z_far % 8, 0, 0, 0)
    p9 = at(N_Z // 2, 0, 0, 0)
    p7s = [at(k, 0, 0, 0) for k in (2, 6, 10, 14)]

    barrier = pltpu.get_barrier_semaphore()

    def greet(condition, devices):
        @pl.when(condition)
        def _():
            for device in devices:
                pl.semaphore_signal(barrier, inc=1, device_id=device, device_id_type=MESH)

    greet(is_p1, [left_leaf, column[2], my_p3])
    greet(is_p2, [column[1], column[3], my_p3])
    greet(y == 0, [column[1], column[2]])
    greet(both(y == 0, x % 2 == 0), [my_p3])
    greet(is_p3, [at(z, core, x - 1, 2), p4, gate])
    greet(is_p4, p3s)
    greet(is_gate, [*p4s_of_gate, p6, p7])
    greet(is_p6, gates_of_p6)
    greet(is_p7, [*p6s_of_p7, *gates_of_p7, p8, far_same, far_other, p9])
    greet(is_p8, p7s_of_p8)
    sizes = (
        (is_even, 1),
        (y == 1, 2),
        (y == 3, 1),
        (is_p2, 3),
        (both(is_p2, x % 2 == 0), 1),
        (is_p3, 8),
        (is_p4, 3),
        (is_gate, 6),
        (is_p6, 3),
        (is_p7, 7),
        (is_p8, 2),
        (is_p9, 4),
    )
    greeted = sum(condition.astype(jnp.int32) * size for condition, size in sizes)

    def remote(source, target, send, recv, device):
        return pltpu.make_async_remote_copy(
            src_ref=source,
            dst_ref=target,
            send_sem=send_sem.at[send],
            recv_sem=recv_sem.at[recv],
            device_id=device,
            device_id_type=MESH,
        )

    left_part, right_part = pl.ds(0, width), pl.ds(width, width)
    narrow = pl.ds(0, leaf_width)

    leaf_up = remote(leaf_coef, child.at[:, narrow], 0, 0, leaf_peer)
    side = jnp.where(
        is_p1,
        y // 2,
        jnp.where(is_p2, x % 2, jnp.where(is_p3, x // 2, jnp.where(is_p4, core, jnp.where(is_gate, z % 2, jnp.where(is_p6, z // 2 % 2, z // 4 % 2))))),
    )
    steps = ((is_p1, column[2]), (is_p2, my_p3), (is_p3, p4), (is_p4, gate), (is_gate, p6), (is_p6, p7), (is_p7, p8))
    parent = tuple(sum(condition.astype(jnp.int32) * device[k] for condition, device in steps) for k in range(2))
    up_left = remote(coef, child.at[:, left_part], 1, 0, parent)
    up_right = remote(coef, child.at[:, right_part], 1, 1, parent)
    send_cross1 = [remote(cross_sum.at[0, :, narrow], leaf_cross1, 2, 2, left_leaf)]
    send_down1 = [remote(down.at[0, 0, :, narrow], leaf_map1, 3, 3, left_leaf)]
    sides2 = ((0, 0), (1, 0), (3, 1))
    send_cross2 = [remote(cross_sum.at[s], leaf_cross2, 2 + n, 4, column[k]) for n, (k, s) in enumerate(sides2)]
    send_down2 = [remote(down.at[s, 0], leaf_map2, 5 + n, 5, column[k]) for n, (k, s) in enumerate(sides2)]
    send_cross4 = [remote(cross_sum.at[s], cross_a, 2 + s, 11, p3s[s]) for s in range(2)]
    send_down4 = [remote(down.at[s, 0], map_d, 5 + s, 10, p3s[s]) for s in range(2)]
    send_cross6 = [remote(cross_sum.at[s], cross_b, 2 + s, 12, gates_of_p6[s]) for s in range(2)]
    send_up6 = [remote(up.at[s, 0], map_a, 4 + s, 7, gates_of_p6[s]) for s in range(2)]
    send_down6 = [remote(down.at[s, 0], map_c, 6 + s, 9, gates_of_p6[s]) for s in range(2)]
    send_cross7 = [remote(cross_sum.at[k // 2], cross_a, 2 + k, 11, gates_of_p7[k]) for k in range(4)]
    send_up7 = [remote(up.at[k // 2, 0], map_b, 6 + k, 8, gates_of_p7[k]) for k in range(4)]
    send_down7 = [remote(down.at[k // 2, 0], map_d, 10 + k, 10, gates_of_p7[k]) for k in range(4)]
    send_cross8 = [remote(cross_sum.at[s], cross_a, 2 + s, 11, p7s_of_p8[s]) for s in range(2)]
    send_up8 = [remote(up.at[s, 0], map_a, 4 + s, 7, p7s_of_p8[s]) for s in range(2)]
    send_down8 = [remote(down.at[s, 0], map_c, 6 + s, 9, p7s_of_p8[s]) for s in range(2)]
    send_cross9 = [remote(cross.at[1 - k // 2, 0], map_b, 2 + k, 8, p7s[k]) for k in range(4)]
    send_part7 = [remote(path_coef, parts7.at[k], 2, 14 + k, p7) for k in range(4)]
    send_part8 = [
        [remote(path_coef, parts8.at[k], 14, 18 + k, far_same), remote(path_coef, parts8.at[k], 15, 18 + k, far_other)]
        for k in range(2)
    ]
    send_above7 = [remote(outgoing.at[0], above, 16 + k, 13, gates_of_p7[k]) for k in (0, 3, 1, 2)]
    send_above4 = [remote(outgoing.at[k // 2], above, 3 + k, 13, p3s_of_gate[k]) for k in range(4)]
    send_above2_left = [remote(outgoing.at[0], leaf_above, 2 + k, 6, left_column[k]) for k in (2, 1, 3, 0)]
    send_above2_right = [remote(outgoing.at[1], leaf_above, 5 + k, 6, column[k]) for k in (2, 1, 3)]

    def start(copies):
        for copy in copies:
            copy.start()

    def dot(a, b):
        return jnp.dot(a, b, preferred_element_type=F32)

    load_rhs.wait()
    load_in.wait()
    load_rank.wait()
    leaf_rank, node_rank = rank[0, 0], rank[0, 1]
    leaf_keep = lax.broadcasted_iota(jnp.int32, (rows, leaf_width), 1) < leaf_rank
    node_keep = lax.broadcasted_iota(jnp.int32, (rows, width), 1) < node_rank
    leaf_coef[...] = jnp.where(leaf_keep, dot(rhs[...], leaf_in[...]), 0.0).astype(BF16)

    pl.semaphore_wait(barrier, greeted)

    def mask_up():
        keep = lax.broadcasted_iota(jnp.int32, (width, width), 1) < node_rank
        for s in range(2):
            up[s, 0] = jnp.where(keep, up[s, 0], jnp.zeros((width, width), BF16))

    def mask_down():
        keep = lax.broadcasted_iota(jnp.int32, (width, width), 0) < node_rank
        for s in range(2):
            down[s, 0] = jnp.where(keep, down[s, 0], jnp.zeros((width, width), BF16))

    def send_up(summed):
        coef[...] = jnp.where(node_keep, summed, 0.0).astype(BF16)

        @pl.when(side == 0)
        def _():
            up_left.start()

        @pl.when(side == 1)
        def _():
            up_right.start()

    def cross_terms():
        cross_sum[0] = dot(child[:, right_part], cross[0, 0])
        cross_sum[1] = dot(child[:, left_part], cross[1, 0])

    @pl.when(is_even)
    def _():
        leaf_up.start()

    @pl.when(is_p1)
    def _():
        load_up.wait()
        summed = dot(leaf_coef[...], up[1, 0, narrow, :])
        leaf_up.wait_recv()
        send_up(summed + dot(child[:, narrow], up[0, 0, narrow, :]))
        load_cross.wait()
        cross_sum[0, :, narrow] = dot(leaf_coef[...], cross[0, 0, narrow, narrow])
        leaf_cross1[...] = dot(child[:, narrow], cross[1, 0, narrow, narrow])
        start(send_cross1)
        load_down.wait()
        mask_down()
        start(send_down1)
        leaf_map1[...] = down[1, 0, :, narrow]

    def lift():
        up_left.wait_recv()
        summed = dot(child[:, left_part], up[0, 0])
        up_right.wait_recv()
        send_up(summed + dot(child[:, right_part], up[1, 0]))

    @pl.when(is_p2)
    def _():
        load_up.wait()
        lift()
        load_cross.wait()
        cross_terms()
        start(send_cross2)
        leaf_cross2[...] = cross_sum[1]
        load_down.wait()
        mask_down()
        start(send_down2)
        leaf_map2[...] = down[1, 0]

    @pl.when(is_p3)
    def _():
        load_up.wait()
        lift()
        load_cross.wait()
        cross_terms()
        load_down.wait()
        mask_down()

    @pl.when(is_p4)
    def _():
        load_up.wait()
        lift()
        load_cross.wait()
        cross_terms()
        start(send_cross4)
        load_down.wait()
        mask_down()
        start(send_down4)

    @pl.when(is_gate)
    def _():
        load_up.wait()
        load_cross.wait()
        load_down.wait()
        mask_down()
        lift()
        send_up6[0].wait_recv()
        path_coef[...] = dot(coef[...], map_a[...]).astype(BF16)
        send_up7[0].wait_recv()
        path_coef[...] = dot(path_coef[...], map_b[...]).astype(BF16)
        for k in range(4):

            @pl.when(z % 4 == k)
            def _():
                send_part7[k].start()

        cross_terms()

    @pl.when(is_p6)
    def _():
        load_up.wait()
        mask_up()
        start(send_up6)
        load_cross.wait()
        load_down.wait()
        mask_down()
        for copy in send_up6:
            copy.wait_send()
        start(send_down6)
        lift()
        cross_terms()
        start(send_cross6)

    @pl.when(is_p7)
    def _():
        load_up.wait()
        mask_up()
        start(send_up7)
        load_cross.wait()
        load_down.wait()
        mask_down()
        for copy in send_up7:
            copy.wait_send()
        start(send_down7)
        summed = jnp.zeros((rows, width), F32)
        for k in range(4):
            send_part7[k].wait_recv()
            summed += parts7[k].astype(F32)
        send_up(summed)
        send_up8[0].wait_recv()
        part = dot(coef[...], map_a[...]).astype(BF16)
        send_cross9[0].wait_recv()
        path_coef[...] = dot(part, map_b[...]).astype(BF16)
        for k in range(2):

            @pl.when(z // 4 % 2 == k)
            def _():
                start(send_part8[k])

        up_left.wait_recv()
        up_right.wait_recv()
        cross_terms()
        start(send_cross7)

    @pl.when(is_p8)
    def _():
        load_up.wait()
        mask_up()
        start(send_up8)
        load_cross.wait()
        load_down.wait()
        mask_down()
        for copy in send_up8:
            copy.wait_send()
        start(send_down8)
        up_left.wait_recv()
        up_right.wait_recv()
        cross_terms()
        start(send_cross8)

    @pl.when(both(on_top, z % 8 == 0))
    def _():
        load_up.wait()
        load_cross.wait()
        load_down.wait()

    @pl.when(is_p9)
    def _():
        start(send_cross9)

    load_diag.wait()
    product[...] = dot(rhs[...], diag[...])
    load_out.wait()

    @pl.when(is_p7)
    def _():
        send_down8[0].wait_recv()
        send_cross8[0].wait_recv()
        for k in range(2):
            send_part8[k][0].wait_recv()
        crossed = (parts8[0].astype(F32) + parts8[1].astype(F32)).astype(BF16)
        outgoing[0] = (cross_a[...] + dot(crossed, map_c[...])).astype(BF16)
        start(send_above7)

    @pl.when(is_gate)
    def _():
        send_down7[0].wait_recv()
        send_cross7[0].wait_recv()
        send_down6[0].wait_recv()
        send_cross6[0].wait_recv()
        send_above7[0].wait_recv()
        six = (cross_a[...] + dot(above[...], map_d[...])).astype(BF16)
        five = (cross_b[...] + dot(six, map_c[...])).astype(BF16)
        for s in range(2):
            outgoing[s] = (cross_sum[s] + dot(five, down[s, 0])).astype(BF16)
            start(send_above4[2 * s : 2 * s + 2])

    @pl.when(is_p3)
    def _():
        send_down4[0].wait_recv()
        send_cross4[0].wait_recv()
        send_above4[0].wait_recv()
        three = (cross_a[...] + dot(above[...], map_d[...])).astype(BF16)
        outgoing[0] = (cross_sum[0] + dot(three, down[0, 0])).astype(BF16)
        start(send_above2_left)
        outgoing[1] = (cross_sum[1] + dot(three, down[1, 0])).astype(BF16)
        start(send_above2_right)
        leaf_above[...] = outgoing[1]

    @pl.when(is_even)
    def _():
        send_cross1[0].wait_recv()
        send_down1[0].wait_recv()

    @pl.when(jnp.logical_not(is_p2))
    def _():
        send_cross2[0].wait_recv()
        send_down2[0].wait_recv()

    @pl.when(jnp.logical_not(is_p3))
    def _():
        send_above2_left[0].wait_recv()

    one = (leaf_cross2[...] + dot(leaf_above[...], leaf_map2[...])).astype(BF16)
    zero = (leaf_cross1[...] + dot(one, leaf_map1[...])).astype(BF16)
    zero = jnp.where(leaf_keep, zero, jnp.zeros_like(zero))
    product[...] += dot(zero, leaf_out[...])

    def sent(condition, copies):
        @pl.when(condition)
        def _():
            for copy in copies:
                copy.wait_send()

    sent(is_even, [leaf_up])
    sent(is_p1, [up_left, *send_cross1, *send_down1])
    sent(is_p2, [up_left, *send_cross2, *send_down2])
    sent(is_p3, [up_left, *send_above2_left, *send_above2_right])
    sent(is_p4, [up_left, *send_cross4, *send_down4])
    sent(is_gate, [up_left, send_part7[0], *send_above4])
    sent(is_p6, [up_left, *send_down6, *send_cross6])
    sent(is_p7, [up_left, *send_down7, *send_part8[0], *send_cross7, *send_above7])
    sent(is_p8, [*send_down8, *send_cross8])
    sent(is_p9, send_cross9)


def on_device(rhs, diag_blocks, leaf_in, leaf_out, up_maps, cross_maps, down_maps, node_rank):
    rows, leaf = rhs.shape
    width, leaf_width = up_maps.shape[-1], leaf_in.shape[1]
    operands = (rhs, diag_blocks, leaf_in, leaf_out, up_maps, cross_maps, down_maps)

    def vector(*lead, kind=BF16, columns=width):
        return pltpu.VMEM((*lead, rows, columns), kind)

    full_map = pltpu.VMEM((width, width), BF16)
    return pl.pallas_call(
        kernel,
        out_shape=jax.ShapeDtypeStruct((rows, leaf), F32),
        in_specs=[pl.BlockSpec(memory_space=pl.ANY)] * 8,
        out_specs=pl.BlockSpec(memory_space=pltpu.VMEM),
        scratch_shapes=[pltpu.VMEM(each.shape, each.dtype) for each in operands]
        + [
            pltpu.SMEM(node_rank.shape, node_rank.dtype),
            vector(columns=leaf_width),
            vector(),
            vector(columns=2 * width),
            vector(2, kind=F32),
            vector(),
            vector(2),
            full_map,
            full_map,
            full_map,
            full_map,
            full_map,
            pltpu.VMEM((width, leaf_width), BF16),
            vector(kind=F32),
            vector(kind=F32),
            vector(kind=F32),
            vector(kind=F32, columns=leaf_width),
            vector(),
            vector(),
            vector(4),
            vector(2),
            pltpu.SemaphoreType.DMA((8,)),
            pltpu.SemaphoreType.DMA((20,)),
            pltpu.SemaphoreType.DMA((20,)),
        ],
        compiler_params=pltpu.CompilerParams(
            collective_id=0, has_side_effects=True, vmem_limit_bytes=60 * 2**20
        ),
    )(*operands, node_rank)


def solution(mesh):
    assert mesh.shape["tx"] == N_Z * N_CORE and mesh.shape["ty"] == N_X * N_Y
    in_specs = (
        P(None, ("tx", "ty")),
        P(("tx", "ty"), None),
        P(("tx", "ty"), None),
        P(("tx", "ty"), None),
        P(None, ("tx", "ty"), None, None),
        P(None, ("tx", "ty"), None, None),
        P(None, ("tx", "ty"), None, None),
        P(("tx", "ty"), None),
    )
    return jax.shard_map(
        on_device, mesh=mesh, in_specs=in_specs, out_specs=P(None, ("tx", "ty")), check_vma=False
    )
```

time: 75.8 us -> 63.6 us (0.84)
  the two profiles are of different devices: /device:TPU:2 before, /device:TPU:1 now
where the time goes in v4:
time: 63.6 us; the launch traced here: 63.4 us
  Pallas kernels  62 us (97%)
  local copies, waits for them, and re-layouts  1.38 us (2%)
    pallas_call x1, Pallas kernels, on_device(): pl.pallas_call(kernel, out_shape=jax.ShapeDtypeStruct((rows, leaf), F32),...  62 us
    unnamed x1, local copies, waits for them, and re-layouts  1.38 us

profile of v4, /device:TPU:1, one launch (start us, length us, event | category | flops | bytes accessed | tf_op | source)
XLA Modules:
  0.0 63.4 jit_solution(17127857568925492678)
XLA Ops:
  0.0 62.0 %shard_map.82 = f32[16,512]{1,0:T(8,128)} custom-call(bf16[16,512]{1,0:T(8,128)(2,1)} %rhs_hbm.1, bf16[512,512]{1,0:T(8,128)(2,1)} %diag_hbm.1, bf16[512,128]{1,0:T(8,128)(2,1)} %in_hbm.1, bf16[128,512]{1,0:T(8,128)(2,1)} %out_hbm.1, bf16[2,1,512,512]{3,2,1,0:T(8,128)(2,1)} %up_hbm.1, bf16[2,1,512,512]{3,2,1,0:T(8,128)(2,1)} %cross_hbm.1, ...), custom_call_target="tpu_custom_call" | custom-call | tf_op jit(solution)/shard_map/pallas_call | solution.py:483
  62.0 1.4 %copy.10 = f32[16,512]{1,0:T(8,128)} copy(f32[16,512]{1,0:T(8,128)} %shard_map.82) | data formatting | bytes 65536

commit v5 on v4

--- a/solution.py
+++ b/solution.py
@@ -54,6 +54,7 @@
     load_sem,
     send_sem,
     recv_sem,
+    go_sem,
 ):
     rows, width = coef.shape
     leaf_width = leaf_coef.shape[1]
@@ -94,7 +95,7 @@
         )
     ]
     load_rhs, load_in, load_rank, load_up, load_cross, load_down, load_diag, load_out = loads
-    for load in loads:
+    for load in loads[:3]:
         load.start()
 
     x_odd = x // 2 * 2 + 1
@@ -128,31 +129,47 @@
             for device in devices:
                 pl.semaphore_signal(barrier, inc=1, device_id=device, device_id_type=MESH)
 
-    greet(is_p1, [left_leaf, column[2], my_p3])
-    greet(is_p2, [column[1], column[3], my_p3])
-    greet(y == 0, [column[1], column[2]])
-    greet(both(y == 0, x % 2 == 0), [my_p3])
-    greet(is_p3, [at(z, core, x - 1, 2), p4, gate])
-    greet(is_p4, p3s)
-    greet(is_gate, [*p4s_of_gate, p6, p7])
-    greet(is_p6, gates_of_p6)
-    greet(is_p7, [*p6s_of_p7, *gates_of_p7, p8, far_same, far_other, p9])
-    greet(is_p8, p7s_of_p8)
+    def collector(z, core, x):
+        return at(z, core, x, 1)
+
+    x_even = x % 2 == 0
+    next_p3 = collector(z, core, x_odd)
+    greet(is_p1, [left_leaf])
+    greet(y == 1, [column[3]])
+    greet(both(y == 1, x_even), [next_p3])
+    greet(y == 3, [next_p3])
+    greet(is_p2, [column[1], column[3], next_p3])
+    greet(y == 0, [column[1], column[3]])
+    greet(both(y == 0, x_even), [next_p3])
+    greet(is_p3, [at(z, core, x - 1, 3), collector(z, core, 2), collector(z, 1, 0)])
+    greet(is_p4, [collector(z, core, 1), collector(z, core, 3)])
+    greet(is_gate, [collector(z, c, 2) for c in range(N_CORE)] + [collector(z_odd, 0, 0), collector(z_seven, 0, 0)])
+    greet(both(is_gate, z % 4 == 0), [collector(z + 1, 1, 0)])
+    greet(is_p6, [collector(z_odd - 1, 1, 0), collector(z_odd, 1, 0)])
+    greet(
+        is_p7,
+        [collector(z_seven - 1, 0, 0), collector(z_seven + 1, 0, 0)]
+        + [collector(z_seven - 2 + k, 1, 0) for k in range(4)]
+        + [collector(z_eight, 0, 0), collector(N_Z // 2, 0, 0)],
+    )
+    greet(is_p8, [collector(z_eight - 2, 0, 0), collector(z_eight + 2, 0, 0)])
     sizes = (
         (is_even, 1),
+        (y == 3, 3),
+        (both(y == 3, x_even), 1),
         (y == 1, 2),
-        (y == 3, 1),
-        (is_p2, 3),
-        (both(is_p2, x % 2 == 0), 1),
-        (is_p3, 8),
-        (is_p4, 3),
-        (is_gate, 6),
-        (is_p6, 3),
-        (is_p7, 7),
-        (is_p8, 2),
-        (is_p9, 4),
+        (both(y == 1, x % 2 == 1), 7),
+        (both(y == 1, x == 2), 3),
+        (both(ty == 1, core == 1), 6),
+        (both(both(ty == 1, core == 1), z % 4 == 1), 1),
+        (both(both(ty == 1, core == 0), z % 2 == 1), 3),
+        (both(both(ty == 1, core == 0), z % 4 == 2), 5),
+        (both(both(ty == 1, core == 0), z % 8 == 4), 2),
+        (both(both(ty == 1, core == 0), z == 8), 4),
     )
     greeted = sum(condition.astype(jnp.int32) * size for condition, size in sizes)
+    for load in loads[3:]:
+        load.start()
 
     def remote(source, target, send, recv, device):
         return pltpu.make_async_remote_copy(
@@ -190,6 +207,8 @@
     send_cross7 = [remote(cross_sum.at[k // 2], cross_a, 2 + k, 11, gates_of_p7[k]) for k in range(4)]
     send_up7 = [remote(up.at[k // 2, 0], map_b, 6 + k, 8, gates_of_p7[k]) for k in range(4)]
     send_down7 = [remote(down.at[k // 2, 0], map_d, 10 + k, 10, gates_of_p7[k]) for k in range(4)]
+    pass_up7 = remote(map_b, map_b, 7, 8, at(z - 1, 1, 0, 0))
+    pass_down7 = remote(map_d, map_d, 8, 10, at(z - 1, 1, 0, 0))
     send_cross8 = [remote(cross_sum.at[s], cross_a, 2 + s, 11, p7s_of_p8[s]) for s in range(2)]
     send_up8 = [remote(up.at[s, 0], map_a, 4 + s, 7, p7s_of_p8[s]) for s in range(2)]
     send_down8 = [remote(down.at[s, 0], map_c, 6 + s, 9, p7s_of_p8[s]) for s in range(2)]
@@ -221,6 +240,10 @@
 
     pl.semaphore_wait(barrier, greeted)
 
+    @pl.when(is_p1)
+    def _():
+        pl.semaphore_signal(go_sem, inc=1, device_id=left_leaf, device_id_type=MESH)
+
     def mask_up():
         keep = lax.broadcasted_iota(jnp.int32, (width, width), 1) < node_rank
         for s in range(2):
@@ -231,8 +254,10 @@
         for s in range(2):
             down[s, 0] = jnp.where(keep, down[s, 0], jnp.zeros((width, width), BF16))
 
-    def send_up(summed):
+    def send_up(summed, waits=False):
         coef[...] = jnp.where(node_keep, summed, 0.0).astype(BF16)
+        if waits:
+            pl.semaphore_wait(go_sem, 1)
 
         @pl.when(side == 0)
         def _():
@@ -250,6 +275,10 @@
     def _():
         leaf_up.start()
 
+    @pl.when(on_line)
+    def _():
+        pl.semaphore_wait(go_sem, 1)
+
     @pl.when(is_p1)
     def _():
         load_up.wait()
@@ -265,11 +294,11 @@
         start(send_down1)
         leaf_map1[...] = down[1, 0, :, narrow]
 
-    def lift():
+    def lift(waits=True):
         up_left.wait_recv()
         summed = dot(child[:, left_part], up[0, 0])
         up_right.wait_recv()
-        send_up(summed + dot(child[:, right_part], up[1, 0]))
+        send_up(summed + dot(child[:, right_part], up[1, 0]), waits)
 
     @pl.when(is_p2)
     def _():
@@ -310,10 +339,15 @@
         load_cross.wait()
         load_down.wait()
         mask_down()
-        lift()
+        send_up7[0].wait_recv()
+
+        @pl.when(z % 4 == 1)
+        def _():
+            pass_up7.start()
+
+        lift(waits=False)
         send_up6[0].wait_recv()
         path_coef[...] = dot(coef[...], map_a[...]).astype(BF16)
-        send_up7[0].wait_recv()
         path_coef[...] = dot(path_coef[...], map_b[...]).astype(BF16)
         for k in range(4):
 
@@ -322,6 +356,11 @@
                 send_part7[k].start()
 
         cross_terms()
+        send_down7[0].wait_recv()
+
+        @pl.when(z % 4 == 1)
+        def _():
+            pass_down7.start()
 
     @pl.when(is_p6)
     def _():
@@ -334,7 +373,7 @@
         for copy in send_up6:
             copy.wait_send()
         start(send_down6)
-        lift()
+        lift(waits=False)
         cross_terms()
         start(send_cross6)
 
@@ -342,13 +381,13 @@
     def _():
         load_up.wait()
         mask_up()
-        start(send_up7)
-        load_cross.wait()
-        load_down.wait()
-        mask_down()
-        for copy in send_up7:
+        start(send_up7[1:])
+        load_cross.wait()
+        load_down.wait()
+        mask_down()
+        for copy in send_up7[1:]:
             copy.wait_send()
-        start(send_down7)
+        start(send_down7[1:])
         summed = jnp.zeros((rows, width), F32)
         for k in range(4):
             send_part7[k].wait_recv()
@@ -411,7 +450,6 @@
 
     @pl.when(is_gate)
     def _():
-        send_down7[0].wait_recv()
         send_cross7[0].wait_recv()
         send_down6[0].wait_recv()
         send_cross6[0].wait_recv()
@@ -465,8 +503,9 @@
     sent(is_p3, [up_left, *send_above2_left, *send_above2_right])
     sent(is_p4, [up_left, *send_cross4, *send_down4])
     sent(is_gate, [up_left, send_part7[0], *send_above4])
+    sent(both(is_gate, z % 4 == 1), [pass_up7, pass_down7])
     sent(is_p6, [up_left, *send_down6, *send_cross6])
-    sent(is_p7, [up_left, *send_down7, *send_part8[0], *send_cross7, *send_above7])
+    sent(is_p7, [up_left, *send_down7[1:], *send_part8[0], *send_cross7, *send_above7])
     sent(is_p8, [*send_down8, *send_cross8])
     sent(is_p9, send_cross9)
 
@@ -511,6 +550,7 @@
             pltpu.SemaphoreType.DMA((8,)),
             pltpu.SemaphoreType.DMA((20,)),
             pltpu.SemaphoreType.DMA((20,)),
+            pltpu.SemaphoreType.REGULAR,
         ],
         compiler_params=pltpu.CompilerParams(
             collective_id=0, has_side_effects=True, vmem_limit_bytes=60 * 2**20

time: 63.6 us -> 58.7 us (0.923)
  Pallas kernels: 62 us -> 57.1 us
    pallas_call x1, Pallas kernels: 62 us -> 57.1 us  [on_device(): pl.pallas_call(kernel, out_shape=jax.ShapeDtypeStruct((rows, leaf), F32),...]
where the time goes in v5:
time: 58.7 us; the launch traced here: 58.5 us
  Pallas kernels  57.1 us (97%)
  local copies, waits for them, and re-layouts  1.38 us (2%)
    pallas_call x1, Pallas kernels, on_device(): pl.pallas_call(kernel, out_shape=jax.ShapeDtypeStruct((rows, leaf), F32),...  57.1 us
    unnamed x1, local copies, waits for them, and re-layouts  1.38 us

profile of v5, /device:TPU:1, one launch (start us, length us, event | category | flops | bytes accessed | tf_op | source)
XLA Modules:
  0.0 58.5 jit_solution(9154744123769842124)
XLA Ops:
  0.0 57.1 %shard_map.82 = f32[16,512]{1,0:T(8,128)} custom-call(bf16[16,512]{1,0:T(8,128)(2,1)} %rhs_hbm.1, bf16[512,512]{1,0:T(8,128)(2,1)} %diag_hbm.1, bf16[512,128]{1,0:T(8,128)(2,1)} %in_hbm.1, bf16[128,512]{1,0:T(8,128)(2,1)} %out_hbm.1, bf16[2,1,512,512]{3,2,1,0:T(8,128)(2,1)} %up_hbm.1, bf16[2,1,512,512]{3,2,1,0:T(8,128)(2,1)} %cross_hbm.1, ...), custom_call_target="tpu_custom_call" | custom-call | tf_op jit(solution)/shard_map/pallas_call | solution.py:522
  57.1 1.4 %copy.10 = f32[16,512]{1,0:T(8,128)} copy(f32[16,512]{1,0:T(8,128)} %shard_map.82) | data formatting | bytes 65536

commit v6 on v5

--- a/solution.py
+++ b/solution.py
@@ -45,11 +45,12 @@
     leaf_map1,
     cross_a,
     cross_b,
+    cross_c,
     leaf_cross2,
     leaf_cross1,
     above,
     leaf_above,
-    parts7,
+    parts6,
     parts8,
     load_sem,
     send_sem,
@@ -78,6 +79,11 @@
     is_p8 = both(on_top, z % 8 == 4)
     is_p9 = both(on_top, z == 8)
     is_even = y % 2 == 0
+    is_first = both(is_gate, z < 4)
+    is_left_p8 = both(on_top, z == 4)
+    is_right_p8 = both(on_top, z == 12)
+    is_right_p7 = both(is_p7, z >= 8)
+    is_second_p7 = both(on_top, z == 6)
 
     loads = [
         pltpu.make_async_copy(source, target, load_sem.at[n])
@@ -100,8 +106,6 @@
 
     x_odd = x // 2 * 2 + 1
     z_odd, z_seven, z_eight = z // 2 * 2 + 1, z // 4 * 4 + 2, z // 8 * 8 + 4
-    z_far = (z + N_Z // 2) % N_Z
-    z_far_half = z_far // 8 * 8
     leaf_peer = at(z, core, x, y + 1)
     left_leaf = at(z, core, x, y - 1)
     column = [at(z, core, x, k) for k in range(N_Y)]
@@ -115,11 +119,10 @@
     p6, p7, p8 = at(z_odd, 0, 0, 0), at(z_seven, 0, 0, 0), at(z_eight, 0, 0, 0)
     gates_of_p6 = [at(z_odd - 1, 1, 0, 0), at(z_odd, 1, 0, 0)]
     gates_of_p7 = [at(z_seven - 2 + k, 1, 0, 0) for k in range(4)]
-    p6s_of_p7 = [at(z_seven - 1, 0, 0, 0), at(z_seven + 1, 0, 0, 0)]
     p7s_of_p8 = [at(z_eight - 2, 0, 0, 0), at(z_eight + 2, 0, 0, 0)]
-    far_same, far_other = at(z_far, 0, 0, 0), at(z_far_half + 8 - z_far % 8, 0, 0, 0)
-    p9 = at(N_Z // 2, 0, 0, 0)
-    p7s = [at(k, 0, 0, 0) for k in (2, 6, 10, 14)]
+    first_gates = [at(k, 1, 0, 0) for k in range(4)]
+    second_p7, left_p8 = at(6, 0, 0, 0), at(4, 0, 0, 0)
+    right_p7s = [at(k, 0, 0, 0) for k in (10, 14)]
 
     barrier = pltpu.get_barrier_semaphore()
 
@@ -145,14 +148,12 @@
     greet(is_p4, [collector(z, core, 1), collector(z, core, 3)])
     greet(is_gate, [collector(z, c, 2) for c in range(N_CORE)] + [collector(z_odd, 0, 0), collector(z_seven, 0, 0)])
     greet(both(is_gate, z % 4 == 0), [collector(z + 1, 1, 0)])
+    greet(is_first, [collector(4, 0, 0), collector(8, 0, 0)])
     greet(is_p6, [collector(z_odd - 1, 1, 0), collector(z_odd, 1, 0)])
-    greet(
-        is_p7,
-        [collector(z_seven - 1, 0, 0), collector(z_seven + 1, 0, 0)]
-        + [collector(z_seven - 2 + k, 1, 0) for k in range(4)]
-        + [collector(z_eight, 0, 0), collector(N_Z // 2, 0, 0)],
-    )
+    greet(is_p7, [collector(z_seven - 2 + k, 1, 0) for k in range(4)])
+    greet(both(is_p7, z > 2), [collector(z_eight, 0, 0), collector(8, 0, 0)])
     greet(is_p8, [collector(z_eight - 2, 0, 0), collector(z_eight + 2, 0, 0)])
+    greet(is_left_p8, [collector(8, 0, 0)])
     sizes = (
         (is_even, 1),
         (y == 3, 3),
@@ -162,10 +163,11 @@
         (both(y == 1, x == 2), 3),
         (both(ty == 1, core == 1), 6),
         (both(both(ty == 1, core == 1), z % 4 == 1), 1),
-        (both(both(ty == 1, core == 0), z % 2 == 1), 3),
+        (both(both(ty == 1, core == 0), z % 2 == 1), 2),
         (both(both(ty == 1, core == 0), z % 4 == 2), 5),
-        (both(both(ty == 1, core == 0), z % 8 == 4), 2),
-        (both(both(ty == 1, core == 0), z == 8), 4),
+        (both(both(ty == 1, core == 0), z == 4), 5),
+        (both(both(ty == 1, core == 0), z == 12), 2),
+        (both(both(ty == 1, core == 0), z == 8), 8),
     )
     greeted = sum(condition.astype(jnp.int32) * size for condition, size in sizes)
     for load in loads[3:]:
@@ -188,9 +190,9 @@
     side = jnp.where(
         is_p1,
         y // 2,
-        jnp.where(is_p2, x % 2, jnp.where(is_p3, x // 2, jnp.where(is_p4, core, jnp.where(is_gate, z % 2, jnp.where(is_p6, z // 2 % 2, z // 4 % 2))))),
+        jnp.where(is_p2, x % 2, jnp.where(is_p3, x // 2, jnp.where(is_p4, core, jnp.where(is_gate, z % 2, z // 4 % 2)))),
     )
-    steps = ((is_p1, column[2]), (is_p2, my_p3), (is_p3, p4), (is_p4, gate), (is_gate, p6), (is_p6, p7), (is_p7, p8))
+    steps = ((is_p1, column[2]), (is_p2, my_p3), (is_p3, p4), (is_p4, gate), (is_gate, p6), (is_p7, p8))
     parent = tuple(sum(condition.astype(jnp.int32) * device[k] for condition, device in steps) for k in range(2))
     up_left = remote(coef, child.at[:, left_part], 1, 0, parent)
     up_right = remote(coef, child.at[:, right_part], 1, 1, parent)
@@ -205,19 +207,22 @@
     send_up6 = [remote(up.at[s, 0], map_a, 4 + s, 7, gates_of_p6[s]) for s in range(2)]
     send_down6 = [remote(down.at[s, 0], map_c, 6 + s, 9, gates_of_p6[s]) for s in range(2)]
     send_cross7 = [remote(cross_sum.at[k // 2], cross_a, 2 + k, 11, gates_of_p7[k]) for k in range(4)]
-    send_up7 = [remote(up.at[k // 2, 0], map_b, 6 + k, 8, gates_of_p7[k]) for k in range(4)]
     send_down7 = [remote(down.at[k // 2, 0], map_d, 10 + k, 10, gates_of_p7[k]) for k in range(4)]
-    pass_up7 = remote(map_b, map_b, 7, 8, at(z - 1, 1, 0, 0))
-    pass_down7 = remote(map_d, map_d, 8, 10, at(z - 1, 1, 0, 0))
+    pass_down7 = remote(map_d, map_d, 7, 10, at(z - 1, 1, 0, 0))
     send_cross8 = [remote(cross_sum.at[s], cross_a, 2 + s, 11, p7s_of_p8[s]) for s in range(2)]
+    send_cross8_first = [remote(cross_sum.at[0], cross_c, 10 + k, 20, first_gates[k]) for k in range(4)]
     send_up8 = [remote(up.at[s, 0], map_a, 4 + s, 7, p7s_of_p8[s]) for s in range(2)]
     send_down8 = [remote(down.at[s, 0], map_c, 6 + s, 9, p7s_of_p8[s]) for s in range(2)]
-    send_cross9 = [remote(cross.at[1 - k // 2, 0], map_b, 2 + k, 8, p7s[k]) for k in range(4)]
-    send_part7 = [remote(path_coef, parts7.at[k], 2, 14 + k, p7) for k in range(4)]
+    send_down8_first = [remote(down.at[0, 0], map_b, 14 + k, 8, first_gates[k]) for k in range(4)]
+    pass_down8 = remote(map_b, map_b, 8, 8, at(z - 1, 1, 0, 0))
+    send_cross9 = [remote(cross.at[0, 0], map_b, 2 + k, 8, right_p7s[k]) for k in range(2)]
+    send_cross9 += [remote(cross.at[1, 0], map_b, 4, 8, left_p8)]
+    send_part6 = [remote(path_coef, parts6.at[k], 2, 14 + k, p7) for k in range(4)]
     send_part8 = [
-        [remote(path_coef, parts8.at[k], 14, 18 + k, far_same), remote(path_coef, parts8.at[k], 15, 18 + k, far_other)]
+        [remote(path_coef, parts8.at[k], 6 + n, 18 + k, device) for n, device in enumerate((*first_gates, second_p7))]
         for k in range(2)
     ]
+    send_part8_right = [remote(path_coef, parts8.at[0], 8 + k, 18, right_p7s[k]) for k in range(2)]
     send_above7 = [remote(outgoing.at[0], above, 16 + k, 13, gates_of_p7[k]) for k in (0, 3, 1, 2)]
     send_above4 = [remote(outgoing.at[k // 2], above, 3 + k, 13, p3s_of_gate[k]) for k in range(4)]
     send_above2_left = [remote(outgoing.at[0], leaf_above, 2 + k, 6, left_column[k]) for k in (2, 1, 3, 0)]
@@ -339,28 +344,27 @@
         load_cross.wait()
         load_down.wait()
         mask_down()
-        send_up7[0].wait_recv()
 
         @pl.when(z % 4 == 1)
         def _():
-            pass_up7.start()
+            send_down7[0].wait_recv()
+            pass_down7.start()
 
         lift(waits=False)
         send_up6[0].wait_recv()
         path_coef[...] = dot(coef[...], map_a[...]).astype(BF16)
-        path_coef[...] = dot(path_coef[...], map_b[...]).astype(BF16)
         for k in range(4):
 
             @pl.when(z % 4 == k)
             def _():
-                send_part7[k].start()
+                send_part6[k].start()
 
         cross_terms()
-        send_down7[0].wait_recv()
-
-        @pl.when(z % 4 == 1)
-        def _():
-            pass_down7.start()
+
+        @pl.when(z == 1)
+        def _():
+            send_down8_first[0].wait_recv()
+            pass_down8.start()
 
     @pl.when(is_p6)
     def _():
@@ -373,56 +377,78 @@
         for copy in send_up6:
             copy.wait_send()
         start(send_down6)
-        lift(waits=False)
-        cross_terms()
-        start(send_cross6)
-
-    @pl.when(is_p7)
-    def _():
-        load_up.wait()
-        mask_up()
-        start(send_up7[1:])
-        load_cross.wait()
-        load_down.wait()
-        mask_down()
-        for copy in send_up7[1:]:
-            copy.wait_send()
-        start(send_down7[1:])
-        summed = jnp.zeros((rows, width), F32)
-        for k in range(4):
-            send_part7[k].wait_recv()
-            summed += parts7[k].astype(F32)
-        send_up(summed)
-        send_up8[0].wait_recv()
-        part = dot(coef[...], map_a[...]).astype(BF16)
-        send_cross9[0].wait_recv()
-        path_coef[...] = dot(part, map_b[...]).astype(BF16)
-        for k in range(2):
-
-            @pl.when(z // 4 % 2 == k)
-            def _():
-                start(send_part8[k])
-
         up_left.wait_recv()
         up_right.wait_recv()
         cross_terms()
+        start(send_cross6)
+
+    @pl.when(is_p7)
+    def _():
+        load_down.wait()
+        mask_down()
+        start(send_down7[1:])
+        load_up.wait()
+        load_cross.wait()
+        for s in range(2):
+            for k in (2 * s, 2 * s + 1):
+                send_part6[k].wait_recv()
+            six = parts6[2 * s].astype(F32) + parts6[2 * s + 1].astype(F32)
+            child[:, (left_part, right_part)[s]] = six.astype(BF16)
+        send_up(dot(child[:, left_part], up[0, 0]) + dot(child[:, right_part], up[1, 0]))
+
+        @pl.when(is_right_p7)
+        def _():
+            send_up8[0].wait_recv()
+            eight = dot(coef[...], map_a[...]).astype(BF16)
+            send_cross9[0].wait_recv()
+            path_coef[...] = dot(eight, map_b[...]).astype(BF16)
+            for k in range(2):
+
+                @pl.when(z // 4 % 2 == k)
+                def _():
+                    start(send_part8[k])
+
+        cross_terms()
         start(send_cross7)
 
     @pl.when(is_p8)
     def _():
         load_up.wait()
-        mask_up()
-        start(send_up8)
-        load_cross.wait()
-        load_down.wait()
-        mask_down()
-        for copy in send_up8:
-            copy.wait_send()
-        start(send_down8)
-        up_left.wait_recv()
-        up_right.wait_recv()
-        cross_terms()
-        start(send_cross8)
+        load_cross.wait()
+        load_down.wait()
+        mask_down()
+        send_cross1[0].wait_recv()
+        send_down1[0].wait_recv()
+
+        @pl.when(is_right_p8)
+        def _():
+            mask_up()
+            start(send_up8)
+            for copy in send_up8:
+                copy.wait_send()
+            start(send_down8)
+            up_left.wait_recv()
+            up_right.wait_recv()
+            cross_terms()
+            start(send_cross8)
+
+        @pl.when(is_left_p8)
+        def _():
+            send_down8[1].start()
+            for copy in send_down8_first[1:]:
+                copy.start()
+                copy.wait_send()
+            up_left.wait_recv()
+            eight = dot(child[:, left_part], up[0, 0])
+            up_right.wait_recv()
+            cross_terms()
+            start(send_cross8_first)
+            send_cross8[1].start()
+            eight += dot(child[:, right_part], up[1, 0])
+            coef[...] = jnp.where(node_keep, eight, 0.0).astype(BF16)
+            send_cross9[2].wait_recv()
+            path_coef[...] = dot(coef[...], map_b[...]).astype(BF16)
+            start(send_part8_right)
 
     @pl.when(both(on_top, z % 8 == 0))
     def _():
@@ -438,22 +464,47 @@
     product[...] = dot(rhs[...], diag[...])
     load_out.wait()
 
-    @pl.when(is_p7)
+    @pl.when(both(is_p7, z > 2))
     def _():
         send_down8[0].wait_recv()
         send_cross8[0].wait_recv()
-        for k in range(2):
-            send_part8[k][0].wait_recv()
-        crossed = (parts8[0].astype(F32) + parts8[1].astype(F32)).astype(BF16)
-        outgoing[0] = (cross_a[...] + dot(crossed, map_c[...])).astype(BF16)
+        send_part8[0][0].wait_recv()
+
+        @pl.when(is_second_p7)
+        def _():
+            send_part8[1][0].wait_recv()
+            crossed = parts8[0].astype(F32) + parts8[1].astype(F32)
+            parts8[0] = crossed.astype(BF16)
+
+        outgoing[0] = (cross_a[...] + dot(parts8[0], map_c[...])).astype(BF16)
         start(send_above7)
 
     @pl.when(is_gate)
     def _():
+        @pl.when(z % 4 != 1)
+        def _():
+            send_down7[0].wait_recv()
+
         send_cross7[0].wait_recv()
         send_down6[0].wait_recv()
         send_cross6[0].wait_recv()
-        send_above7[0].wait_recv()
+
+        @pl.when(both(z < 4, z != 1))
+        def _():
+            send_down8_first[0].wait_recv()
+
+        @pl.when(z < 4)
+        def _():
+            send_cross8_first[0].wait_recv()
+            for k in range(2):
+                send_part8[k][0].wait_recv()
+            crossed = (parts8[0].astype(F32) + parts8[1].astype(F32)).astype(BF16)
+            above[...] = (cross_c[...] + dot(crossed, map_b[...])).astype(BF16)
+
+        @pl.when(z >= 4)
+        def _():
+            send_above7[0].wait_recv()
+
         six = (cross_a[...] + dot(above[...], map_d[...])).astype(BF16)
         five = (cross_b[...] + dot(six, map_c[...])).astype(BF16)
         for s in range(2):
@@ -472,7 +523,7 @@
         start(send_above2_right)
         leaf_above[...] = outgoing[1]
 
-    @pl.when(is_even)
+    @pl.when(both(is_even, jnp.logical_not(is_p8)))
     def _():
         send_cross1[0].wait_recv()
         send_down1[0].wait_recv()
@@ -502,11 +553,15 @@
     sent(is_p2, [up_left, *send_cross2, *send_down2])
     sent(is_p3, [up_left, *send_above2_left, *send_above2_right])
     sent(is_p4, [up_left, *send_cross4, *send_down4])
-    sent(is_gate, [up_left, send_part7[0], *send_above4])
-    sent(both(is_gate, z % 4 == 1), [pass_up7, pass_down7])
-    sent(is_p6, [up_left, *send_down6, *send_cross6])
-    sent(is_p7, [up_left, *send_down7[1:], *send_part8[0], *send_cross7, *send_above7])
-    sent(is_p8, [*send_down8, *send_cross8])
+    sent(is_gate, [up_left, send_part6[0], *send_above4])
+    sent(both(is_gate, z % 4 == 1), [pass_down7])
+    sent(both(is_gate, z == 1), [pass_down8])
+    sent(is_p6, [*send_down6, *send_cross6])
+    sent(is_p7, [up_left, *send_down7[1:], *send_cross7])
+    sent(both(is_p7, z > 2), send_above7)
+    sent(is_right_p7, send_part8[0])
+    sent(is_right_p8, [*send_down8, *send_cross8])
+    sent(is_left_p8, [send_down8[1], *send_cross8_first, send_cross8[1], *send_part8_right])
     sent(is_p9, send_cross9)
 
 
@@ -542,6 +597,7 @@
             vector(kind=F32),
             vector(kind=F32),
             vector(kind=F32),
+            vector(kind=F32),
             vector(kind=F32, columns=leaf_width),
             vector(),
             vector(),
@@ -549,7 +605,7 @@
             vector(2),
             pltpu.SemaphoreType.DMA((8,)),
             pltpu.SemaphoreType.DMA((20,)),
-            pltpu.SemaphoreType.DMA((20,)),
+            pltpu.SemaphoreType.DMA((21,)),
             pltpu.SemaphoreType.REGULAR,
         ],
         compiler_params=pltpu.CompilerParams(

time: 58.7 us -> 49.6 us (0.84)
  Pallas kernels: 57.1 us -> 48 us
    pallas_call x1, Pallas kernels: 57.1 us -> 48 us  [on_device(): pl.pallas_call(kernel, out_shape=jax.ShapeDtypeStruct((rows, leaf), F32),...]
where the time goes in v6:
time: 49.6 us; the launch traced here: 49.4 us
  Pallas kernels  48 us (97%)
  local copies, waits for them, and re-layouts  1.38 us (3%)
    pallas_call x1, Pallas kernels, on_device(): pl.pallas_call(kernel, out_shape=jax.ShapeDtypeStruct((rows, leaf), F32),...  48 us
    unnamed x1, local copies, waits for them, and re-layouts  1.38 us

profile of v6, /device:TPU:1, one launch (start us, length us, event | category | flops | bytes accessed | tf_op | source)
XLA Modules:
  0.0 49.4 jit_solution(2757309741170748173)
XLA Ops:
  0.0 48.0 %shard_map.82 = f32[16,512]{1,0:T(8,128)} custom-call(bf16[16,512]{1,0:T(8,128)(2,1)} %rhs_hbm.1, bf16[512,512]{1,0:T(8,128)(2,1)} %diag_hbm.1, bf16[512,128]{1,0:T(8,128)(2,1)} %in_hbm.1, bf16[128,512]{1,0:T(8,128)(2,1)} %out_hbm.1, bf16[2,1,512,512]{3,2,1,0:T(8,128)(2,1)} %up_hbm.1, bf16[2,1,512,512]{3,2,1,0:T(8,128)(2,1)} %cross_hbm.1, ...), custom_call_target="tpu_custom_call" | custom-call | tf_op jit(solution)/shard_map/pallas_call | solution.py:577
  48.0 1.4 %copy.10 = f32[16,512]{1,0:T(8,128)} copy(f32[16,512]{1,0:T(8,128)} %shard_map.82) | data formatting | bytes 65536

commit v7 on v6

--- a/solution.py
+++ b/solution.py
@@ -50,7 +50,7 @@
     leaf_cross1,
     above,
     leaf_above,
-    parts6,
+    parts,
     parts8,
     load_sem,
     send_sem,
@@ -82,7 +82,7 @@
     is_first = both(is_gate, z < 4)
     is_left_p8 = both(on_top, z == 4)
     is_right_p8 = both(on_top, z == 12)
-    is_right_p7 = both(is_p7, z >= 8)
+    is_third_p7 = both(on_top, z == 10)
     is_second_p7 = both(on_top, z == 6)
 
     loads = [
@@ -146,28 +146,29 @@
     greet(both(y == 0, x_even), [next_p3])
     greet(is_p3, [at(z, core, x - 1, 3), collector(z, core, 2), collector(z, 1, 0)])
     greet(is_p4, [collector(z, core, 1), collector(z, core, 3)])
-    greet(is_gate, [collector(z, c, 2) for c in range(N_CORE)] + [collector(z_odd, 0, 0), collector(z_seven, 0, 0)])
+    greet(is_gate, [collector(z, 0, 1), collector(z, 0, 3), collector(z, 1, 2)] + [collector(z_odd, 0, 0), collector(z_seven, 0, 0)])
     greet(both(is_gate, z % 4 == 0), [collector(z + 1, 1, 0)])
     greet(is_first, [collector(4, 0, 0), collector(8, 0, 0)])
     greet(is_p6, [collector(z_odd - 1, 1, 0), collector(z_odd, 1, 0)])
     greet(is_p7, [collector(z_seven - 2 + k, 1, 0) for k in range(4)])
     greet(both(is_p7, z > 2), [collector(z_eight, 0, 0), collector(8, 0, 0)])
     greet(is_p8, [collector(z_eight - 2, 0, 0), collector(z_eight + 2, 0, 0)])
-    greet(is_left_p8, [collector(8, 0, 0)])
+    greet(is_p8, [collector(8, 0, 0)])
     sizes = (
         (is_even, 1),
         (y == 3, 3),
         (both(y == 3, x_even), 1),
         (y == 1, 2),
         (both(y == 1, x % 2 == 1), 7),
-        (both(y == 1, x == 2), 3),
+        (both(both(y == 1, x % 2 == 1), core == 0), 1),
+        (both(y == 1, x == 2), 2 + core),
         (both(ty == 1, core == 1), 6),
         (both(both(ty == 1, core == 1), z % 4 == 1), 1),
         (both(both(ty == 1, core == 0), z % 2 == 1), 2),
         (both(both(ty == 1, core == 0), z % 4 == 2), 5),
         (both(both(ty == 1, core == 0), z == 4), 5),
         (both(both(ty == 1, core == 0), z == 12), 2),
-        (both(both(ty == 1, core == 0), z == 8), 8),
+        (both(both(ty == 1, core == 0), z == 8), 9),
     )
     greeted = sum(condition.astype(jnp.int32) * size for condition, size in sizes)
     for load in loads[3:]:
@@ -202,6 +203,8 @@
     send_cross2 = [remote(cross_sum.at[s], leaf_cross2, 2 + n, 4, column[k]) for n, (k, s) in enumerate(sides2)]
     send_down2 = [remote(down.at[s, 0], leaf_map2, 5 + n, 5, column[k]) for n, (k, s) in enumerate(sides2)]
     send_cross4 = [remote(cross_sum.at[s], cross_a, 2 + s, 11, p3s[s]) for s in range(2)]
+    send_up4 = [remote(up.at[s, 0], map_a, 7 + s, 7, p3s[s]) for s in range(2)]
+    send_part4 = [remote(path_coef, parts.at[k], 9, 14 + k, gate) for k in range(2)]
     send_down4 = [remote(down.at[s, 0], map_d, 5 + s, 10, p3s[s]) for s in range(2)]
     send_cross6 = [remote(cross_sum.at[s], cross_b, 2 + s, 12, gates_of_p6[s]) for s in range(2)]
     send_up6 = [remote(up.at[s, 0], map_a, 4 + s, 7, gates_of_p6[s]) for s in range(2)]
@@ -211,15 +214,17 @@
     pass_down7 = remote(map_d, map_d, 7, 10, at(z - 1, 1, 0, 0))
     send_cross8 = [remote(cross_sum.at[s], cross_a, 2 + s, 11, p7s_of_p8[s]) for s in range(2)]
     send_cross8_first = [remote(cross_sum.at[0], cross_c, 10 + k, 20, first_gates[k]) for k in range(4)]
-    send_up8 = [remote(up.at[s, 0], map_a, 4 + s, 7, p7s_of_p8[s]) for s in range(2)]
+    send_up8 = remote(up.at[0, 0], map_a, 4, 7, p7s_of_p8[0])
     send_down8 = [remote(down.at[s, 0], map_c, 6 + s, 9, p7s_of_p8[s]) for s in range(2)]
+    halves = [pl.ds(k * (width // 2), width // 2) for k in range(2)]
+    send_down8_half = [remote(down.at[0, 0, half], map_c.at[half], 6 + 5 * k, 9, p7s_of_p8[0]) for k, half in enumerate(halves)]
     send_down8_first = [remote(down.at[0, 0], map_b, 14 + k, 8, first_gates[k]) for k in range(4)]
     pass_down8 = remote(map_b, map_b, 8, 8, at(z - 1, 1, 0, 0))
-    send_cross9 = [remote(cross.at[0, 0], map_b, 2 + k, 8, right_p7s[k]) for k in range(2)]
+    send_cross9 = [remote(cross.at[0, 0], map_b, 2 + k, 8, at((10, 12)[k], 0, 0, 0)) for k in range(2)]
     send_cross9 += [remote(cross.at[1, 0], map_b, 4, 8, left_p8)]
-    send_part6 = [remote(path_coef, parts6.at[k], 2, 14 + k, p7) for k in range(4)]
+    send_part6 = [remote(path_coef, parts.at[k], 2, 14 + k, p7) for k in range(4)]
     send_part8 = [
-        [remote(path_coef, parts8.at[k], 6 + n, 18 + k, device) for n, device in enumerate((*first_gates, second_p7))]
+        [remote(path_coef, parts8.at[k], 12 + n, 18 + k, device) for n, device in enumerate((*first_gates, second_p7))]
         for k in range(2)
     ]
     send_part8_right = [remote(path_coef, parts8.at[0], 8 + k, 18, right_p7s[k]) for k in range(2)]
@@ -322,6 +327,17 @@
     def _():
         load_up.wait()
         lift()
+
+        @pl.when(core == 0)
+        def _():
+            send_up4[0].wait_recv()
+            path_coef[...] = dot(coef[...], map_a[...]).astype(BF16)
+            for k in range(2):
+
+                @pl.when(x // 2 == k)
+                def _():
+                    send_part4[k].start()
+
         load_cross.wait()
         cross_terms()
         load_down.wait()
@@ -330,7 +346,19 @@
     @pl.when(is_p4)
     def _():
         load_up.wait()
-        lift()
+        mask_up()
+        pl.semaphore_wait(go_sem, 1)
+
+        @pl.when(core == 0)
+        def _():
+            start(send_up4)
+            up_left.wait_recv()
+            up_right.wait_recv()
+
+        @pl.when(core == 1)
+        def _():
+            lift(waits=False)
+
         load_cross.wait()
         cross_terms()
         start(send_cross4)
@@ -350,7 +378,11 @@
             send_down7[0].wait_recv()
             pass_down7.start()
 
-        lift(waits=False)
+        for copy in send_part4:
+            copy.wait_recv()
+        child[:, left_part] = (parts[0].astype(F32) + parts[1].astype(F32)).astype(BF16)
+        up_right.wait_recv()
+        send_up(dot(child[:, left_part], up[0, 0]) + dot(child[:, right_part], up[1, 0]))
         send_up6[0].wait_recv()
         path_coef[...] = dot(coef[...], map_a[...]).astype(BF16)
         for k in range(4):
@@ -389,24 +421,24 @@
         start(send_down7[1:])
         load_up.wait()
         load_cross.wait()
+
+        @pl.when(is_third_p7)
+        def _():
+            send_up8.wait_recv()
+            send_cross9[0].wait_recv()
+            map_a[...] = dot(map_a[...], map_b[...]).astype(BF16)
+
         for s in range(2):
             for k in (2 * s, 2 * s + 1):
                 send_part6[k].wait_recv()
-            six = parts6[2 * s].astype(F32) + parts6[2 * s + 1].astype(F32)
+            six = parts[2 * s].astype(F32) + parts[2 * s + 1].astype(F32)
             child[:, (left_part, right_part)[s]] = six.astype(BF16)
         send_up(dot(child[:, left_part], up[0, 0]) + dot(child[:, right_part], up[1, 0]))
 
-        @pl.when(is_right_p7)
-        def _():
-            send_up8[0].wait_recv()
-            eight = dot(coef[...], map_a[...]).astype(BF16)
-            send_cross9[0].wait_recv()
-            path_coef[...] = dot(eight, map_b[...]).astype(BF16)
-            for k in range(2):
-
-                @pl.when(z // 4 % 2 == k)
-                def _():
-                    start(send_part8[k])
+        @pl.when(is_third_p7)
+        def _():
+            path_coef[...] = dot(coef[...], map_a[...]).astype(BF16)
+            start(send_part8[0])
 
         cross_terms()
         start(send_cross7)
@@ -417,27 +449,36 @@
         load_cross.wait()
         load_down.wait()
         mask_down()
+        @pl.when(is_right_p8)
+        def _():
+            send_down8[1].start()
+            mask_up()
+
         send_cross1[0].wait_recv()
-        send_down1[0].wait_recv()
 
         @pl.when(is_right_p8)
         def _():
-            mask_up()
-            start(send_up8)
-            for copy in send_up8:
-                copy.wait_send()
-            start(send_down8)
+            send_down1[0].wait_recv()
+            send_up8.start()
+            send_up8.wait_send()
+            send_down8_half[0].start()
+            send_cross9[1].wait_recv()
+            map_a[...] = dot(up[1, 0], map_b[...]).astype(BF16)
+            up_right.wait_recv()
+            path_coef[...] = dot(child[:, right_part], map_a[...]).astype(BF16)
+            start(send_part8[1])
+            send_down8_half[1].start()
             up_left.wait_recv()
-            up_right.wait_recv()
             cross_terms()
             start(send_cross8)
 
         @pl.when(is_left_p8)
         def _():
             send_down8[1].start()
-            for copy in send_down8_first[1:]:
-                copy.start()
-                copy.wait_send()
+            send_down8_first[1].start()
+            send_down1[0].wait_recv()
+            send_down8_first[1].wait_send()
+            start(send_down8_first[2:])
             up_left.wait_recv()
             eight = dot(child[:, left_part], up[0, 0])
             up_right.wait_recv()
@@ -485,41 +526,58 @@
         def _():
             send_down7[0].wait_recv()
 
+        @pl.when(z % 4 == 1)
+        def _():
+            pass_down7.wait_send()
+
+        send_down6[0].wait_recv()
+        map_d[...] = dot(map_d[...], map_c[...]).astype(BF16)
+
+        @pl.when(both(z < 4, z != 1))
+        def _():
+            send_down8_first[0].wait_recv()
+
+        @pl.when(z == 1)
+        def _():
+            pass_down8.wait_send()
+
+        @pl.when(z < 4)
+        def _():
+            map_b[...] = dot(map_b[...], map_d[...]).astype(BF16)
+
         send_cross7[0].wait_recv()
-        send_down6[0].wait_recv()
         send_cross6[0].wait_recv()
-
-        @pl.when(both(z < 4, z != 1))
-        def _():
-            send_down8_first[0].wait_recv()
+        cross_b[...] += dot(cross_a[...].astype(BF16), map_c[...])
 
         @pl.when(z < 4)
         def _():
             send_cross8_first[0].wait_recv()
+            cross_b[...] += dot(cross_c[...].astype(BF16), map_d[...])
             for k in range(2):
                 send_part8[k][0].wait_recv()
             crossed = (parts8[0].astype(F32) + parts8[1].astype(F32)).astype(BF16)
-            above[...] = (cross_c[...] + dot(crossed, map_b[...])).astype(BF16)
+            above[...] = (cross_b[...] + dot(crossed, map_b[...])).astype(BF16)
 
         @pl.when(z >= 4)
         def _():
             send_above7[0].wait_recv()
-
-        six = (cross_a[...] + dot(above[...], map_d[...])).astype(BF16)
-        five = (cross_b[...] + dot(six, map_c[...])).astype(BF16)
+            above[...] = (cross_b[...] + dot(above[...], map_d[...])).astype(BF16)
+
         for s in range(2):
-            outgoing[s] = (cross_sum[s] + dot(five, down[s, 0])).astype(BF16)
+            outgoing[s] = (cross_sum[s] + dot(above[...], down[s, 0])).astype(BF16)
             start(send_above4[2 * s : 2 * s + 2])
 
     @pl.when(is_p3)
     def _():
         send_down4[0].wait_recv()
         send_cross4[0].wait_recv()
+        for s in range(2):
+            cross_sum[s] += dot(cross_a[...].astype(BF16), down[s, 0])
+            down[s, 0] = dot(map_d[...], down[s, 0]).astype(BF16)
         send_above4[0].wait_recv()
-        three = (cross_a[...] + dot(above[...], map_d[...])).astype(BF16)
-        outgoing[0] = (cross_sum[0] + dot(three, down[0, 0])).astype(BF16)
+        outgoing[0] = (cross_sum[0] + dot(above[...], down[0, 0])).astype(BF16)
         start(send_above2_left)
-        outgoing[1] = (cross_sum[1] + dot(three, down[1, 0])).astype(BF16)
+        outgoing[1] = (cross_sum[1] + dot(above[...], down[1, 0])).astype(BF16)
         start(send_above2_right)
         leaf_above[...] = outgoing[1]
 
@@ -533,14 +591,18 @@
         send_cross2[0].wait_recv()
         send_down2[0].wait_recv()
 
+    zero = dot(leaf_cross2[...].astype(BF16), leaf_map1[...]) + leaf_cross1[...]
+    zero = jnp.where(leaf_keep, zero, 0.0).astype(BF16)
+    product[...] += dot(zero, leaf_out[...])
+    map_keep = lax.broadcasted_iota(jnp.int32, (width, leaf_width), 1) < leaf_rank
+    leaf_map1[...] = jnp.where(map_keep, dot(leaf_map2[...], leaf_map1[...]), 0.0).astype(BF16)
+    leaf_map2[...] = dot(leaf_map1[...], leaf_out[...]).astype(BF16)
+
     @pl.when(jnp.logical_not(is_p3))
     def _():
         send_above2_left[0].wait_recv()
 
-    one = (leaf_cross2[...] + dot(leaf_above[...], leaf_map2[...])).astype(BF16)
-    zero = (leaf_cross1[...] + dot(one, leaf_map1[...])).astype(BF16)
-    zero = jnp.where(leaf_keep, zero, jnp.zeros_like(zero))
-    product[...] += dot(zero, leaf_out[...])
+    product[...] += dot(leaf_above[...], leaf_map2[...])
 
     def sent(condition, copies):
         @pl.when(condition)
@@ -551,17 +613,18 @@
     sent(is_even, [leaf_up])
     sent(is_p1, [up_left, *send_cross1, *send_down1])
     sent(is_p2, [up_left, *send_cross2, *send_down2])
+    sent(both(is_p3, core == 0), [send_part4[0]])
     sent(is_p3, [up_left, *send_above2_left, *send_above2_right])
-    sent(is_p4, [up_left, *send_cross4, *send_down4])
+    sent(both(is_p4, core == 0), send_up4)
+    sent(both(is_p4, core == 1), [up_left])
+    sent(is_p4, [*send_cross4, *send_down4])
     sent(is_gate, [up_left, send_part6[0], *send_above4])
-    sent(both(is_gate, z % 4 == 1), [pass_down7])
-    sent(both(is_gate, z == 1), [pass_down8])
     sent(is_p6, [*send_down6, *send_cross6])
     sent(is_p7, [up_left, *send_down7[1:], *send_cross7])
     sent(both(is_p7, z > 2), send_above7)
-    sent(is_right_p7, send_part8[0])
-    sent(is_right_p8, [*send_down8, *send_cross8])
-    sent(is_left_p8, [send_down8[1], *send_cross8_first, send_cross8[1], *send_part8_right])
+    sent(is_third_p7, send_part8[0])
+    sent(is_right_p8, [send_down8[1], *send_down8_half, *send_part8[1], *send_cross8])
+    sent(is_left_p8, [send_down8[1], *send_down8_first[2:], *send_cross8_first, send_cross8[1], *send_part8_right])
     sent(is_p9, send_cross9)
 
 

time: 49.6 us -> 46.9 us (0.946)
  Pallas kernels: 48 us -> 45.4 us
    pallas_call x1, Pallas kernels: 48 us -> 45.4 us  [on_device(): pl.pallas_call(kernel, out_shape=jax.ShapeDtypeStruct((rows, leaf), F32),...]
where the time goes in v7:
time: 46.9 us; the launch traced here: 46.7 us
  Pallas kernels  45.4 us (97%)
  local copies, waits for them, and re-layouts  1.38 us (3%)
    pallas_call x1, Pallas kernels, on_device(): pl.pallas_call(kernel, out_shape=jax.ShapeDtypeStruct((rows, leaf), F32),...  45.4 us
    unnamed x1, local copies, waits for them, and re-layouts  1.38 us

profile of v7, /device:TPU:1, one launch (start us, length us, event | category | flops | bytes accessed | tf_op | source)
XLA Modules:
  0.0 46.7 jit_solution(12009450091295756322)
XLA Ops:
  0.0 45.4 %shard_map.82 = f32[16,512]{1,0:T(8,128)} custom-call(bf16[16,512]{1,0:T(8,128)(2,1)} %rhs_hbm.1, bf16[512,512]{1,0:T(8,128)(2,1)} %diag_hbm.1, bf16[512,128]{1,0:T(8,128)(2,1)} %in_hbm.1, bf16[128,512]{1,0:T(8,128)(2,1)} %out_hbm.1, bf16[2,1,512,512]{3,2,1,0:T(8,128)(2,1)} %up_hbm.1, bf16[2,1,512,512]{3,2,1,0:T(8,128)(2,1)} %cross_hbm.1, ...), custom_call_target="tpu_custom_call" | custom-call | tf_op jit(solution)/shard_map/pallas_call | solution.py:640
  45.4 1.4 %copy.10 = f32[16,512]{1,0:T(8,128)} copy(f32[16,512]{1,0:T(8,128)} %shard_map.82) | data formatting | bytes 65536

commit v8 on v7

--- a/solution.py
+++ b/solution.py
@@ -41,6 +41,16 @@
     map_b,
     map_c,
     map_d,
+    map_e,
+    map_f,
+    top_up,
+    top_cross,
+    top_child,
+    top_coef,
+    top_sum,
+    top_out,
+    far_out,
+    gate_up,
     leaf_map2,
     leaf_map1,
     cross_a,
@@ -50,12 +60,14 @@
     leaf_cross1,
     above,
     leaf_above,
-    parts,
+    parts4,
+    parts6,
     parts8,
     load_sem,
     send_sem,
     recv_sem,
     go_sem,
+    late_sem,
 ):
     rows, width = coef.shape
     leaf_width = leaf_coef.shape[1]
@@ -79,11 +91,13 @@
     is_p8 = both(on_top, z % 8 == 4)
     is_p9 = both(on_top, z == 8)
     is_even = y % 2 == 0
-    is_first = both(is_gate, z < 4)
+    is_hub = both(is_gate, z % 4 == 2)
+    is_late_hub = both(is_hub, z > 2)
+    is_far_hub = both(is_hub, z >= 8)
+    is_left_center = both(is_gate, z == 4)
+    is_right_center = both(is_gate, z == 12)
     is_left_p8 = both(on_top, z == 4)
     is_right_p8 = both(on_top, z == 12)
-    is_third_p7 = both(on_top, z == 10)
-    is_second_p7 = both(on_top, z == 6)
 
     loads = [
         pltpu.make_async_copy(source, target, load_sem.at[n])
@@ -119,10 +133,10 @@
     p6, p7, p8 = at(z_odd, 0, 0, 0), at(z_seven, 0, 0, 0), at(z_eight, 0, 0, 0)
     gates_of_p6 = [at(z_odd - 1, 1, 0, 0), at(z_odd, 1, 0, 0)]
     gates_of_p7 = [at(z_seven - 2 + k, 1, 0, 0) for k in range(4)]
-    p7s_of_p8 = [at(z_eight - 2, 0, 0, 0), at(z_eight + 2, 0, 0, 0)]
+    hub, center = at(z_seven, 1, 0, 0), at(z_eight, 1, 0, 0)
+    hubs_of_center = [at(z_eight - 2, 1, 0, 0), at(z_eight + 2, 1, 0, 0)]
     first_gates = [at(k, 1, 0, 0) for k in range(4)]
-    second_p7, left_p8 = at(6, 0, 0, 0), at(4, 0, 0, 0)
-    right_p7s = [at(k, 0, 0, 0) for k in (10, 14)]
+    second_hub, third_hub, fourth_hub = at(6, 1, 0, 0), at(10, 1, 0, 0), at(14, 1, 0, 0)
 
     barrier = pltpu.get_barrier_semaphore()
 
@@ -148,12 +162,21 @@
     greet(is_p4, [collector(z, core, 1), collector(z, core, 3)])
     greet(is_gate, [collector(z, 0, 1), collector(z, 0, 3), collector(z, 1, 2)] + [collector(z_odd, 0, 0), collector(z_seven, 0, 0)])
     greet(both(is_gate, z % 4 == 0), [collector(z + 1, 1, 0)])
-    greet(is_first, [collector(4, 0, 0), collector(8, 0, 0)])
+    greet(both(is_gate, z < 4), [collector(4, 0, 0), collector(8, 0, 0), collector(4, 1, 0)])
+    greet(both(both(is_gate, z >= 4), z % 4 != 2), [collector(z_seven, 1, 0)])
+    greet(is_hub, [collector(z_seven - 2 + k, 1, 0) for k in (0, 1, 3)])
+    greet(is_late_hub, [collector(z_eight, 0, 0), collector(z_eight, 1, 0)])
+    greet(both(is_late_hub, z < 12), [collector(8, 0, 0)])
+    greet(both(is_late_hub, z > 12), [collector(4, 1, 0), collector(8, 1, 0)])
+    greet(is_p9, [collector(8, 1, 0)])
+    greet(
+        both(is_gate, z % 8 == 4),
+        [collector(z_eight - 2, 1, 0), collector(z_eight + 2, 1, 0), collector(z, 0, 0)],
+    )
+    greet(is_left_center, [collector(8, 0, 0)])
     greet(is_p6, [collector(z_odd - 1, 1, 0), collector(z_odd, 1, 0)])
-    greet(is_p7, [collector(z_seven - 2 + k, 1, 0) for k in range(4)])
-    greet(both(is_p7, z > 2), [collector(z_eight, 0, 0), collector(8, 0, 0)])
-    greet(is_p8, [collector(z_eight - 2, 0, 0), collector(z_eight + 2, 0, 0)])
-    greet(is_p8, [collector(8, 0, 0)])
+    greet(is_p7, [collector(z, 1, 0)])
+    greet(is_right_p8, [collector(z, 1, 0)])
     sizes = (
         (is_even, 1),
         (y == 3, 3),
@@ -162,13 +185,19 @@
         (both(y == 1, x % 2 == 1), 7),
         (both(both(y == 1, x % 2 == 1), core == 0), 1),
         (both(y == 1, x == 2), 2 + core),
-        (both(ty == 1, core == 1), 6),
+        (both(ty == 1, core == 1), 5),
+        (both(both(ty == 1, core == 1), z % 4 != 2), 1),
         (both(both(ty == 1, core == 1), z % 4 == 1), 1),
+        (both(both(ty == 1, core == 1), z % 4 == 2), 2),
+        (both(both(ty == 1, core == 1), both(z % 4 == 2, z > 2)), 3),
+        (both(both(ty == 1, core == 1), z == 4), 6),
+        (both(both(ty == 1, core == 1), z == 12), 3),
+        (both(both(ty == 1, core == 1), z == 8), 2),
         (both(both(ty == 1, core == 0), z % 2 == 1), 2),
-        (both(both(ty == 1, core == 0), z % 4 == 2), 5),
-        (both(both(ty == 1, core == 0), z == 4), 5),
-        (both(both(ty == 1, core == 0), z == 12), 2),
-        (both(both(ty == 1, core == 0), z == 8), 9),
+        (both(both(ty == 1, core == 0), z % 4 == 2), 4),
+        (both(both(ty == 1, core == 0), z == 4), 6),
+        (both(both(ty == 1, core == 0), z == 12), 3),
+        (both(both(ty == 1, core == 0), z == 8), 7),
     )
     greeted = sum(condition.astype(jnp.int32) * size for condition, size in sizes)
     for load in loads[3:]:
@@ -191,9 +220,9 @@
     side = jnp.where(
         is_p1,
         y // 2,
-        jnp.where(is_p2, x % 2, jnp.where(is_p3, x // 2, jnp.where(is_p4, core, jnp.where(is_gate, z % 2, z // 4 % 2)))),
+        jnp.where(is_p2, x % 2, jnp.where(is_p3, x // 2, jnp.where(is_p4, core, z % 2))),
     )
-    steps = ((is_p1, column[2]), (is_p2, my_p3), (is_p3, p4), (is_p4, gate), (is_gate, p6), (is_p7, p8))
+    steps = ((is_p1, column[2]), (is_p2, my_p3), (is_p3, p4), (is_p4, gate), (is_gate, p6))
     parent = tuple(sum(condition.astype(jnp.int32) * device[k] for condition, device in steps) for k in range(2))
     up_left = remote(coef, child.at[:, left_part], 1, 0, parent)
     up_right = remote(coef, child.at[:, right_part], 1, 1, parent)
@@ -204,31 +233,36 @@
     send_down2 = [remote(down.at[s, 0], leaf_map2, 5 + n, 5, column[k]) for n, (k, s) in enumerate(sides2)]
     send_cross4 = [remote(cross_sum.at[s], cross_a, 2 + s, 11, p3s[s]) for s in range(2)]
     send_up4 = [remote(up.at[s, 0], map_a, 7 + s, 7, p3s[s]) for s in range(2)]
-    send_part4 = [remote(path_coef, parts.at[k], 9, 14 + k, gate) for k in range(2)]
+    send_part4 = [remote(path_coef, parts4.at[k], 9, 21 + k, gate) for k in range(2)]
     send_down4 = [remote(down.at[s, 0], map_d, 5 + s, 10, p3s[s]) for s in range(2)]
     send_cross6 = [remote(cross_sum.at[s], cross_b, 2 + s, 12, gates_of_p6[s]) for s in range(2)]
     send_up6 = [remote(up.at[s, 0], map_a, 4 + s, 7, gates_of_p6[s]) for s in range(2)]
     send_down6 = [remote(down.at[s, 0], map_c, 6 + s, 9, gates_of_p6[s]) for s in range(2)]
+    halves = [pl.ds(k * (width // 2), width // 2) for k in range(2)]
+    send_down6_half = [remote(down.at[0, 0, half], map_c.at[half], (6, 8)[k], 9, gates_of_p6[0]) for k, half in enumerate(halves)]
     send_cross7 = [remote(cross_sum.at[k // 2], cross_a, 2 + k, 11, gates_of_p7[k]) for k in range(4)]
     send_down7 = [remote(down.at[k // 2, 0], map_d, 10 + k, 10, gates_of_p7[k]) for k in range(4)]
     pass_down7 = remote(map_d, map_d, 7, 10, at(z - 1, 1, 0, 0))
-    send_cross8 = [remote(cross_sum.at[s], cross_a, 2 + s, 11, p7s_of_p8[s]) for s in range(2)]
-    send_cross8_first = [remote(cross_sum.at[0], cross_c, 10 + k, 20, first_gates[k]) for k in range(4)]
-    send_up8 = remote(up.at[0, 0], map_a, 4, 7, p7s_of_p8[0])
-    send_down8 = [remote(down.at[s, 0], map_c, 6 + s, 9, p7s_of_p8[s]) for s in range(2)]
-    halves = [pl.ds(k * (width // 2), width // 2) for k in range(2)]
-    send_down8_half = [remote(down.at[0, 0, half], map_c.at[half], 6 + 5 * k, 9, p7s_of_p8[0]) for k, half in enumerate(halves)]
+    send_cross8 = [remote(top_sum.at[s], cross_c, 16 + s, 20, hubs_of_center[s]) for s in range(2)]
+    send_cross8_first = [remote(top_sum.at[0], cross_c, 18 + k, 20, first_gates[k]) for k in range(4)]
+    send_top_up7 = remote(up, top_up, 6, 23, hub)
+    send_top_up8 = remote(up, top_up, 4, 23, center)
+    send_top_cross = remote(cross, top_cross, 8, 24, center)
+    send_up8 = [remote(up.at[s, 0], map_e, 4 + s, 27, hubs_of_center[s]) for s in range(2)]
+    send_down8 = [remote(down.at[s, 0], map_b, 6 + s, 8, hubs_of_center[s]) for s in range(2)]
     send_down8_first = [remote(down.at[0, 0], map_b, 14 + k, 8, first_gates[k]) for k in range(4)]
     pass_down8 = remote(map_b, map_b, 8, 8, at(z - 1, 1, 0, 0))
-    send_cross9 = [remote(cross.at[0, 0], map_b, 2 + k, 8, at((10, 12)[k], 0, 0, 0)) for k in range(2)]
-    send_cross9 += [remote(cross.at[1, 0], map_b, 4, 8, left_p8)]
-    send_part6 = [remote(path_coef, parts.at[k], 2, 14 + k, p7) for k in range(4)]
+    send_cross9 = [remote(cross.at[0, 0], map_f, 2, 28, third_hub), remote(cross.at[0, 0], map_f, 3, 28, fourth_hub)]
+    send_cross9 += [remote(cross.at[1, 0], map_f, 4, 28, at(4, 1, 0, 0))]
+    send_part6 = [remote(path_coef, parts6.at[k], 2, 14 + k, hub) for k in range(4)]
+    send_child7 = remote(top_child, child, 9, 0, p7)
+    send_coef7 = [remote(top_coef, top_child.at[:, part], 10, 25 + k, center) for k, part in enumerate((left_part, right_part))]
     send_part8 = [
-        [remote(path_coef, parts8.at[k], 12 + n, 18 + k, device) for n, device in enumerate((*first_gates, second_p7))]
+        [remote(far_out, parts8.at[k], 11 + n, 18 + k, device) for n, device in enumerate((*first_gates, second_hub))]
         for k in range(2)
     ]
-    send_part8_right = [remote(path_coef, parts8.at[0], 8 + k, 18, right_p7s[k]) for k in range(2)]
-    send_above7 = [remote(outgoing.at[0], above, 16 + k, 13, gates_of_p7[k]) for k in (0, 3, 1, 2)]
+    send_part8_right = [remote(far_out, parts8.at[0], 11 + k, 18, (third_hub, fourth_hub)[k]) for k in range(2)]
+    send_above7 = [remote(top_out, above, 16 + n, 13, gates_of_p7[k]) for n, k in enumerate((0, 3, 1))]
     send_above4 = [remote(outgoing.at[k // 2], above, 3 + k, 13, p3s_of_gate[k]) for k in range(4)]
     send_above2_left = [remote(outgoing.at[0], leaf_above, 2 + k, 6, left_column[k]) for k in (2, 1, 3, 0)]
     send_above2_right = [remote(outgoing.at[1], leaf_above, 5 + k, 6, column[k]) for k in (2, 1, 3)]
@@ -253,6 +287,10 @@
     @pl.when(is_p1)
     def _():
         pl.semaphore_signal(go_sem, inc=1, device_id=left_leaf, device_id_type=MESH)
+
+    @pl.when(both(both(ty == 1, core == 1), z == 8))
+    def _():
+        pl.semaphore_signal(late_sem, inc=1, device_id=at(8, 0, 0, 0), device_id_type=MESH)
 
     def mask_up():
         keep = lax.broadcasted_iota(jnp.int32, (width, width), 1) < node_rank
@@ -378,18 +416,86 @@
             send_down7[0].wait_recv()
             pass_down7.start()
 
+        map_keep = lax.broadcasted_iota(jnp.int32, (width, width), 1) < node_rank
+        send_up6[0].wait_recv()
+        for s in range(2):
+            ahead = dot(jnp.where(map_keep, up[s, 0], jnp.zeros((width, width), BF16)), map_a[...])
+            gate_up[s] = ahead.astype(BF16)
         for copy in send_part4:
             copy.wait_recv()
-        child[:, left_part] = (parts[0].astype(F32) + parts[1].astype(F32)).astype(BF16)
+        child[:, left_part] = (parts4[0].astype(F32) + parts4[1].astype(F32)).astype(BF16)
         up_right.wait_recv()
-        send_up(dot(child[:, left_part], up[0, 0]) + dot(child[:, right_part], up[1, 0]))
-        send_up6[0].wait_recv()
-        path_coef[...] = dot(coef[...], map_a[...]).astype(BF16)
-        for k in range(4):
+        six = dot(child[:, left_part], gate_up[0]) + dot(child[:, right_part], gate_up[1])
+        path_coef[...] = six.astype(BF16)
+        for k in (0, 1, 3):
 
             @pl.when(z % 4 == k)
             def _():
                 send_part6[k].start()
+
+        send_up(dot(child[:, left_part], up[0, 0]) + dot(child[:, right_part], up[1, 0]))
+
+        @pl.when(is_hub)
+        def _():
+            parts6[2] = path_coef[...]
+            send_top_up7.wait_recv()
+
+            @pl.when(is_far_hub)
+            def _():
+                send_up8[0].wait_recv()
+                send_cross9[0].wait_recv()
+                map_e[...] = dot(map_e[...], map_f[...]).astype(BF16)
+
+            for k in (0, 1, 3):
+                send_part6[k].wait_recv()
+            for k, part in enumerate((left_part, right_part)):
+                six = parts6[2 * k].astype(F32) + parts6[2 * k + 1].astype(F32)
+                top_child[:, part] = six.astype(BF16)
+            seven = dot(top_child[:, left_part], top_up[0, 0]) + dot(top_child[:, right_part], top_up[1, 0])
+            top_coef[...] = seven.astype(BF16)
+            for k in range(2):
+
+                @pl.when(z // 4 % 2 == k)
+                def _():
+                    send_coef7[k].start()
+
+            @pl.when(is_far_hub)
+            def _():
+                far_out[...] = dot(top_coef[...], map_e[...]).astype(BF16)
+                for k in range(2):
+
+                    @pl.when(z == 10 + 4 * k)
+                    def _():
+                        start(send_part8[k])
+
+            send_child7.start()
+
+        def center_cross_terms():
+            send_top_cross.wait_recv()
+            top_sum[0] = dot(top_child[:, right_part], top_cross[0, 0]).astype(BF16)
+            top_sum[1] = dot(top_child[:, left_part], top_cross[1, 0]).astype(BF16)
+
+        @pl.when(is_left_center)
+        def _():
+            send_top_up8.wait_recv()
+            send_coef7[0].wait_recv()
+            send_coef7[1].wait_recv()
+            center_cross_terms()
+            start(send_cross8_first)
+            send_cross8[1].start()
+            eight = dot(top_child[:, left_part], top_up[0, 0]) + dot(top_child[:, right_part], top_up[1, 0])
+            top_coef[...] = eight.astype(BF16)
+            send_cross9[2].wait_recv()
+            far_out[...] = dot(top_coef[...], map_f[...]).astype(BF16)
+            start(send_part8_right)
+
+        @pl.when(is_right_center)
+        def _():
+            pl.semaphore_signal(late_sem, inc=1, device_id=p8, device_id_type=MESH)
+            send_coef7[1].wait_recv()
+            send_coef7[0].wait_recv()
+            center_cross_terms()
+            start(send_cross8)
 
         cross_terms()
 
@@ -408,118 +514,95 @@
         mask_down()
         for copy in send_up6:
             copy.wait_send()
-        start(send_down6)
+        send_down6[1].start()
+
+        @pl.when(z % 4 == 1)
+        def _():
+            send_down6[0].start()
+
+        @pl.when(both(z % 4 == 3, z != 7))
+        def _():
+            send_down6_half[0].start()
+
+        up_right.wait_recv()
+
+        @pl.when(both(z % 4 == 3, z != 7))
+        def _():
+            send_down6_half[1].start()
+
+        @pl.when(z == 7)
+        def _():
+            send_down6[0].start()
+
         up_left.wait_recv()
-        up_right.wait_recv()
         cross_terms()
         start(send_cross6)
 
     @pl.when(is_p7)
     def _():
+        load_up.wait()
+        mask_up()
+        send_top_up7.start()
         load_down.wait()
         mask_down()
         start(send_down7[1:])
-        load_up.wait()
         load_cross.wait()
-
-        @pl.when(is_third_p7)
-        def _():
-            send_up8.wait_recv()
-            send_cross9[0].wait_recv()
-            map_a[...] = dot(map_a[...], map_b[...]).astype(BF16)
-
-        for s in range(2):
-            for k in (2 * s, 2 * s + 1):
-                send_part6[k].wait_recv()
-            six = parts[2 * s].astype(F32) + parts[2 * s + 1].astype(F32)
-            child[:, (left_part, right_part)[s]] = six.astype(BF16)
-        send_up(dot(child[:, left_part], up[0, 0]) + dot(child[:, right_part], up[1, 0]))
-
-        @pl.when(is_third_p7)
-        def _():
-            path_coef[...] = dot(coef[...], map_a[...]).astype(BF16)
-            start(send_part8[0])
-
+        send_child7.wait_recv()
         cross_terms()
         start(send_cross7)
 
     @pl.when(is_p8)
+    def _():
+        load_up.wait()
+        mask_up()
+        load_cross.wait()
+        send_top_cross.start()
+        load_down.wait()
+        mask_down()
+
+        @pl.when(is_left_p8)
+        def _():
+            send_down8[1].start()
+
+        @pl.when(is_right_p8)
+        def _():
+            send_up8[1].start()
+
+        send_cross1[0].wait_recv()
+
+        @pl.when(is_right_p8)
+        def _():
+            send_down1[0].wait_recv()
+            send_up8[0].start()
+            pl.semaphore_wait(late_sem, 1)
+            start(send_down8)
+
+        @pl.when(is_left_p8)
+        def _():
+            send_top_up8.start()
+            send_down8_first[1].start()
+            send_down1[0].wait_recv()
+            for k, after in ((1, 3), (3, 2)):
+                send_down8_first[k].wait_send()
+                send_down8_first[after].start()
+
+    @pl.when(both(on_top, z % 8 == 0))
     def _():
         load_up.wait()
         load_cross.wait()
         load_down.wait()
-        mask_down()
-        @pl.when(is_right_p8)
-        def _():
-            send_down8[1].start()
-            mask_up()
-
-        send_cross1[0].wait_recv()
-
-        @pl.when(is_right_p8)
-        def _():
-            send_down1[0].wait_recv()
-            send_up8.start()
-            send_up8.wait_send()
-            send_down8_half[0].start()
-            send_cross9[1].wait_recv()
-            map_a[...] = dot(up[1, 0], map_b[...]).astype(BF16)
-            up_right.wait_recv()
-            path_coef[...] = dot(child[:, right_part], map_a[...]).astype(BF16)
-            start(send_part8[1])
-            send_down8_half[1].start()
-            up_left.wait_recv()
-            cross_terms()
-            start(send_cross8)
-
-        @pl.when(is_left_p8)
-        def _():
-            send_down8[1].start()
-            send_down8_first[1].start()
-            send_down1[0].wait_recv()
-            send_down8_first[1].wait_send()
-            start(send_down8_first[2:])
-            up_left.wait_recv()
-            eight = dot(child[:, left_part], up[0, 0])
-            up_right.wait_recv()
-            cross_terms()
-            start(send_cross8_first)
-            send_cross8[1].start()
-            eight += dot(child[:, right_part], up[1, 0])
-            coef[...] = jnp.where(node_keep, eight, 0.0).astype(BF16)
-            send_cross9[2].wait_recv()
-            path_coef[...] = dot(coef[...], map_b[...]).astype(BF16)
-            start(send_part8_right)
-
-    @pl.when(both(on_top, z % 8 == 0))
-    def _():
-        load_up.wait()
-        load_cross.wait()
-        load_down.wait()
 
     @pl.when(is_p9)
     def _():
-        start(send_cross9)
+        send_cross9[0].start()
+        send_cross9[2].start()
+        pl.semaphore_wait(late_sem, 1)
+        send_cross9[1].start()
 
     load_diag.wait()
     product[...] = dot(rhs[...], diag[...])
     load_out.wait()
 
-    @pl.when(both(is_p7, z > 2))
-    def _():
-        send_down8[0].wait_recv()
-        send_cross8[0].wait_recv()
-        send_part8[0][0].wait_recv()
-
-        @pl.when(is_second_p7)
-        def _():
-            send_part8[1][0].wait_recv()
-            crossed = parts8[0].astype(F32) + parts8[1].astype(F32)
-            parts8[0] = crossed.astype(BF16)
-
-        outgoing[0] = (cross_a[...] + dot(parts8[0], map_c[...])).astype(BF16)
-        start(send_above7)
-
     @pl.when(is_gate)
     def _():
         @pl.when(z % 4 != 1)
@@ -552,15 +635,34 @@
         @pl.when(z < 4)
         def _():
             send_cross8_first[0].wait_recv()
-            cross_b[...] += dot(cross_c[...].astype(BF16), map_d[...])
+            cross_b[...] += dot(cross_c[...], map_d[...])
             for k in range(2):
                 send_part8[k][0].wait_recv()
             crossed = (parts8[0].astype(F32) + parts8[1].astype(F32)).astype(BF16)
             above[...] = (cross_b[...] + dot(crossed, map_b[...])).astype(BF16)
 
+        @pl.when(is_late_hub)
+        def _():
+            send_down8[0].wait_recv()
+            send_cross8[0].wait_recv()
+            send_part8[0][0].wait_recv()
+
+            @pl.when(z == 6)
+            def _():
+                send_part8[1][0].wait_recv()
+                crossed = parts8[0].astype(F32) + parts8[1].astype(F32)
+                parts8[0] = crossed.astype(BF16)
+
+            top_out[...] = (cross_c[...].astype(F32) + dot(parts8[0], map_b[...])).astype(BF16)
+            start(send_above7)
+            above[...] = top_out[...]
+
+        @pl.when(both(z >= 4, z % 4 != 2))
+        def _():
+            send_above7[0].wait_recv()
+
         @pl.when(z >= 4)
         def _():
-            send_above7[0].wait_recv()
             above[...] = (cross_b[...] + dot(above[...], map_d[...])).astype(BF16)
 
         for s in range(2):
@@ -576,7 +678,15 @@
             down[s, 0] = dot(map_d[...], down[s, 0]).astype(BF16)
         send_above4[0].wait_recv()
         outgoing[0] = (cross_sum[0] + dot(above[...], down[0, 0])).astype(BF16)
-        start(send_above2_left)
+
+        @pl.when(core == 0)
+        def _():
+            start(send_above2_left)
+
+        @pl.when(core == 1)
+        def _():
+            start([send_above2_left[3], *send_above2_left[:3]])
+
         outgoing[1] = (cross_sum[1] + dot(above[...], down[1, 0])).astype(BF16)
         start(send_above2_right)
         leaf_above[...] = outgoing[1]
@@ -618,13 +728,20 @@
     sent(both(is_p4, core == 0), send_up4)
     sent(both(is_p4, core == 1), [up_left])
     sent(is_p4, [*send_cross4, *send_down4])
-    sent(is_gate, [up_left, send_part6[0], *send_above4])
-    sent(is_p6, [*send_down6, *send_cross6])
-    sent(is_p7, [up_left, *send_down7[1:], *send_cross7])
-    sent(both(is_p7, z > 2), send_above7)
-    sent(is_third_p7, send_part8[0])
-    sent(is_right_p8, [send_down8[1], *send_down8_half, *send_part8[1], *send_cross8])
-    sent(is_left_p8, [send_down8[1], *send_down8_first[2:], *send_cross8_first, send_cross8[1], *send_part8_right])
+    sent(is_gate, [up_left, *send_above4])
+    sent(both(is_gate, z % 4 != 2), [send_part6[0]])
+    sent(is_hub, [send_coef7[0], send_child7])
+    sent(is_late_hub, send_above7)
+    sent(is_far_hub, send_part8[0])
+    sent(is_left_center, [*send_cross8_first, send_cross8[1], *send_part8_right])
+    sent(is_right_center, send_cross8)
+    sent(is_p6, [send_down6[1], *send_cross6])
+    sent(both(is_p6, both(z % 4 == 3, z != 7)), send_down6_half)
+    sent(both(is_p6, jnp.logical_not(both(z % 4 == 3, z != 7))), [send_down6[0]])
+    sent(is_p7, [send_top_up7, *send_down7[1:], *send_cross7])
+    sent(is_p8, [send_top_cross, send_down8[1]])
+    sent(is_left_p8, [send_top_up8, send_down8_first[2]])
+    sent(is_right_p8, [*send_up8, send_down8[0]])
     sent(is_p9, send_cross9)
 
 
@@ -656,19 +773,31 @@
             full_map,
             full_map,
             full_map,
+            full_map,
+            pltpu.VMEM(up_maps.shape, BF16),
+            pltpu.VMEM(cross_maps.shape, BF16),
+            vector(columns=2 * width),
+            vector(),
+            vector(2),
+            vector(),
+            vector(),
+            pltpu.VMEM((2, width, width), BF16),
+            full_map,
             pltpu.VMEM((width, leaf_width), BF16),
             vector(kind=F32),
             vector(kind=F32),
-            vector(kind=F32),
+            vector(),
             vector(kind=F32),
             vector(kind=F32, columns=leaf_width),
             vector(),
             vector(),
+            vector(2),
             vector(4),
             vector(2),
             pltpu.SemaphoreType.DMA((8,)),
-            pltpu.SemaphoreType.DMA((20,)),
-            pltpu.SemaphoreType.DMA((21,)),
+            pltpu.SemaphoreType.DMA((22,)),
+            pltpu.SemaphoreType.DMA((29,)),
+            pltpu.SemaphoreType.REGULAR,
             pltpu.SemaphoreType.REGULAR,
         ],
         compiler_params=pltpu.CompilerParams(

time: 46.9 us -> 44 us (0.938)
  Pallas kernels: 45.4 us -> 42.2 us
    pallas_call x1, Pallas kernels: 45.4 us -> 42.2 us  [on_device(): pl.pallas_call(kernel, out_shape=jax.ShapeDtypeStruct((rows, leaf), F32),...]
where the time goes in v8:
time: 44 us; the launch traced here: 43.6 us
  Pallas kernels  42.2 us (96%)
  local copies, waits for them, and re-layouts  1.38 us (3%)
    pallas_call x1, Pallas kernels, on_device(): pl.pallas_call(kernel, out_shape=jax.ShapeDtypeStruct((rows, leaf), F32),...  42.2 us
    unnamed x1, local copies, waits for them, and re-layouts  1.38 us

profile of v8, /device:TPU:1, one launch (start us, length us, event | category | flops | bytes accessed | tf_op | source)
XLA Modules:
  0.0 43.6 jit_solution(8287740758639297178)
XLA Ops:
  0.0 42.2 %shard_map.82 = f32[16,512]{1,0:T(8,128)} custom-call(bf16[16,512]{1,0:T(8,128)(2,1)} %rhs_hbm.1, bf16[512,512]{1,0:T(8,128)(2,1)} %diag_hbm.1, bf16[512,128]{1,0:T(8,128)(2,1)} %in_hbm.1, bf16[128,512]{1,0:T(8,128)(2,1)} %out_hbm.1, bf16[2,1,512,512]{3,2,1,0:T(8,128)(2,1)} %up_hbm.1, bf16[2,1,512,512]{3,2,1,0:T(8,128)(2,1)} %cross_hbm.1, ...), custom_call_target="tpu_custom_call" | custom-call | tf_op jit(solution)/shard_map/pallas_call | solution.py:757
  42.2 1.4 %copy.10 = f32[16,512]{1,0:T(8,128)} copy(f32[16,512]{1,0:T(8,128)} %shard_map.82) | data formatting | bytes 65536

commit v9 on v8

--- a/solution.py
+++ b/solution.py
@@ -51,6 +51,9 @@
     top_out,
     far_out,
     gate_up,
+    head_map,
+    head_base,
+    head_out,
     leaf_map2,
     leaf_map1,
     cross_a,
@@ -91,6 +94,7 @@
     is_p8 = both(on_top, z % 8 == 4)
     is_p9 = both(on_top, z == 8)
     is_even = y % 2 == 0
+    is_head = both(y == 0, x % 2 == 0)
     is_hub = both(is_gate, z % 4 == 2)
     is_late_hub = both(is_hub, z > 2)
     is_far_hub = both(is_hub, z >= 8)
@@ -123,7 +127,6 @@
     leaf_peer = at(z, core, x, y + 1)
     left_leaf = at(z, core, x, y - 1)
     column = [at(z, core, x, k) for k in range(N_Y)]
-    left_column = [at(z, core, x - 1, k) for k in range(N_Y)]
     my_p3 = at(z, core, x_odd, 0)
     p3s = [at(z, core, 1, 0), at(z, core, 3, 0)]
     p4 = at(z, core, 2, 0)
@@ -135,7 +138,7 @@
     gates_of_p7 = [at(z_seven - 2 + k, 1, 0, 0) for k in range(4)]
     hub, center = at(z_seven, 1, 0, 0), at(z_eight, 1, 0, 0)
     hubs_of_center = [at(z_eight - 2, 1, 0, 0), at(z_eight + 2, 1, 0, 0)]
-    first_gates = [at(k, 1, 0, 0) for k in range(4)]
+    first_gates = [at(k, 1, 0, 0) for k in range(6)]
     second_hub, third_hub, fourth_hub = at(6, 1, 0, 0), at(10, 1, 0, 0), at(14, 1, 0, 0)
 
     barrier = pltpu.get_barrier_semaphore()
@@ -153,17 +156,18 @@
     next_p3 = collector(z, core, x_odd)
     greet(is_p1, [left_leaf])
     greet(y == 1, [column[3]])
-    greet(both(y == 1, x_even), [next_p3])
-    greet(y == 3, [next_p3])
-    greet(is_p2, [column[1], column[3], next_p3])
+    greet(y == 3, [collector(z, core, x)])
+    greet(is_p2, [column[1], column[3]])
+    greet(both(is_p2, x % 2 == 1), [column[1]])
+    greet(on_top, [collector(z, 1, 0)])
     greet(y == 0, [column[1], column[3]])
     greet(both(y == 0, x_even), [next_p3])
     greet(is_p3, [at(z, core, x - 1, 3), collector(z, core, 2), collector(z, 1, 0)])
-    greet(is_p4, [collector(z, core, 1), collector(z, core, 3)])
+    greet(is_p4, [collector(z, core, 1), collector(z, core, 3), collector(z, 1, 0)])
     greet(is_gate, [collector(z, 0, 1), collector(z, 0, 3), collector(z, 1, 2)] + [collector(z_odd, 0, 0), collector(z_seven, 0, 0)])
     greet(both(is_gate, z % 4 == 0), [collector(z + 1, 1, 0)])
-    greet(both(is_gate, z < 4), [collector(4, 0, 0), collector(8, 0, 0), collector(4, 1, 0)])
-    greet(both(both(is_gate, z >= 4), z % 4 != 2), [collector(z_seven, 1, 0)])
+    greet(both(is_gate, both(z < 6, z != 4)), [collector(4, 0, 0), collector(8, 0, 0), collector(4, 1, 0)])
+    greet(both(both(is_gate, z > 6), z % 4 != 2), [collector(z_seven, 1, 0)])
     greet(is_hub, [collector(z_seven - 2 + k, 1, 0) for k in (0, 1, 3)])
     greet(is_late_hub, [collector(z_eight, 0, 0), collector(z_eight, 1, 0)])
     greet(both(is_late_hub, z < 12), [collector(8, 0, 0)])
@@ -182,22 +186,24 @@
         (y == 3, 3),
         (both(y == 3, x_even), 1),
         (y == 1, 2),
-        (both(y == 1, x % 2 == 1), 7),
+        (both(y == 1, x_even), 1),
+        (both(y == 1, x % 2 == 1), 4),
         (both(both(y == 1, x % 2 == 1), core == 0), 1),
         (both(y == 1, x == 2), 2 + core),
-        (both(ty == 1, core == 1), 5),
+        (both(ty == 1, core == 1), 8),
         (both(both(ty == 1, core == 1), z % 4 != 2), 1),
         (both(both(ty == 1, core == 1), z % 4 == 1), 1),
         (both(both(ty == 1, core == 1), z % 4 == 2), 2),
-        (both(both(ty == 1, core == 1), both(z % 4 == 2, z > 2)), 3),
-        (both(both(ty == 1, core == 1), z == 4), 6),
+        (both(both(ty == 1, core == 1), z == 6), 1),
+        (both(both(ty == 1, core == 1), both(z % 4 == 2, z > 6)), 3),
+        (both(both(ty == 1, core == 1), z == 4), 7),
         (both(both(ty == 1, core == 1), z == 12), 3),
         (both(both(ty == 1, core == 1), z == 8), 2),
         (both(both(ty == 1, core == 0), z % 2 == 1), 2),
         (both(both(ty == 1, core == 0), z % 4 == 2), 4),
-        (both(both(ty == 1, core == 0), z == 4), 6),
+        (both(both(ty == 1, core == 0), z == 4), 7),
         (both(both(ty == 1, core == 0), z == 12), 3),
-        (both(both(ty == 1, core == 0), z == 8), 7),
+        (both(both(ty == 1, core == 0), z == 8), 8),
     )
     greeted = sum(condition.astype(jnp.int32) * size for condition, size in sizes)
     for load in loads[3:]:
@@ -242,15 +248,16 @@
     send_down6_half = [remote(down.at[0, 0, half], map_c.at[half], (6, 8)[k], 9, gates_of_p6[0]) for k, half in enumerate(halves)]
     send_cross7 = [remote(cross_sum.at[k // 2], cross_a, 2 + k, 11, gates_of_p7[k]) for k in range(4)]
     send_down7 = [remote(down.at[k // 2, 0], map_d, 10 + k, 10, gates_of_p7[k]) for k in range(4)]
-    pass_down7 = remote(map_d, map_d, 7, 10, at(z - 1, 1, 0, 0))
+    pass_down7 = remote(map_d, map_d, 22, 10, at(z - 1, 1, 0, 0))
     send_cross8 = [remote(top_sum.at[s], cross_c, 16 + s, 20, hubs_of_center[s]) for s in range(2)]
     send_cross8_first = [remote(top_sum.at[0], cross_c, 18 + k, 20, first_gates[k]) for k in range(4)]
+    send_cross8_first += [remote(top_sum.at[1], cross_c, 13, 20, first_gates[5])]
     send_top_up7 = remote(up, top_up, 6, 23, hub)
     send_top_up8 = remote(up, top_up, 4, 23, center)
     send_top_cross = remote(cross, top_cross, 8, 24, center)
     send_up8 = [remote(up.at[s, 0], map_e, 4 + s, 27, hubs_of_center[s]) for s in range(2)]
     send_down8 = [remote(down.at[s, 0], map_b, 6 + s, 8, hubs_of_center[s]) for s in range(2)]
-    send_down8_first = [remote(down.at[0, 0], map_b, 14 + k, 8, first_gates[k]) for k in range(4)]
+    send_down8_first = [remote(down.at[k // 4, 0], map_b, 14 + k, 8, first_gates[k]) for k in range(6)]
     pass_down8 = remote(map_b, map_b, 8, 8, at(z - 1, 1, 0, 0))
     send_cross9 = [remote(cross.at[0, 0], map_f, 2, 28, third_hub), remote(cross.at[0, 0], map_f, 3, 28, fourth_hub)]
     send_cross9 += [remote(cross.at[1, 0], map_f, 4, 28, at(4, 1, 0, 0))]
@@ -262,10 +269,15 @@
         for k in range(2)
     ]
     send_part8_right = [remote(far_out, parts8.at[0], 11 + k, 18, (third_hub, fourth_hub)[k]) for k in range(2)]
-    send_above7 = [remote(top_out, above, 16 + n, 13, gates_of_p7[k]) for n, k in enumerate((0, 3, 1))]
-    send_above4 = [remote(outgoing.at[k // 2], above, 3 + k, 13, p3s_of_gate[k]) for k in range(4)]
-    send_above2_left = [remote(outgoing.at[0], leaf_above, 2 + k, 6, left_column[k]) for k in (2, 1, 3, 0)]
-    send_above2_right = [remote(outgoing.at[1], leaf_above, 5 + k, 6, column[k]) for k in (2, 1, 3)]
+    send_above7 = [remote(top_out, above, 18 + n, 13, gates_of_p7[k]) for n, k in enumerate((3, 0, 1))]
+    others = [at(z, 0, 2, 0), p3s_of_gate[1], at(z, 0, 0, 0), p3s_of_gate[0], at(z, 1, 2, 0), p3s_of_gate[3], p3s_of_gate[2]]
+    above4_sems = (3, 4, 5, 6, 7, 23, 24)
+    send_above4 = [remote(outgoing.at[n // 4], above, above4_sems[n], 13, device) for n, device in enumerate(others)]
+    head = at(z, core, x - 1, 0)
+    send_head_map = remote(head_map, head_map, 2, 29, head)
+    send_head_base = remote(cross_sum.at[0], head_base, 3, 30, head)
+    send_above2 = [remote(head_out, leaf_above, 24 + k, 6, column[k]) for k in (3, 2, 1)]
+    send_above2_right = [remote(outgoing.at[1], leaf_above, 5 + k, 6, column[k]) for k in (3, 2, 1)]
 
     def start(copies):
         for copy in copies:
@@ -390,6 +402,9 @@
         @pl.when(core == 0)
         def _():
             start(send_up4)
+            load_down.wait()
+            mask_down()
+            start(send_down4)
             up_left.wait_recv()
             up_right.wait_recv()
 
@@ -400,9 +415,12 @@
         load_cross.wait()
         cross_terms()
         start(send_cross4)
-        load_down.wait()
-        mask_down()
-        start(send_down4)
+
+        @pl.when(core == 1)
+        def _():
+            load_down.wait()
+            mask_down()
+            start(send_down4)
 
     @pl.when(is_gate)
     def _():
@@ -483,6 +501,7 @@
             center_cross_terms()
             start(send_cross8_first)
             send_cross8[1].start()
+            cross_c[...] = top_sum[1]
             eight = dot(top_child[:, left_part], top_up[0, 0]) + dot(top_child[:, right_part], top_up[1, 0])
             top_coef[...] = eight.astype(BF16)
             send_cross9[2].wait_recv()
@@ -563,6 +582,7 @@
         @pl.when(is_left_p8)
         def _():
             send_down8[1].start()
+            start(send_down8_first[4:])
 
         @pl.when(is_right_p8)
         def _():
@@ -616,7 +636,7 @@
         send_down6[0].wait_recv()
         map_d[...] = dot(map_d[...], map_c[...]).astype(BF16)
 
-        @pl.when(both(z < 4, z != 1))
+        @pl.when(both(z < 6, z != 1))
         def _():
             send_down8_first[0].wait_recv()
 
@@ -624,7 +644,7 @@
         def _():
             pass_down8.wait_send()
 
-        @pl.when(z < 4)
+        @pl.when(z < 6)
         def _():
             map_b[...] = dot(map_b[...], map_d[...]).astype(BF16)
 
@@ -632,9 +652,12 @@
         send_cross6[0].wait_recv()
         cross_b[...] += dot(cross_a[...].astype(BF16), map_c[...])
 
-        @pl.when(z < 4)
-        def _():
-            send_cross8_first[0].wait_recv()
+        @pl.when(z < 6)
+        def _():
+            @pl.when(z != 4)
+            def _():
+                send_cross8_first[0].wait_recv()
+
             cross_b[...] += dot(cross_c[...], map_d[...])
             for k in range(2):
                 send_part8[k][0].wait_recv()
@@ -654,42 +677,58 @@
                 parts8[0] = crossed.astype(BF16)
 
             top_out[...] = (cross_c[...].astype(F32) + dot(parts8[0], map_b[...])).astype(BF16)
-            start(send_above7)
+            send_above7[0].start()
+
+            @pl.when(z > 6)
+            def _():
+                start(send_above7[1:])
+
             above[...] = top_out[...]
 
-        @pl.when(both(z >= 4, z % 4 != 2))
+        @pl.when(both(z > 6, z % 4 != 2))
         def _():
             send_above7[0].wait_recv()
 
-        @pl.when(z >= 4)
+        @pl.when(z >= 6)
         def _():
             above[...] = (cross_b[...] + dot(above[...], map_d[...])).astype(BF16)
 
         for s in range(2):
             outgoing[s] = (cross_sum[s] + dot(above[...], down[s, 0])).astype(BF16)
-            start(send_above4[2 * s : 2 * s + 2])
+            start(send_above4[4 * s : 4 * s + 4])
 
     @pl.when(is_p3)
     def _():
         send_down4[0].wait_recv()
+        head_map[...] = dot(map_d[...], down[0, 0]).astype(BF16)
+        send_head_map.start()
         send_cross4[0].wait_recv()
-        for s in range(2):
-            cross_sum[s] += dot(cross_a[...].astype(BF16), down[s, 0])
-            down[s, 0] = dot(map_d[...], down[s, 0]).astype(BF16)
+        cross_four = cross_a[...].astype(BF16)
+        cross_sum[0] += dot(cross_four, down[0, 0])
+        send_head_base.start()
+        cross_sum[1] += dot(cross_four, down[1, 0])
+        down[1, 0] = dot(map_d[...], down[1, 0]).astype(BF16)
         send_above4[0].wait_recv()
-        outgoing[0] = (cross_sum[0] + dot(above[...], down[0, 0])).astype(BF16)
-
-        @pl.when(core == 0)
-        def _():
-            start(send_above2_left)
-
-        @pl.when(core == 1)
-        def _():
-            start([send_above2_left[3], *send_above2_left[:3]])
-
         outgoing[1] = (cross_sum[1] + dot(above[...], down[1, 0])).astype(BF16)
         start(send_above2_right)
         leaf_above[...] = outgoing[1]
+
+    @pl.when(is_head)
+    def _():
+        send_head_map.wait_recv()
+        send_head_base.wait_recv()
+
+        @pl.when(is_gate)
+        def _():
+            head_out[...] = (head_base[...] + dot(outgoing[1], head_map[...])).astype(BF16)
+
+        @pl.when(jnp.logical_not(is_gate))
+        def _():
+            send_above4[0].wait_recv()
+            head_out[...] = (head_base[...] + dot(above[...], head_map[...])).astype(BF16)
+
+        start(send_above2)
+        leaf_above[...] = head_out[...]
 
     @pl.when(both(is_even, jnp.logical_not(is_p8)))
     def _():
@@ -708,9 +747,9 @@
     leaf_map1[...] = jnp.where(map_keep, dot(leaf_map2[...], leaf_map1[...]), 0.0).astype(BF16)
     leaf_map2[...] = dot(leaf_map1[...], leaf_out[...]).astype(BF16)
 
-    @pl.when(jnp.logical_not(is_p3))
-    def _():
-        send_above2_left[0].wait_recv()
+    @pl.when(y > 0)
+    def _():
+        send_above2[0].wait_recv()
 
     product[...] += dot(leaf_above[...], leaf_map2[...])
 
@@ -724,14 +763,16 @@
     sent(is_p1, [up_left, *send_cross1, *send_down1])
     sent(is_p2, [up_left, *send_cross2, *send_down2])
     sent(both(is_p3, core == 0), [send_part4[0]])
-    sent(is_p3, [up_left, *send_above2_left, *send_above2_right])
+    sent(is_p3, [up_left, send_head_map, send_head_base, *send_above2_right])
+    sent(is_head, send_above2)
     sent(both(is_p4, core == 0), send_up4)
     sent(both(is_p4, core == 1), [up_left])
     sent(is_p4, [*send_cross4, *send_down4])
     sent(is_gate, [up_left, *send_above4])
     sent(both(is_gate, z % 4 != 2), [send_part6[0]])
     sent(is_hub, [send_coef7[0], send_child7])
-    sent(is_late_hub, send_above7)
+    sent(is_late_hub, send_above7[:1])
+    sent(is_far_hub, send_above7[1:])
     sent(is_far_hub, send_part8[0])
     sent(is_left_center, [*send_cross8_first, send_cross8[1], *send_part8_right])
     sent(is_right_center, send_cross8)
@@ -740,7 +781,7 @@
     sent(both(is_p6, jnp.logical_not(both(z % 4 == 3, z != 7))), [send_down6[0]])
     sent(is_p7, [send_top_up7, *send_down7[1:], *send_cross7])
     sent(is_p8, [send_top_cross, send_down8[1]])
-    sent(is_left_p8, [send_top_up8, send_down8_first[2]])
+    sent(is_left_p8, [send_top_up8, send_down8_first[2], *send_down8_first[4:]])
     sent(is_right_p8, [*send_up8, send_down8[0]])
     sent(is_p9, send_cross9)
 
@@ -783,6 +824,9 @@
             vector(),
             pltpu.VMEM((2, width, width), BF16),
             full_map,
+            vector(kind=F32),
+            vector(),
+            full_map,
             pltpu.VMEM((width, leaf_width), BF16),
             vector(kind=F32),
             vector(kind=F32),
@@ -795,8 +839,8 @@
             vector(4),
             vector(2),
             pltpu.SemaphoreType.DMA((8,)),
-            pltpu.SemaphoreType.DMA((22,)),
-            pltpu.SemaphoreType.DMA((29,)),
+            pltpu.SemaphoreType.DMA((28,)),
+            pltpu.SemaphoreType.DMA((31,)),
             pltpu.SemaphoreType.REGULAR,
             pltpu.SemaphoreType.REGULAR,
         ],

time: 44 us -> 42.9 us (0.975)
  the two profiles are of different devices: /device:TPU:1 before, /device:TPU:10 now
where the time goes in v9:
time: 42.9 us; the launch traced here: 42.7 us
  Pallas kernels  41.3 us (96%)
  local copies, waits for them, and re-layouts  1.38 us (3%)
    pallas_call x1, Pallas kernels, on_device(): pl.pallas_call(kernel, out_shape=jax.ShapeDtypeStruct((rows, leaf), F32),...  41.3 us
    unnamed x1, local copies, waits for them, and re-layouts  1.38 us

profile of v9, /device:TPU:10, one launch (start us, length us, event | category | flops | bytes accessed | tf_op | source)
XLA Modules:
  0.0 42.7 jit_solution(1285315314928989750)
XLA Ops:
  0.0 41.3 %shard_map.82 = f32[16,512]{1,0:T(8,128)} custom-call(bf16[16,512]{1,0:T(8,128)(2,1)} %rhs_hbm.1, bf16[512,512]{1,0:T(8,128)(2,1)} %diag_hbm.1, bf16[512,128]{1,0:T(8,128)(2,1)} %in_hbm.1, bf16[128,512]{1,0:T(8,128)(2,1)} %out_hbm.1, bf16[2,1,512,512]{3,2,1,0:T(8,128)(2,1)} %up_hbm.1, bf16[2,1,512,512]{3,2,1,0:T(8,128)(2,1)} %cross_hbm.1, ...), custom_call_target="tpu_custom_call" | custom-call | tf_op jit(solution)/shard_map/pallas_call | solution.py:798
  41.3 1.4 %copy.10 = f32[16,512]{1,0:T(8,128)} copy(f32[16,512]{1,0:T(8,128)} %shard_map.82) | data formatting | bytes 65536

commit v10 on v9

--- a/solution.py
+++ b/solution.py
@@ -50,7 +50,7 @@
     top_sum,
     top_out,
     far_out,
-    gate_up,
+    gate_maps,
     head_map,
     head_base,
     head_out,
@@ -74,6 +74,29 @@
 ):
     rows, width = coef.shape
     leaf_width = leaf_coef.shape[1]
+    loads = [
+        pltpu.make_async_copy(source, target, load_sem.at[n])
+        for n, (source, target) in enumerate(
+            (
+                (rhs_hbm, rhs),
+                (in_hbm, leaf_in),
+                (rank_hbm, rank),
+                (up_hbm, up),
+                (cross_hbm, cross),
+                (down_hbm, down),
+                (diag_hbm, diag),
+                (out_hbm, leaf_out),
+            )
+        )
+    ]
+    load_rhs, load_in, load_rank, load_up, load_cross, load_down, load_diag, load_out = loads
+    quarter = in_hbm.shape[0] // 4
+    for n in range(4):
+        part = pl.ds(n * quarter, quarter)
+        pltpu.make_async_copy(in_hbm.at[part], leaf_in.at[part], load_sem.at[1]).start()
+    load_rhs.start()
+    load_rank.start()
+
     tx, ty = lax.axis_index("tx"), lax.axis_index("ty")
     z, core = tx // N_CORE, tx % N_CORE
     x, y = ty // N_Y, ty % N_Y
@@ -103,25 +126,6 @@
     is_left_p8 = both(on_top, z == 4)
     is_right_p8 = both(on_top, z == 12)
 
-    loads = [
-        pltpu.make_async_copy(source, target, load_sem.at[n])
-        for n, (source, target) in enumerate(
-            (
-                (rhs_hbm, rhs),
-                (in_hbm, leaf_in),
-                (rank_hbm, rank),
-                (up_hbm, up),
-                (cross_hbm, cross),
-                (down_hbm, down),
-                (diag_hbm, diag),
-                (out_hbm, leaf_out),
-            )
-        )
-    ]
-    load_rhs, load_in, load_rank, load_up, load_cross, load_down, load_diag, load_out = loads
-    for load in loads[:3]:
-        load.start()
-
     x_odd = x // 2 * 2 + 1
     z_odd, z_seven, z_eight = z // 2 * 2 + 1, z // 4 * 4 + 2, z // 8 * 8 + 4
     leaf_peer = at(z, core, x, y + 1)
@@ -171,7 +175,7 @@
     greet(is_hub, [collector(z_seven - 2 + k, 1, 0) for k in (0, 1, 3)])
     greet(is_late_hub, [collector(z_eight, 0, 0), collector(z_eight, 1, 0)])
     greet(both(is_late_hub, z < 12), [collector(8, 0, 0)])
-    greet(both(is_late_hub, z > 12), [collector(4, 1, 0), collector(8, 1, 0)])
+    greet(both(is_late_hub, z > 12), [collector(8, 1, 0)])
     greet(is_p9, [collector(8, 1, 0)])
     greet(
         both(is_gate, z % 8 == 4),
@@ -196,7 +200,7 @@
         (both(both(ty == 1, core == 1), z % 4 == 2), 2),
         (both(both(ty == 1, core == 1), z == 6), 1),
         (both(both(ty == 1, core == 1), both(z % 4 == 2, z > 6)), 3),
-        (both(both(ty == 1, core == 1), z == 4), 7),
+        (both(both(ty == 1, core == 1), z == 4), 6),
         (both(both(ty == 1, core == 1), z == 12), 3),
         (both(both(ty == 1, core == 1), z == 8), 2),
         (both(both(ty == 1, core == 0), z % 2 == 1), 2),
@@ -239,7 +243,7 @@
     send_down2 = [remote(down.at[s, 0], leaf_map2, 5 + n, 5, column[k]) for n, (k, s) in enumerate(sides2)]
     send_cross4 = [remote(cross_sum.at[s], cross_a, 2 + s, 11, p3s[s]) for s in range(2)]
     send_up4 = [remote(up.at[s, 0], map_a, 7 + s, 7, p3s[s]) for s in range(2)]
-    send_part4 = [remote(path_coef, parts4.at[k], 9, 21 + k, gate) for k in range(2)]
+    send_part4 = [remote(path_coef, parts4.at[k], 9, (19, 0)[k], gate) for k in range(2)]
     send_down4 = [remote(down.at[s, 0], map_d, 5 + s, 10, p3s[s]) for s in range(2)]
     send_cross6 = [remote(cross_sum.at[s], cross_b, 2 + s, 12, gates_of_p6[s]) for s in range(2)]
     send_up6 = [remote(up.at[s, 0], map_a, 4 + s, 7, gates_of_p6[s]) for s in range(2)]
@@ -247,37 +251,36 @@
     halves = [pl.ds(k * (width // 2), width // 2) for k in range(2)]
     send_down6_half = [remote(down.at[0, 0, half], map_c.at[half], (6, 8)[k], 9, gates_of_p6[0]) for k, half in enumerate(halves)]
     send_cross7 = [remote(cross_sum.at[k // 2], cross_a, 2 + k, 11, gates_of_p7[k]) for k in range(4)]
-    send_down7 = [remote(down.at[k // 2, 0], map_d, 10 + k, 10, gates_of_p7[k]) for k in range(4)]
-    pass_down7 = remote(map_d, map_d, 22, 10, at(z - 1, 1, 0, 0))
-    send_cross8 = [remote(top_sum.at[s], cross_c, 16 + s, 20, hubs_of_center[s]) for s in range(2)]
-    send_cross8_first = [remote(top_sum.at[0], cross_c, 18 + k, 20, first_gates[k]) for k in range(4)]
-    send_cross8_first += [remote(top_sum.at[1], cross_c, 13, 20, first_gates[5])]
-    send_top_up7 = remote(up, top_up, 6, 23, hub)
-    send_top_up8 = remote(up, top_up, 4, 23, center)
-    send_top_cross = remote(cross, top_cross, 8, 24, center)
-    send_up8 = [remote(up.at[s, 0], map_e, 4 + s, 27, hubs_of_center[s]) for s in range(2)]
+    send_down7 = [remote(down.at[k // 2, 0], map_d, 6 + k, 10, gates_of_p7[k]) for k in range(4)]
+    pass_down7 = remote(map_d, map_d, 3, 10, at(z - 1, 1, 0, 0))
+    send_cross8 = [remote(top_sum.at[s], cross_c, 7 + s, 18, hubs_of_center[s]) for s in range(2)]
+    send_cross8_first = [remote(top_sum.at[0], cross_c, 9 + k, 18, first_gates[k]) for k in range(4)]
+    send_cross8_first += [remote(top_sum.at[1], cross_c, 13, 18, first_gates[5])]
+    send_top_up7 = remote(up, top_up, 6, 20, hub)
+    send_top_up8 = remote(up, top_up, 4, 20, center)
+    send_top_cross = remote(cross, top_cross, 8, 14, center)
+    send_up8 = [remote(up.at[s, 0], map_e, 4 + s, 21, hubs_of_center[s]) for s in range(2)]
     send_down8 = [remote(down.at[s, 0], map_b, 6 + s, 8, hubs_of_center[s]) for s in range(2)]
-    send_down8_first = [remote(down.at[k // 4, 0], map_b, 14 + k, 8, first_gates[k]) for k in range(6)]
-    pass_down8 = remote(map_b, map_b, 8, 8, at(z - 1, 1, 0, 0))
-    send_cross9 = [remote(cross.at[0, 0], map_f, 2, 28, third_hub), remote(cross.at[0, 0], map_f, 3, 28, fourth_hub)]
-    send_cross9 += [remote(cross.at[1, 0], map_f, 4, 28, at(4, 1, 0, 0))]
-    send_part6 = [remote(path_coef, parts6.at[k], 2, 14 + k, hub) for k in range(4)]
-    send_child7 = remote(top_child, child, 9, 0, p7)
-    send_coef7 = [remote(top_coef, top_child.at[:, part], 10, 25 + k, center) for k, part in enumerate((left_part, right_part))]
+    send_down8_first = [remote(down.at[k // 4, 0], map_b, 8 + k, 8, first_gates[k]) for k in range(6)]
+    pass_down8 = remote(map_b, map_b, 4, 8, at(z - 1, 1, 0, 0))
+    send_cross9 = [remote(cross.at[0, 0], map_f, 2, 22, third_hub), remote(cross.at[0, 0], map_f, 3, 22, fourth_hub)]
+    send_cross9 += [remote(cross.at[1, 0], map_f, 4, 22, at(4, 1, 0, 0))]
+    send_part6 = [remote(path_coef, parts6.at[k], 2, (14, 15, 16, 16)[k], hub) for k in range(4)]
+    send_child7 = remote(top_child, child, 3, 0, p7)
+    send_coef7 = [remote(top_coef, top_child.at[:, part], 4, 15 + k, center) for k, part in enumerate((left_part, right_part))]
     send_part8 = [
-        [remote(far_out, parts8.at[k], 11 + n, 18 + k, device) for n, device in enumerate((*first_gates, second_hub))]
+        [remote(far_out, parts8.at[k], 5 + n, (17, 13)[k], device) for n, device in enumerate((*first_gates, second_hub))]
         for k in range(2)
     ]
-    send_part8_right = [remote(far_out, parts8.at[0], 11 + k, 18, (third_hub, fourth_hub)[k]) for k in range(2)]
-    send_above7 = [remote(top_out, above, 18 + n, 13, gates_of_p7[k]) for n, k in enumerate((3, 0, 1))]
-    others = [at(z, 0, 2, 0), p3s_of_gate[1], at(z, 0, 0, 0), p3s_of_gate[0], at(z, 1, 2, 0), p3s_of_gate[3], p3s_of_gate[2]]
-    above4_sems = (3, 4, 5, 6, 7, 23, 24)
-    send_above4 = [remote(outgoing.at[n // 4], above, above4_sems[n], 13, device) for n, device in enumerate(others)]
+    send_part8_right = [remote(far_out, parts8.at[0], 5 + k, 17, (third_hub, fourth_hub)[k]) for k in range(2)]
+    send_above7 = [remote(top_out, above, n, 13, gates_of_p7[k]) for n, k in enumerate((3, 0, 1))]
+    others = [at(z, 0, 2, 0), p3s_of_gate[0], p3s_of_gate[1], at(z, 0, 0, 0), at(z, 1, 2, 0), p3s_of_gate[2], p3s_of_gate[3]]
+    send_above4 = [remote(outgoing.at[n // 4], above, 3 + n, 13, device) for n, device in enumerate(others)]
     head = at(z, core, x - 1, 0)
-    send_head_map = remote(head_map, head_map, 2, 29, head)
-    send_head_base = remote(cross_sum.at[0], head_base, 3, 30, head)
-    send_above2 = [remote(head_out, leaf_above, 24 + k, 6, column[k]) for k in (3, 2, 1)]
-    send_above2_right = [remote(outgoing.at[1], leaf_above, 5 + k, 6, column[k]) for k in (3, 2, 1)]
+    send_head_map = remote(head_map, head_map, 0, 23, head)
+    send_head_base = remote(cross_sum.at[0], head_base, 1, 24, head)
+    send_above2 = [remote(head_out, leaf_above, 9 + k, 6, column[k]) for k in (3, 2, 1)]
+    send_above2_right = [remote(outgoing.at[1], leaf_above, 1 + k, 6, column[k]) for k in (1, 3, 2)]
 
     def start(copies):
         for copy in copies:
@@ -438,12 +441,12 @@
         send_up6[0].wait_recv()
         for s in range(2):
             ahead = dot(jnp.where(map_keep, up[s, 0], jnp.zeros((width, width), BF16)), map_a[...])
-            gate_up[s] = ahead.astype(BF16)
+            gate_maps[s] = ahead.astype(BF16)
         for copy in send_part4:
             copy.wait_recv()
         child[:, left_part] = (parts4[0].astype(F32) + parts4[1].astype(F32)).astype(BF16)
         up_right.wait_recv()
-        six = dot(child[:, left_part], gate_up[0]) + dot(child[:, right_part], gate_up[1])
+        six = dot(child[:, left_part], gate_maps[0]) + dot(child[:, right_part], gate_maps[1])
         path_coef[...] = six.astype(BF16)
         for k in (0, 1, 3):
 
@@ -615,16 +618,69 @@
     @pl.when(is_p9)
     def _():
         send_cross9[0].start()
-        send_cross9[2].start()
         pl.semaphore_wait(late_sem, 1)
         send_cross9[1].start()
+        send_cross9[2].start()
 
     load_diag.wait()
     product[...] = dot(rhs[...], diag[...])
     load_out.wait()
 
+    def sent(condition, copies):
+        @pl.when(condition)
+        def _():
+            for copy in copies:
+                copy.wait_send()
+
+    sent(is_even, [leaf_up])
+    sent(is_p1, [up_left, *send_cross1, *send_down1])
+    sent(is_p2, [up_left, *send_cross2, *send_down2])
+    sent(both(is_p3, core == 0), [send_part4[0]])
+    sent(is_p3, [up_left])
+    sent(both(is_p4, core == 0), send_up4)
+    sent(both(is_p4, core == 1), [up_left])
+    sent(is_p4, [*send_cross4, *send_down4])
+    sent(is_gate, [up_left])
+    sent(both(is_gate, z % 4 != 2), [send_part6[0]])
+    sent(is_hub, [send_coef7[0], send_child7])
+    sent(is_far_hub, send_part8[0])
+    sent(is_left_center, [*send_cross8_first, send_cross8[1], *send_part8_right])
+    sent(is_right_center, send_cross8)
+    sent(is_p6, [send_down6[1], *send_cross6])
+    sent(both(is_p6, both(z % 4 == 3, z != 7)), send_down6_half)
+    sent(both(is_p6, jnp.logical_not(both(z % 4 == 3, z != 7))), [send_down6[0]])
+    sent(is_p7, [send_top_up7, *send_down7[1:], *send_cross7])
+    sent(is_p8, [send_top_cross, send_down8[1]])
+    sent(is_left_p8, [send_top_up8, send_down8_first[2], *send_down8_first[4:]])
+    sent(is_right_p8, [*send_up8, send_down8[0]])
+    sent(is_p9, send_cross9)
+
+    def lower_hub():
+        send_down8[0].wait_recv()
+        send_cross8[0].wait_recv()
+        send_part8[0][0].wait_recv()
+
+        @pl.when(z == 6)
+        def _():
+            send_part8[1][0].wait_recv()
+            crossed = parts8[0].astype(F32) + parts8[1].astype(F32)
+            parts8[0] = crossed.astype(BF16)
+
+        top_out[...] = (cross_c[...].astype(F32) + dot(parts8[0], map_b[...])).astype(BF16)
+        send_above7[0].start()
+
+        @pl.when(z > 6)
+        def _():
+            start(send_above7[1:])
+
+        above[...] = top_out[...]
+
     @pl.when(is_gate)
     def _():
+        @pl.when(z == 10)
+        def _():
+            lower_hub()
+
         @pl.when(z % 4 != 1)
         def _():
             send_down7[0].wait_recv()
@@ -635,6 +691,8 @@
 
         send_down6[0].wait_recv()
         map_d[...] = dot(map_d[...], map_c[...]).astype(BF16)
+        for s in range(2):
+            gate_maps[s] = dot(map_d[...], down[s, 0]).astype(BF16)
 
         @pl.when(both(z < 6, z != 1))
         def _():
@@ -646,11 +704,14 @@
 
         @pl.when(z < 6)
         def _():
-            map_b[...] = dot(map_b[...], map_d[...]).astype(BF16)
+            for s in range(2):
+                top_up[s, 0] = dot(map_b[...], gate_maps[s]).astype(BF16)
 
         send_cross7[0].wait_recv()
         send_cross6[0].wait_recv()
-        cross_b[...] += dot(cross_a[...].astype(BF16), map_c[...])
+        five = (cross_b[...] + dot(cross_a[...].astype(BF16), map_c[...])).astype(BF16)
+        for s in range(2):
+            cross_sum[s] += dot(five, down[s, 0])
 
         @pl.when(z < 6)
         def _():
@@ -658,32 +719,17 @@
             def _():
                 send_cross8_first[0].wait_recv()
 
-            cross_b[...] += dot(cross_c[...], map_d[...])
             for k in range(2):
                 send_part8[k][0].wait_recv()
-            crossed = (parts8[0].astype(F32) + parts8[1].astype(F32)).astype(BF16)
-            above[...] = (cross_b[...] + dot(crossed, map_b[...])).astype(BF16)
-
-        @pl.when(is_late_hub)
-        def _():
-            send_down8[0].wait_recv()
-            send_cross8[0].wait_recv()
-            send_part8[0][0].wait_recv()
-
-            @pl.when(z == 6)
-            def _():
-                send_part8[1][0].wait_recv()
-                crossed = parts8[0].astype(F32) + parts8[1].astype(F32)
-                parts8[0] = crossed.astype(BF16)
-
-            top_out[...] = (cross_c[...].astype(F32) + dot(parts8[0], map_b[...])).astype(BF16)
-            send_above7[0].start()
-
-            @pl.when(z > 6)
-            def _():
-                start(send_above7[1:])
-
-            above[...] = top_out[...]
+            above[...] = (parts8[0].astype(F32) + parts8[1].astype(F32)).astype(BF16)
+            for s in range(2):
+                four = cross_sum[s] + dot(cross_c[...], gate_maps[s]) + dot(above[...], top_up[s, 0])
+                outgoing[s] = four.astype(BF16)
+                start(send_above4[4 * s : 4 * s + 4])
+
+        @pl.when(both(is_late_hub, z != 10))
+        def _():
+            lower_hub()
 
         @pl.when(both(z > 6, z % 4 != 2))
         def _():
@@ -691,11 +737,9 @@
 
         @pl.when(z >= 6)
         def _():
-            above[...] = (cross_b[...] + dot(above[...], map_d[...])).astype(BF16)
-
-        for s in range(2):
-            outgoing[s] = (cross_sum[s] + dot(above[...], down[s, 0])).astype(BF16)
-            start(send_above4[4 * s : 4 * s + 4])
+            for s in range(2):
+                outgoing[s] = (cross_sum[s] + dot(above[...], gate_maps[s])).astype(BF16)
+                start(send_above4[4 * s : 4 * s + 4])
 
     @pl.when(is_p3)
     def _():
@@ -753,37 +797,11 @@
 
     product[...] += dot(leaf_above[...], leaf_map2[...])
 
-    def sent(condition, copies):
-        @pl.when(condition)
-        def _():
-            for copy in copies:
-                copy.wait_send()
-
-    sent(is_even, [leaf_up])
-    sent(is_p1, [up_left, *send_cross1, *send_down1])
-    sent(is_p2, [up_left, *send_cross2, *send_down2])
-    sent(both(is_p3, core == 0), [send_part4[0]])
-    sent(is_p3, [up_left, send_head_map, send_head_base, *send_above2_right])
     sent(is_head, send_above2)
-    sent(both(is_p4, core == 0), send_up4)
-    sent(both(is_p4, core == 1), [up_left])
-    sent(is_p4, [*send_cross4, *send_down4])
-    sent(is_gate, [up_left, *send_above4])
-    sent(both(is_gate, z % 4 != 2), [send_part6[0]])
-    sent(is_hub, [send_coef7[0], send_child7])
+    sent(is_p3, [send_head_map, send_head_base, *send_above2_right])
+    sent(is_gate, send_above4)
     sent(is_late_hub, send_above7[:1])
     sent(is_far_hub, send_above7[1:])
-    sent(is_far_hub, send_part8[0])
-    sent(is_left_center, [*send_cross8_first, send_cross8[1], *send_part8_right])
-    sent(is_right_center, send_cross8)
-    sent(is_p6, [send_down6[1], *send_cross6])
-    sent(both(is_p6, both(z % 4 == 3, z != 7)), send_down6_half)
-    sent(both(is_p6, jnp.logical_not(both(z % 4 == 3, z != 7))), [send_down6[0]])
-    sent(is_p7, [send_top_up7, *send_down7[1:], *send_cross7])
-    sent(is_p8, [send_top_cross, send_down8[1]])
-    sent(is_left_p8, [send_top_up8, send_down8_first[2], *send_down8_first[4:]])
-    sent(is_right_p8, [*send_up8, send_down8[0]])
-    sent(is_p9, send_cross9)
 
 
 def on_device(rhs, diag_blocks, leaf_in, leaf_out, up_maps, cross_maps, down_maps, node_rank):
@@ -797,7 +815,7 @@
     full_map = pltpu.VMEM((width, width), BF16)
     return pl.pallas_call(
         kernel,
-        out_shape=jax.ShapeDtypeStruct((rows, leaf), F32),
+        out_shape=pltpu.VMEM((rows, leaf), F32),
         in_specs=[pl.BlockSpec(memory_space=pl.ANY)] * 8,
         out_specs=pl.BlockSpec(memory_space=pltpu.VMEM),
         scratch_shapes=[pltpu.VMEM(each.shape, each.dtype) for each in operands]
@@ -839,8 +857,8 @@
             vector(4),
             vector(2),
             pltpu.SemaphoreType.DMA((8,)),
-            pltpu.SemaphoreType.DMA((28,)),
-            pltpu.SemaphoreType.DMA((31,)),
+            pltpu.SemaphoreType.DMA((14,)),
+            pltpu.SemaphoreType.DMA((25,)),
             pltpu.SemaphoreType.REGULAR,
             pltpu.SemaphoreType.REGULAR,
         ],

time: 42.9 us -> 41.1 us (0.958)
  the two profiles are of different devices: /device:TPU:10 before, /device:TPU:18 now
where the time goes in v10:
time: 41.1 us; the launch traced here: 40.9 us
  Pallas kernels  40.3 us (98%)
  local copies, waits for them, and re-layouts  0.62 us (2%)
    pallas_call x1, Pallas kernels, on_device(): pl.pallas_call(kernel, out_shape=pltpu.VMEM((rows, leaf), F32), in_specs=...  40.3 us

profile of v10, /device:TPU:18, one launch (start us, length us, event | category | flops | bytes accessed | tf_op | source)
XLA Modules:
  0.0 40.9 jit_solution(5999280159233043852)
XLA Ops:
  0.0 40.3 %shard_map.82 = f32[16,512]{1,0:T(8,128)S(1)} custom-call(bf16[16,512]{1,0:T(8,128)(2,1)} %rhs_hbm.1, bf16[512,512]{1,0:T(8,128)(2,1)} %diag_hbm.1, bf16[512,128]{1,0:T(8,128)(2,1)} %in_hbm.1, bf16[128,512]{1,0:T(8,128)(2,1)} %out_hbm.1, bf16[2,1,512,512]{3,2,1,0:T(8,128)(2,1)} %up_hbm.1, bf16[2,1,512,512]{3,2,1,0:T(8,128)(2,1)} %cross_hbm.1, ...), custom_call_target="tpu_custom_call" | custom-call | tf_op jit(solution)/shard_map/pallas_call | solution.py:816
  40.3 0.6 %copy.10 = f32[16,512]{1,0:T(8,128)} copy(f32[16,512]{1,0:T(8,128)S(1)} %shard_map.82) | data formatting | bytes 65536

commit v11 on v10

--- a/solution.py
+++ b/solution.py
@@ -279,7 +279,7 @@
     head = at(z, core, x - 1, 0)
     send_head_map = remote(head_map, head_map, 0, 23, head)
     send_head_base = remote(cross_sum.at[0], head_base, 1, 24, head)
-    send_above2 = [remote(head_out, leaf_above, 9 + k, 6, column[k]) for k in (3, 2, 1)]
+    send_above2 = [remote(head_out, leaf_above, 9 + k, 6, column[k]) for k in (1, 3, 2)]
     send_above2_right = [remote(outgoing.at[1], leaf_above, 1 + k, 6, column[k]) for k in (1, 3, 2)]
 
     def start(copies):
@@ -467,11 +467,23 @@
                 send_cross9[0].wait_recv()
                 map_e[...] = dot(map_e[...], map_f[...]).astype(BF16)
 
+                @pl.when(z == 10)
+                def _():
+                    for k in range(2):
+                        top_cross[k, 0] = dot(top_up[k, 0], map_e[...]).astype(BF16)
+
             for k in (0, 1, 3):
                 send_part6[k].wait_recv()
             for k, part in enumerate((left_part, right_part)):
                 six = parts6[2 * k].astype(F32) + parts6[2 * k + 1].astype(F32)
                 top_child[:, part] = six.astype(BF16)
+
+            @pl.when(z == 10)
+            def _():
+                far = dot(top_child[:, left_part], top_cross[0, 0]) + dot(top_child[:, right_part], top_cross[1, 0])
+                far_out[...] = far.astype(BF16)
+                start(send_part8[0])
+
             seven = dot(top_child[:, left_part], top_up[0, 0]) + dot(top_child[:, right_part], top_up[1, 0])
             top_coef[...] = seven.astype(BF16)
             for k in range(2):
@@ -480,14 +492,10 @@
                 def _():
                     send_coef7[k].start()
 
-            @pl.when(is_far_hub)
+            @pl.when(z == 14)
             def _():
                 far_out[...] = dot(top_coef[...], map_e[...]).astype(BF16)
-                for k in range(2):
-
-                    @pl.when(z == 10 + 4 * k)
-                    def _():
-                        start(send_part8[k])
+                start(send_part8[1])
 
             send_child7.start()
 
@@ -715,15 +723,17 @@
 
         @pl.when(z < 6)
         def _():
+            send_part8[1][0].wait_recv()
+            for s in range(2):
+                cross_sum[s] += dot(parts8[1], top_up[s, 0])
+
             @pl.when(z != 4)
             def _():
                 send_cross8_first[0].wait_recv()
 
-            for k in range(2):
-                send_part8[k][0].wait_recv()
-            above[...] = (parts8[0].astype(F32) + parts8[1].astype(F32)).astype(BF16)
+            send_part8[0][0].wait_recv()
             for s in range(2):
-                four = cross_sum[s] + dot(cross_c[...], gate_maps[s]) + dot(above[...], top_up[s, 0])
+                four = cross_sum[s] + dot(cross_c[...], gate_maps[s]) + dot(parts8[0], top_up[s, 0])
                 outgoing[s] = four.astype(BF16)
                 start(send_above4[4 * s : 4 * s + 4])
 

time: 41.1 us -> 40.9 us (level)
  no operation moved by 1% of the time
where the time goes in v11:
time: 40.9 us; the launch traced here: 40.8 us
  Pallas kernels  40.1 us (98%)
  local copies, waits for them, and re-layouts  0.62 us (2%)
    pallas_call x1, Pallas kernels, on_device(): pl.pallas_call(kernel, out_shape=pltpu.VMEM((rows, leaf), F32), in_specs=...  40.1 us

profile of v11, /device:TPU:18, one launch (start us, length us, event | category | flops | bytes accessed | tf_op | source)
XLA Modules:
  0.0 40.8 jit_solution(7083976689641210891)
XLA Ops:
  0.0 40.1 %shard_map.82 = f32[16,512]{1,0:T(8,128)S(1)} custom-call(bf16[16,512]{1,0:T(8,128)(2,1)} %rhs_hbm.1, bf16[512,512]{1,0:T(8,128)(2,1)} %diag_hbm.1, bf16[512,128]{1,0:T(8,128)(2,1)} %in_hbm.1, bf16[128,512]{1,0:T(8,128)(2,1)} %out_hbm.1, bf16[2,1,512,512]{3,2,1,0:T(8,128)(2,1)} %up_hbm.1, bf16[2,1,512,512]{3,2,1,0:T(8,128)(2,1)} %cross_hbm.1, ...), custom_call_target="tpu_custom_call" | custom-call | tf_op jit(solution)/shard_map/pallas_call | solution.py:826
  40.1 0.6 %copy.10 = f32[16,512]{1,0:T(8,128)} copy(f32[16,512]{1,0:T(8,128)S(1)} %shard_map.82) | data formatting | bytes 65536

commit v12 on v11

--- a/solution.py
+++ b/solution.py
@@ -54,6 +54,10 @@
     head_map,
     head_base,
     head_out,
+    map_0,
+    base_0,
+    above_0,
+    out_0,
     leaf_map2,
     leaf_map1,
     cross_a,
@@ -160,14 +164,17 @@
     next_p3 = collector(z, core, x_odd)
     greet(is_p1, [left_leaf])
     greet(y == 1, [column[3]])
-    greet(y == 3, [collector(z, core, x)])
+    on_one = core == 1
+    greet(core == 0, [collector(z, 1, x)])
+    greet(both(y == 3, on_one), [collector(z, core, x)])
     greet(is_p2, [column[1], column[3]])
-    greet(both(is_p2, x % 2 == 1), [column[1]])
-    greet(on_top, [collector(z, 1, 0)])
+    greet(both(both(is_p2, x % 2 == 1), on_one), [column[1]])
     greet(y == 0, [column[1], column[3]])
-    greet(both(y == 0, x_even), [next_p3])
-    greet(is_p3, [at(z, core, x - 1, 3), collector(z, core, 2), collector(z, 1, 0)])
-    greet(is_p4, [collector(z, core, 1), collector(z, core, 3), collector(z, 1, 0)])
+    greet(both(is_head, on_one), [next_p3, collector(z, 0, x_odd)])
+    greet(is_p3, [at(z, core, x - 1, 3), collector(z, core, 2)])
+    greet(both(is_p3, on_one), [collector(z, 1, 0), collector(z, 0, x)])
+    greet(is_p4, [collector(z, core, 1), collector(z, core, 3)])
+    greet(both(is_p4, on_one), [collector(z, 1, 0)])
     greet(is_gate, [collector(z, 0, 1), collector(z, 0, 3), collector(z, 1, 2)] + [collector(z_odd, 0, 0), collector(z_seven, 0, 0)])
     greet(both(is_gate, z % 4 == 0), [collector(z + 1, 1, 0)])
     greet(both(is_gate, both(z < 6, z != 4)), [collector(4, 0, 0), collector(8, 0, 0), collector(4, 1, 0)])
@@ -190,11 +197,11 @@
         (y == 3, 3),
         (both(y == 3, x_even), 1),
         (y == 1, 2),
-        (both(y == 1, x_even), 1),
+        (both(y == 1, on_one), 4),
+        (both(both(y == 1, x_even), on_one), 1),
         (both(y == 1, x % 2 == 1), 4),
-        (both(both(y == 1, x % 2 == 1), core == 0), 1),
         (both(y == 1, x == 2), 2 + core),
-        (both(ty == 1, core == 1), 8),
+        (both(ty == 1, core == 1), 4),
         (both(both(ty == 1, core == 1), z % 4 != 2), 1),
         (both(both(ty == 1, core == 1), z % 4 == 1), 1),
         (both(both(ty == 1, core == 1), z % 4 == 2), 2),
@@ -274,11 +281,17 @@
     ]
     send_part8_right = [remote(far_out, parts8.at[0], 5 + k, 17, (third_hub, fourth_hub)[k]) for k in range(2)]
     send_above7 = [remote(top_out, above, n, 13, gates_of_p7[k]) for n, k in enumerate((3, 0, 1))]
-    others = [at(z, 0, 2, 0), p3s_of_gate[0], p3s_of_gate[1], at(z, 0, 0, 0), at(z, 1, 2, 0), p3s_of_gate[2], p3s_of_gate[3]]
-    send_above4 = [remote(outgoing.at[n // 4], above, 3 + n, 13, device) for n, device in enumerate(others)]
-    head = at(z, core, x - 1, 0)
+    servers = [at(z, 1, 2, 0), at(z, 1, 1, 0), at(z, 1, 3, 0)]
+    send_above4 = [remote(outgoing.at[0], above_0, 3 + n, 27, device) for n, device in enumerate(servers)]
+    send_above4 += [remote(outgoing.at[1], above, 6 + n, 13, device) for n, device in enumerate(servers)]
+    head = at(z, 1, x - 1, 0)
     send_head_map = remote(head_map, head_map, 0, 23, head)
     send_head_base = remote(cross_sum.at[0], head_base, 1, 24, head)
+    send_head_map_0 = remote(head_map, map_0, 0, 25, head)
+    send_head_base_0 = remote(cross_sum.at[0], base_0, 1, 26, head)
+    send_map_0 = remote(down.at[1, 0], map_0, 2, 25, at(z, 1, x, 0))
+    send_base_0 = remote(cross_sum.at[1], base_0, 3, 26, at(z, 1, x, 0))
+    send_above2_0 = [remote(out_0, leaf_above, (13, 9, 14, 15)[n], 6, at(z, 0, x, k)) for n, k in enumerate((1, 3, 2, 0))]
     send_above2 = [remote(head_out, leaf_above, 9 + k, 6, column[k]) for k in (1, 3, 2)]
     send_above2_right = [remote(outgoing.at[1], leaf_above, 1 + k, 6, column[k]) for k in (1, 3, 2)]
 
@@ -735,7 +748,7 @@
             for s in range(2):
                 four = cross_sum[s] + dot(cross_c[...], gate_maps[s]) + dot(parts8[0], top_up[s, 0])
                 outgoing[s] = four.astype(BF16)
-                start(send_above4[4 * s : 4 * s + 4])
+                start(send_above4[3 * s : 3 * s + 3])
 
         @pl.when(both(is_late_hub, z != 10))
         def _():
@@ -749,38 +762,80 @@
         def _():
             for s in range(2):
                 outgoing[s] = (cross_sum[s] + dot(above[...], gate_maps[s])).astype(BF16)
-                start(send_above4[4 * s : 4 * s + 4])
+                start(send_above4[3 * s : 3 * s + 3])
 
     @pl.when(is_p3)
     def _():
         send_down4[0].wait_recv()
         head_map[...] = dot(map_d[...], down[0, 0]).astype(BF16)
-        send_head_map.start()
+
+        @pl.when(core == 0)
+        def _():
+            send_head_map_0.start()
+
+        @pl.when(core == 1)
+        def _():
+            send_head_map.start()
+
         send_cross4[0].wait_recv()
         cross_four = cross_a[...].astype(BF16)
         cross_sum[0] += dot(cross_four, down[0, 0])
-        send_head_base.start()
+
+        @pl.when(core == 0)
+        def _():
+            send_head_base_0.start()
+
+        @pl.when(core == 1)
+        def _():
+            send_head_base.start()
+
         cross_sum[1] += dot(cross_four, down[1, 0])
         down[1, 0] = dot(map_d[...], down[1, 0]).astype(BF16)
-        send_above4[0].wait_recv()
+
+        @pl.when(core == 0)
+        def _():
+            send_map_0.start()
+            send_base_0.start()
+
+    is_server = both(y == 0, core == 1)
+
+    @pl.when(is_server)
+    def _():
+        send_map_0.wait_recv()
+        send_base_0.wait_recv()
+
+        @pl.when(is_gate)
+        def _():
+            above_0[...] = outgoing[0]
+
+        @pl.when(jnp.logical_not(is_gate))
+        def _():
+            send_above4[0].wait_recv()
+
+        out_0[...] = (base_0[...] + dot(above_0[...], map_0[...])).astype(BF16)
+        start(send_above2_0)
+
+    @pl.when(both(is_p3, core == 1))
+    def _():
+        send_above4[3].wait_recv()
         outgoing[1] = (cross_sum[1] + dot(above[...], down[1, 0])).astype(BF16)
         start(send_above2_right)
         leaf_above[...] = outgoing[1]
 
-    @pl.when(is_head)
+    @pl.when(both(is_head, core == 1))
     def _():
         send_head_map.wait_recv()
         send_head_base.wait_recv()
 
         @pl.when(is_gate)
         def _():
-            head_out[...] = (head_base[...] + dot(outgoing[1], head_map[...])).astype(BF16)
+            above[...] = outgoing[1]
 
         @pl.when(jnp.logical_not(is_gate))
         def _():
-            send_above4[0].wait_recv()
-            head_out[...] = (head_base[...] + dot(above[...], head_map[...])).astype(BF16)
-
+            send_above4[3].wait_recv()
+
+        head_out[...] = (head_base[...] + dot(above[...], head_map[...])).astype(BF16)
         start(send_above2)
         leaf_above[...] = head_out[...]
 
@@ -801,14 +856,16 @@
     leaf_map1[...] = jnp.where(map_keep, dot(leaf_map2[...], leaf_map1[...]), 0.0).astype(BF16)
     leaf_map2[...] = dot(leaf_map1[...], leaf_out[...]).astype(BF16)
 
-    @pl.when(y > 0)
+    @pl.when(jnp.logical_not(is_server))
     def _():
         send_above2[0].wait_recv()
 
     product[...] += dot(leaf_above[...], leaf_map2[...])
 
-    sent(is_head, send_above2)
-    sent(is_p3, [send_head_map, send_head_base, *send_above2_right])
+    sent(is_server, send_above2_0)
+    sent(both(is_head, core == 1), send_above2)
+    sent(both(is_p3, core == 1), [send_head_map, send_head_base, *send_above2_right])
+    sent(both(is_p3, core == 0), [send_head_map_0, send_head_base_0, send_map_0, send_base_0])
     sent(is_gate, send_above4)
     sent(is_late_hub, send_above7[:1])
     sent(is_far_hub, send_above7[1:])
@@ -855,6 +912,10 @@
             vector(kind=F32),
             vector(),
             full_map,
+            vector(kind=F32),
+            vector(),
+            vector(),
+            full_map,
             pltpu.VMEM((width, leaf_width), BF16),
             vector(kind=F32),
             vector(kind=F32),
@@ -867,8 +928,8 @@
             vector(4),
             vector(2),
             pltpu.SemaphoreType.DMA((8,)),
-            pltpu.SemaphoreType.DMA((14,)),
-            pltpu.SemaphoreType.DMA((25,)),
+            pltpu.SemaphoreType.DMA((16,)),
+            pltpu.SemaphoreType.DMA((28,)),
             pltpu.SemaphoreType.REGULAR,
             pltpu.SemaphoreType.REGULAR,
         ],

time: 40.9 us -> 40.4 us (0.988)
  the two profiles are of different devices: /device:TPU:18 before, /device:TPU:83 now
where the time goes in v12:
time: 40.4 us; the launch traced here: 40.3 us
  Pallas kernels  39.7 us (98%)
  local copies, waits for them, and re-layouts  0.62 us (2%)
    pallas_call x1, Pallas kernels, on_device(): pl.pallas_call(kernel, out_shape=pltpu.VMEM((rows, leaf), F32), in_specs=...  39.7 us

profile of v12, /device:TPU:83, one launch (start us, length us, event | category | flops | bytes accessed | tf_op | source)
XLA Modules:
  0.0 40.3 jit_solution(2798597133087803605)
XLA Ops:
  0.0 39.7 %shard_map.82 = f32[16,512]{1,0:T(8,128)S(1)} custom-call(bf16[16,512]{1,0:T(8,128)(2,1)} %rhs_hbm.1, bf16[512,512]{1,0:T(8,128)(2,1)} %diag_hbm.1, bf16[512,128]{1,0:T(8,128)(2,1)} %in_hbm.1, bf16[128,512]{1,0:T(8,128)(2,1)} %out_hbm.1, bf16[2,1,512,512]{3,2,1,0:T(8,128)(2,1)} %up_hbm.1, bf16[2,1,512,512]{3,2,1,0:T(8,128)(2,1)} %cross_hbm.1, ...), custom_call_target="tpu_custom_call" | custom-call | tf_op jit(solution)/shard_map/pallas_call | solution.py:883
  39.7 0.6 %copy.10 = f32[16,512]{1,0:T(8,128)} copy(f32[16,512]{1,0:T(8,128)S(1)} %shard_map.82) | data formatting | bytes 65536

commit v13 on v12

--- a/solution.py
+++ b/solution.py
@@ -281,7 +281,7 @@
     ]
     send_part8_right = [remote(far_out, parts8.at[0], 5 + k, 17, (third_hub, fourth_hub)[k]) for k in range(2)]
     send_above7 = [remote(top_out, above, n, 13, gates_of_p7[k]) for n, k in enumerate((3, 0, 1))]
-    servers = [at(z, 1, 2, 0), at(z, 1, 1, 0), at(z, 1, 3, 0)]
+    servers = [at(z, 1, 1, 0), at(z, 1, 2, 0), at(z, 1, 3, 0)]
     send_above4 = [remote(outgoing.at[0], above_0, 3 + n, 27, device) for n, device in enumerate(servers)]
     send_above4 += [remote(outgoing.at[1], above, 6 + n, 13, device) for n, device in enumerate(servers)]
     head = at(z, 1, x - 1, 0)
@@ -606,6 +606,7 @@
         @pl.when(is_left_p8)
         def _():
             send_down8[1].start()
+            send_down8_first[1].start()
             start(send_down8_first[4:])
 
         @pl.when(is_right_p8)
@@ -624,7 +625,6 @@
         @pl.when(is_left_p8)
         def _():
             send_top_up8.start()
-            send_down8_first[1].start()
             send_down1[0].wait_recv()
             for k, after in ((1, 3), (3, 2)):
                 send_down8_first[k].wait_send()
@@ -813,13 +813,14 @@
             send_above4[0].wait_recv()
 
         out_0[...] = (base_0[...] + dot(above_0[...], map_0[...])).astype(BF16)
-        start(send_above2_0)
+        start(send_above2_0[:3])
 
     @pl.when(both(is_p3, core == 1))
     def _():
         send_above4[3].wait_recv()
         outgoing[1] = (cross_sum[1] + dot(above[...], down[1, 0])).astype(BF16)
         start(send_above2_right)
+        send_above2_0[3].start()
         leaf_above[...] = outgoing[1]
 
     @pl.when(both(is_head, core == 1))
@@ -837,6 +838,7 @@
 
         head_out[...] = (head_base[...] + dot(above[...], head_map[...])).astype(BF16)
         start(send_above2)
+        send_above2_0[3].start()
         leaf_above[...] = head_out[...]
 
     @pl.when(both(is_even, jnp.logical_not(is_p8)))

time: 40.4 us -> 40.4 us (level)
  the two profiles are of different devices: /device:TPU:83 before, /device:TPU:21 now
where the time goes in v13:
time: 40.4 us; the launch traced here: 40.2 us
  Pallas kernels  39.6 us (98%)
  local copies, waits for them, and re-layouts  0.62 us (2%)
    pallas_call x1, Pallas kernels, on_device(): pl.pallas_call(kernel, out_shape=pltpu.VMEM((rows, leaf), F32), in_specs=...  39.6 us

profile of v13, /device:TPU:21, one launch (start us, length us, event | category | flops | bytes accessed | tf_op | source)
XLA Modules:
  0.0 40.2 jit_solution(2931924016169338819)
XLA Ops:
  0.0 39.6 %shard_map.82 = f32[16,512]{1,0:T(8,128)S(1)} custom-call(bf16[16,512]{1,0:T(8,128)(2,1)} %rhs_hbm.1, bf16[512,512]{1,0:T(8,128)(2,1)} %diag_hbm.1, bf16[512,128]{1,0:T(8,128)(2,1)} %in_hbm.1, bf16[128,512]{1,0:T(8,128)(2,1)} %out_hbm.1, bf16[2,1,512,512]{3,2,1,0:T(8,128)(2,1)} %up_hbm.1, bf16[2,1,512,512]{3,2,1,0:T(8,128)(2,1)} %cross_hbm.1, ...), custom_call_target="tpu_custom_call" | custom-call | tf_op jit(solution)/shard_map/pallas_call | solution.py:885
  39.6 0.6 %copy.10 = f32[16,512]{1,0:T(8,128)} copy(f32[16,512]{1,0:T(8,128)S(1)} %shard_map.82) | data formatting | bytes 65536

commit v14 on v13

--- a/solution.py
+++ b/solution.py
@@ -813,14 +813,14 @@
             send_above4[0].wait_recv()
 
         out_0[...] = (base_0[...] + dot(above_0[...], map_0[...])).astype(BF16)
-        start(send_above2_0[:3])
+        start([send_above2_0[0], send_above2_0[2]])
 
     @pl.when(both(is_p3, core == 1))
     def _():
         send_above4[3].wait_recv()
         outgoing[1] = (cross_sum[1] + dot(above[...], down[1, 0])).astype(BF16)
         start(send_above2_right)
-        send_above2_0[3].start()
+        start([send_above2_0[1], send_above2_0[3]])
         leaf_above[...] = outgoing[1]
 
     @pl.when(both(is_head, core == 1))
@@ -838,7 +838,7 @@
 
         head_out[...] = (head_base[...] + dot(above[...], head_map[...])).astype(BF16)
         start(send_above2)
-        send_above2_0[3].start()
+        start([send_above2_0[1], send_above2_0[3]])
         leaf_above[...] = head_out[...]
 
     @pl.when(both(is_even, jnp.logical_not(is_p8)))

time: 40.4 us -> 40.4 us (level)
  no operation moved by 1% of the time
where the time goes in v14:
time: 40.4 us; the launch traced here: 40.2 us
  Pallas kernels  39.6 us (98%)
  local copies, waits for them, and re-layouts  0.62 us (2%)
    pallas_call x1, Pallas kernels, on_device(): pl.pallas_call(kernel, out_shape=pltpu.VMEM((rows, leaf), F32), in_specs=...  39.6 us

profile of v14, /device:TPU:21, one launch (start us, length us, event | category | flops | bytes accessed | tf_op | source)
XLA Modules:
  0.0 40.2 jit_solution(16932520315985956168)
XLA Ops:
  0.0 39.6 %shard_map.82 = f32[16,512]{1,0:T(8,128)S(1)} custom-call(bf16[16,512]{1,0:T(8,128)(2,1)} %rhs_hbm.1, bf16[512,512]{1,0:T(8,128)(2,1)} %diag_hbm.1, bf16[512,128]{1,0:T(8,128)(2,1)} %in_hbm.1, bf16[128,512]{1,0:T(8,128)(2,1)} %out_hbm.1, bf16[2,1,512,512]{3,2,1,0:T(8,128)(2,1)} %up_hbm.1, bf16[2,1,512,512]{3,2,1,0:T(8,128)(2,1)} %cross_hbm.1, ...), custom_call_target="tpu_custom_call" | custom-call | tf_op jit(solution)/shard_map/pallas_call | solution.py:885
  39.6 0.6 %copy.10 = f32[16,512]{1,0:T(8,128)} copy(f32[16,512]{1,0:T(8,128)S(1)} %shard_map.82) | data formatting | bytes 65536
